TPU v7x, 32 devices: a whole 2x2x4 slice. The times are simulated.
32 devices in a mesh: real: 2 (over x), area: 16 (over z, y, core).
Axes of the slice: x: 2, y: 2, z: 4, core: 2. Of those that a mesh axis runs over, the one named last changes fastest.
Arguments:
- block_owner: int32 [128], replicated, may hold values from 0 to 127, as said below
- transfer_cells: int32 [16384], P('area'), may hold values from 0 to 131071, as said below
- transfer_nodes: int32 [16384], P('area'), may hold values from 0 to 32767, as said below
- transfer_weights: float32 [16384], P('area'), may hold values from 0.2 to 2
- row_counts: int32 [16], P('area'), may hold values from 204 to 1024, as said below
- matrix_start: float32 [16, 256, 1024], P('real', 'area'), parts along dimension 0, may hold values from -6 to 6
- matrix_source: float32 [16, 256, 1024], P('real', 'area'), parts along dimension 0, may hold values from -6 to 6
- matrix_storage: float32 [16, 256, 1024], P('real', 'area'), parts along dimension 0, may hold values from 0.5 to 8
- fracture_start: float32 [128, 512], P('area', 'real'), parts along dimension 1, may hold values from -6 to 6
- fracture_source: float32 [128, 512], P('area', 'real'), parts along dimension 1, may hold values from -6 to 6
- fracture_leak: float32 [128, 512], P('area', 'real'), parts along dimension 1, may hold values from 0.2 to 2
- fracture_links: int32 [4, 128, 256], P(None, 'area'), may hold values from 0 to 255
- link_weights: float32 [8, 128, 256], P('real', 'area'), parts along dimension 0, may hold values from 0.1 to 1
Outputs:
- matrix_pressure: float32 [16, 256, 1024], P('real', 'area'), parts along dimension 0
- fracture_pressure: float32 [128, 512], P('area', 'real'), parts along dimension 1
There are 2 independent parts, one for each index of `real`. A program takes and returns all parts, laid end to end along the dimension named above; an argument that names none is the same for every part. Nothing has to cross between parts.
Inputs may be any that keep to these rules, and one draw needn't show every extreme that they name: `block_owner`: A permutation: the slot of each fracture block; slots 8 i to 8 (i + 1) - 1 lie on the i-th device of area. `transfer_cells`: rows that are not live hold values in the same range, to be ignored. `transfer_nodes`: of the live rows of one device, at most 96 name blocks whose slots lie on any one device; some device receives exactly 96 live rows from every device. The first row_counts[s] rows of device s are live; some device has all 1024 live.
All inputs are finite; a program needn't handle non-finite values.
Results may differ from a plain program's by a relative error of at most 0.0003.
Values sent between devices are 32-bit elements; how exact they have to be, the bound alone decides.
No kernel may reach another device: no remote copies, remote signals or barrier semaphores. Data moves between devices by JAX's collectives and lax.ppermute only.
A program may use at most 64 MiB of HBM per device.

v0:
```python
import functools
import math

import jax
import jax.numpy as jnp
from jax import lax
from jax.experimental import pallas as pl
from jax.experimental.pallas import tpu as pltpu
from jax.sharding import PartitionSpec as P

ITERS = 4
LANES = 128
F32 = jnp.float32
BF16 = jnp.bfloat16
VMEM_LIMIT = 32 * 1024 * 1024


def relax_weights(steps_total):
    return [
        1.0 / (1.0 + 0.75 * math.cos(math.pi * (2 * index + 1) / (2 * steps_total)))
        for index in range(steps_total)
    ]


def log2(value):
    assert value & (value - 1) == 0
    return value.bit_length() - 1


def iota(shape, dim):
    return lax.broadcasted_iota(jnp.int32, shape, dim)


def halves(x):
    high = x.astype(BF16)
    low = (x - high.astype(F32)).astype(BF16)
    return high, low


def matmul(a, b, contract):
    return lax.dot_general(a, b, ((contract[:1], contract[1:]), ((), ())), preferred_element_type=F32)


def to_dense(x, cap):
    return jnp.concatenate([x[i : i + 1, :cap] for i in range(x.shape[0])], axis=1)


def from_dense(x, devices, cap):
    rows = jnp.concatenate([x[:, i * cap : (i + 1) * cap] for i in range(devices)], axis=0)
    return jnp.concatenate([rows, jnp.zeros((devices, LANES - cap), x.dtype)], axis=1)


def lane_gather(table, index):
    return jnp.take_along_axis(table, index, axis=1, mode="promise_in_bounds")


def masked_parts(low, *values):
    mask = iota((LANES, low.shape[1]), 0) == low
    zero = jnp.zeros((), F32)
    parts = []
    for value in values:
        high = value.astype(BF16).astype(F32)
        parts.append(jnp.where(mask, high, zero).astype(BF16))
        parts.append(jnp.where(mask, value - high, zero).astype(BF16))
    return jnp.concatenate(parts, axis=0)


def fold(wide, index):
    start = 2 * index * LANES
    return wide[:, start : start + LANES] + wide[:, start + LANES : start + 2 * LANES]


def pick_low(tall, low):
    both = tall[:LANES] + tall[LANES:]
    return jnp.sum(
        jnp.where(iota(both.shape, 0) == low, both, 0.0), axis=0, keepdims=True
    )


def stack_lanes(x):
    return jnp.concatenate(
        [x[:, i * LANES : (i + 1) * LANES] for i in range(x.shape[1] // LANES)], axis=0
    )


def unstack_lanes(x, rows):
    return jnp.concatenate([x[i : i + rows] for i in range(0, x.shape[0], rows)], axis=1)


def put_columns(chunk, index, columns_ref):
    high, low = halves(chunk.T)
    columns_ref[:LANES, index * LANES : (index + 1) * LANES] = high
    columns_ref[LANES:, index * LANES : (index + 1) * LANES] = low


def setup_kernel(
    devices,
    cap,
    owned,
    blk,
    cols,
    counts_ref,
    owner_ref,
    cells_ref,
    nodes_ref,
    weights_ref,
    matrix_ref,
    fracture_ref,
    hot_ref,
    slot_index_ref,
    slot_weight_ref,
    slot_code_ref,
    message_ref,
    top_ref,
    bottom_ref,
    columns_ref,
):
    groups = cells_ref.shape[0]
    slots = devices * cap
    plane_rows = matrix_ref.shape[0] * matrix_ref.shape[1]
    col_groups = cols // LANES
    shape = (groups, LANES)
    nodes, cells = nodes_ref[...], cells_ref[...]
    live = iota(shape, 0) * LANES + iota(shape, 1) < counts_ref[0]
    weight = jnp.where(live, weights_ref[...], 0.0)
    block = nodes >> log2(blk)
    slot = jnp.zeros(shape, jnp.int32)
    for part in range(owner_ref.shape[0]):
        table = jnp.broadcast_to(owner_ref[part : part + 1, :], shape)
        found = lane_gather(table, block & (LANES - 1))
        slot = jnp.where(block >> log2(LANES) == part, found, slot)
    target = jnp.where(live, slot >> log2(owned), -1)
    node_high = ((nodes & (blk - 1)) >> log2(LANES)) * owned + (slot & (owned - 1))
    node_low = nodes & (LANES - 1)
    cell_plane = cells >> log2(cols)
    cell_group = (cells & (cols - 1)) >> log2(LANES)
    cell_low = cells & (LANES - 1)

    device_rows = iota((devices, LANES), 0)
    member = [(device_rows == target[q : q + 1]).astype(F32) for q in range(groups)]
    earlier = (iota((LANES, LANES), 0) < iota((LANES, LANES), 1)).astype(BF16)
    counted = matmul(jnp.concatenate(member, axis=0).astype(BF16), earlier, (1, 0))
    before = jnp.zeros((devices, 1), F32)
    placed = []
    for q in range(groups):
        rank = jnp.sum(
            member[q] * (counted[q * devices : (q + 1) * devices] + before), axis=0, keepdims=True
        ).astype(jnp.int32)
        before = before + jnp.sum(member[q], axis=1, keepdims=True)
        where = target[q : q + 1]
        placed.append(jnp.where(where >= 0, where * cap + rank, -1))
    placed = jnp.concatenate(placed, axis=1)

    high = weight.astype(BF16).astype(F32)
    middle = (weight - high).astype(BF16).astype(F32)
    low = weight - high - middle
    features = [
        jnp.where(live, 1.0, 0.0),
        node_high.astype(F32),
        node_low.astype(F32),
        cell_plane.astype(F32),
        cell_group.astype(F32),
        cell_low.astype(F32),
        high,
        middle,
        low,
    ]
    features = [jnp.concatenate([x[q : q + 1] for q in range(groups)], axis=1) for x in features]
    features = jnp.concatenate(
        features + [jnp.zeros((16 - len(features), groups * LANES), F32)], axis=0
    ).astype(BF16)
    placing = (iota((slots, groups * LANES), 0) == placed).astype(F32).astype(BF16)
    packed = matmul(features, placing, (1, 1))
    used = packed[0:1] > 0.5
    code = packed[1:2] * LANES + packed[2:3]
    code = jnp.where(used, code, -1.0)
    slot_high = jnp.where(used, packed[4:5] * plane_rows + packed[3:4], -1.0).astype(jnp.int32)
    slot_low = packed[5:6].astype(jnp.int32)
    slot_weight = packed[6:7] + packed[7:8] + packed[8:9]
    hot = (iota((col_groups * plane_rows, slots), 0) == slot_high).astype(F32).astype(BF16)
    hot_ref[...] = hot
    slot_index_ref[...] = slot_low
    slot_weight_ref[...] = slot_weight

    for c in range(col_groups):
        chunk = matrix_ref[:, :, c * LANES : (c + 1) * LANES].reshape(plane_rows, LANES)
        put_columns(chunk, c, columns_ref)
    picked = pick_low(matmul(columns_ref[...], hot, (1, 0)), slot_low)
    code = from_dense(code, devices, cap)
    slot_code_ref[...] = code.astype(jnp.int32)
    message_ref[:, 0, :] = jnp.where(iota((devices, LANES), 1) < cap, code, -1.0)
    message_ref[:, 1, :] = from_dense(slot_weight, devices, cap)
    message_ref[:, 2, :] = from_dense(slot_weight * picked, devices, cap)
    message_ref[:, 3, :] = jnp.zeros((devices, LANES), F32)
    table = stack_lanes(fracture_ref[...])
    message_ref[:, 4:, :] = jnp.broadcast_to(table[None], (devices,) + table.shape)
    top_ref[...] = matrix_ref[:, 0, :]
    bottom_ref[...] = matrix_ref[:, matrix_ref.shape[1] - 1, :]


def relaxed(now, source, inverse, low_side, high_side, relaxation):
    depth, rows, cols = now.shape
    zero_plane = jnp.zeros((1, rows, cols), F32)
    beside = jnp.concatenate([now[1:], zero_plane], axis=0)
    beside = beside + jnp.concatenate([zero_plane, now[:-1]], axis=0)
    beside = beside + jnp.concatenate([now[:, 1:], high_side[:, None]], axis=1)
    beside = beside + jnp.concatenate([low_side[:, None], now[:, :-1]], axis=1)
    flat = now.reshape(depth * rows, cols)
    place = iota(flat.shape, 1)
    left = jnp.where(place == 0, 0.0, pltpu.roll(flat, 1, 1))
    right = jnp.where(place == cols - 1, 0.0, pltpu.roll(flat, cols - 1, 1))
    beside = beside + (left + right).reshape(now.shape)
    return (1.0 - relaxation) * now + (relaxation * inverse) * (source + beside)


def linked(fracture, links_ref, link_weights_ref):
    total = jnp.zeros(fracture.shape, F32)
    width = fracture.shape[1]
    tables = [fracture[:, i : i + LANES] for i in range(0, width, LANES)]
    sums = []
    for start in range(0, width, LANES):
        total = jnp.zeros(tables[0].shape, F32)
        for j in range(links_ref.shape[0]):
            link = links_ref[j, :, start : start + LANES]
            found = jnp.zeros(tables[0].shape, F32)
            for i, table in enumerate(tables):
                found = jnp.where(
                    link >> log2(LANES) == i, lane_gather(table, link & (LANES - 1)), found
                )
            total = total + link_weights_ref[j, :, start : start + LANES] * found
        sums.append(total)
    return jnp.concatenate(sums, axis=1)


def first_window_kernel(
    relaxation,
    matrix_ref,
    low_side_ref,
    high_side_ref,
    source_ref,
    storage_ref,
    hot_ref,
    slot_index_ref,
    slot_weight_ref,
    fracture_ref,
    links_ref,
    link_weights_ref,
    partial_ref,
    inverse_ref,
    link_sum_ref,
):
    plane_rows = matrix_ref.shape[0] * matrix_ref.shape[1]
    parts = masked_parts(slot_index_ref[...], slot_weight_ref[...])
    added = fold(matmul(hot_ref[...], parts, (1, 1)), 0)
    for c in range(matrix_ref.shape[2] // LANES):
        lanes = slice(c * LANES, (c + 1) * LANES)
        extra = added[c * plane_rows : (c + 1) * plane_rows].reshape(matrix_ref.shape[:2] + (LANES,))
        inverse_ref[:, :, lanes] = 1.0 / (6.0 + storage_ref[:, :, lanes] + extra)
    partial_ref[...] = relaxed(
        matrix_ref[...],
        source_ref[...],
        inverse_ref[...],
        low_side_ref[...],
        high_side_ref[...],
        relaxation,
    )
    link_sum_ref[...] = linked(fracture_ref[...], links_ref, link_weights_ref)


def window_kernel(
    relaxation,
    matrix_ref,
    low_side_ref,
    high_side_ref,
    source_ref,
    inverse_ref,
    fracture_ref,
    links_ref,
    link_weights_ref,
    partial_ref,
    link_sum_ref,
):
    partial_ref[...] = relaxed(
        matrix_ref[...],
        source_ref[...],
        inverse_ref[...],
        low_side_ref[...],
        high_side_ref[...],
        relaxation,
    )
    link_sum_ref[...] = linked(fracture_ref[...], links_ref, link_weights_ref)


def couple(
    relaxation,
    cap,
    returned,
    partial_ref,
    inverse_ref,
    hot_ref,
    slot_index_ref,
    slot_weight_ref,
    matrix_ref,
    columns_ref,
):
    plane_rows = partial_ref.shape[0] * partial_ref.shape[1]
    low = slot_index_ref[...]
    weight = slot_weight_ref[...]
    parts = masked_parts(low, weight * to_dense(returned, cap))
    added = fold(matmul(hot_ref[...], parts, (1, 1)), 0)
    for c in range(partial_ref.shape[2] // LANES):
        lanes = slice(c * LANES, (c + 1) * LANES)
        extra = added[c * plane_rows : (c + 1) * plane_rows].reshape(
            partial_ref.shape[:2] + (LANES,)
        )
        chunk = partial_ref[:, :, lanes] + (relaxation * inverse_ref[:, :, lanes]) * extra
        matrix_ref[:, :, lanes] = chunk
        if columns_ref is not None:
            put_columns(chunk.reshape(plane_rows, LANES), c, columns_ref)
    if columns_ref is None:
        return None
    return weight * pick_low(matmul(columns_ref[...], hot_ref[...], (1, 0)), low)


def node_hot(code, rows):
    return (iota((rows, code.shape[1]), 0) == code >> log2(LANES)).astype(F32).astype(BF16)


def node_values(table, code):
    found = jnp.zeros(code.shape, F32)
    low = code & (LANES - 1)
    for row in range(table.shape[0]):
        values = jnp.broadcast_to(table[row : row + 1], code.shape)
        found = jnp.where(code >> log2(LANES) == row, lane_gather(values, low), found)
    return found


def first_step_kernel(
    relaxation,
    cap,
    arrived_ref,
    slot_code_ref,
    partial_ref,
    inverse_ref,
    hot_ref,
    slot_index_ref,
    slot_weight_ref,
    fracture_ref,
    link_sum_ref,
    fracture_source_ref,
    leak_ref,
    link_weights_ref,
    matrix_ref,
    fracture_next_ref,
    fracture_inverse_ref,
    node_code_ref,
    message_ref,
    top_ref,
    bottom_ref,
    columns_ref,
):
    devices = arrived_ref.shape[0]
    owned = fracture_ref.shape[0]
    slot_code = slot_code_ref[...]
    low = slot_code & (LANES - 1)
    returned = jnp.zeros(slot_code.shape, F32)
    table_rows = arrived_ref.shape[1] - 4
    for row in range(table_rows):
        found = lane_gather(arrived_ref[:, 4 + row, :], low)
        returned = jnp.where(slot_code >> log2(LANES) == row, found, returned)
    outgoing = couple(
        relaxation,
        cap,
        returned,
        partial_ref,
        inverse_ref,
        hot_ref,
        slot_index_ref,
        slot_weight_ref,
        matrix_ref,
        columns_ref,
    )
    code = arrived_ref[:, 0, :].astype(jnp.int32)
    node_code_ref[...] = code
    dense = to_dense(code, cap)
    parts = masked_parts(
        dense & (LANES - 1),
        to_dense(arrived_ref[:, 1, :], cap),
        to_dense(arrived_ref[:, 2, :], cap),
    )
    sums = matmul(node_hot(dense, table_rows), parts, (1, 1))
    diag = (
        leak_ref[...] + jnp.sum(link_weights_ref[...], axis=0) + unstack_lanes(fold(sums, 0), owned)
    )
    inverse = 1.0 / diag
    fracture_inverse_ref[...] = inverse
    fracture_next = (1.0 - relaxation) * fracture_ref[...] + (relaxation * inverse) * (
        fracture_source_ref[...] + link_sum_ref[...] + unstack_lanes(fold(sums, 1), owned)
    )
    fracture_next_ref[...] = fracture_next
    message_ref[:, 0, :] = from_dense(outgoing, devices, cap)
    message_ref[:, 1, :] = node_values(stack_lanes(fracture_next), code)
    top_ref[...] = matrix_ref[:, 0, :]
    bottom_ref[...] = matrix_ref[:, matrix_ref.shape[1] - 1, :]


def step_kernel(
    relaxation,
    cap,
    last,
    arrived_ref,
    node_code_ref,
    partial_ref,
    inverse_ref,
    hot_ref,
    slot_index_ref,
    slot_weight_ref,
    fracture_ref,
    link_sum_ref,
    fracture_source_ref,
    fracture_inverse_ref,
    matrix_ref,
    fracture_next_ref,
    message_ref=None,
    top_ref=None,
    bottom_ref=None,
    columns_ref=None,
):
    devices = arrived_ref.shape[0]
    owned, blk = fracture_ref.shape
    outgoing = couple(
        relaxation,
        cap,
        arrived_ref[:, 1, :],
        partial_ref,
        inverse_ref,
        hot_ref,
        slot_index_ref,
        slot_weight_ref,
        matrix_ref,
        columns_ref,
    )
    code = node_code_ref[...]
    dense = to_dense(code, cap)
    parts = masked_parts(dense & (LANES - 1), to_dense(arrived_ref[:, 0, :], cap))
    sums = matmul(node_hot(dense, owned * blk // LANES), parts, (1, 1))
    fracture_next = (1.0 - relaxation) * fracture_ref[...] + (
        relaxation * fracture_inverse_ref[...]
    ) * (fracture_source_ref[...] + link_sum_ref[...] + unstack_lanes(fold(sums, 0), owned))
    fracture_next_ref[...] = fracture_next
    if last:
        return
    message_ref[:, 0, :] = from_dense(outgoing, devices, cap)
    message_ref[:, 1, :] = node_values(stack_lanes(fracture_next), code)
    top_ref[...] = matrix_ref[:, 0, :]
    bottom_ref[...] = matrix_ref[:, matrix_ref.shape[1] - 1, :]


def call(kernel, outs, ins, name, micros, smem=(), scratch=()):
    bytes_accessed = int(micros * 3.0e6)
    return pl.pallas_call(
        kernel,
        out_shape=[jax.ShapeDtypeStruct(shape, dtype) for shape, dtype in outs],
        in_specs=[
            pl.BlockSpec(memory_space=pltpu.SMEM if i in smem else pltpu.VMEM)
            for i in range(len(ins))
        ],
        out_specs=[pl.BlockSpec(memory_space=pltpu.VMEM) for _ in outs],
        scratch_shapes=list(scratch),
        compiler_params=pltpu.CompilerParams(vmem_limit_bytes=VMEM_LIMIT),
        cost_estimate=pl.CostEstimate(flops=0, bytes_accessed=bytes_accessed, transcendentals=0),
        name=name,
    )(*ins)


def local(
    block_owner,
    transfer_cells,
    transfer_nodes,
    transfer_weights,
    row_counts,
    matrix_start,
    matrix_source,
    matrix_storage,
    fracture_start,
    fracture_source,
    fracture_leak,
    fracture_links,
    link_weights,
):
    devices = lax.axis_size("area")
    depth, area_rows, cols = matrix_start.shape
    owned, blk = fracture_start.shape
    total_rows = transfer_cells.shape[0]
    cap = 3 * total_rows // (2 * devices)
    slots = devices * cap
    cells = depth * area_rows * cols // LANES
    table_rows = owned * blk // LANES
    relax = relax_weights(ITERS)
    grid = (matrix_start.shape, F32)
    fracture = (fracture_start.shape, F32)
    side = ((depth, cols), F32)
    columns = pltpu.VMEM((2 * LANES, cells), BF16)
    padded = (devices, LANES)
    forward = [(i, i + 1) for i in range(devices - 1)]
    backward = [(target, source) for source, target in forward]

    def exchange(message):
        return lax.all_to_all(message, "area", split_axis=0, concat_axis=0, tiled=True)

    def sides(top, bottom):
        return lax.ppermute(bottom, "area", forward), lax.ppermute(top, "area", backward)

    hot, slot_index, slot_weight, slot_code, message, top, bottom = call(
        functools.partial(setup_kernel, devices, cap, owned, blk, cols),
        [
            ((cells, slots), BF16),
            ((1, slots), jnp.int32),
            ((1, slots), F32),
            (padded, jnp.int32),
            ((devices, 4 + table_rows, LANES), F32),
            side,
            side,
        ],
        [
            row_counts,
            block_owner.reshape(-1, LANES),
            transfer_cells.reshape(-1, LANES),
            transfer_nodes.reshape(-1, LANES),
            transfer_weights.reshape(-1, LANES),
            matrix_start,
            fracture_start,
        ],
        "place_rows",
        5.0,
        smem=(0,),
        scratch=[columns],
    )
    arrived = exchange(message)
    low_side, high_side = sides(top, bottom)
    partial, inverse, link_sum = call(
        functools.partial(first_window_kernel, relax[0]),
        [grid, grid, fracture],
        [
            matrix_start,
            low_side,
            high_side,
            matrix_source,
            matrix_storage,
            hot,
            slot_index,
            slot_weight,
            fracture_start,
            fracture_links,
            link_weights,
        ],
        "stencil_first",
        4.0,
    )
    matrix, fracture_now, fracture_inverse, node_code, message, top, bottom = call(
        functools.partial(first_step_kernel, relax[0], cap),
        [grid, fracture, fracture, (padded, jnp.int32), ((devices, 2, LANES), F32), side, side],
        [
            arrived,
            slot_code,
            partial,
            inverse,
            hot,
            slot_index,
            slot_weight,
            fracture_start,
            link_sum,
            fracture_source,
            fracture_leak,
            link_weights,
        ],
        "couple_first",
        4.0,
        scratch=[columns],
    )
    for index in range(1, ITERS):
        last = index == ITERS - 1
        arrived = exchange(message)
        low_side, high_side = sides(top, bottom)
        partial, link_sum = call(
            functools.partial(window_kernel, relax[index]),
            [grid, fracture],
            [
                matrix,
                low_side,
                high_side,
                matrix_source,
                inverse,
                fracture_now,
                fracture_links,
                link_weights,
            ],
            "stencil",
            3.0,
        )
        outs = call(
            functools.partial(step_kernel, relax[index], cap, last),
            [grid, fracture] + ([] if last else [((devices, 2, LANES), F32), side, side]),
            [
                arrived,
                node_code,
                partial,
                inverse,
                hot,
                slot_index,
                slot_weight,
                fracture_now,
                link_sum,
                fracture_source,
                fracture_inverse,
            ],
            "couple",
            3.0,
            scratch=[] if last else [columns],
        )
        matrix, fracture_now = outs[:2]
        if not last:
            message, top, bottom = outs[2:]
    return (matrix, fracture_now)


def solution(mesh):
    in_specs = (
        P(),
        P("area"),
        P("area"),
        P("area"),
        P("area"),
        P("real", "area", None),
        P("real", "area", None),
        P("real", "area", None),
        P("area", "real"),
        P("area", "real"),
        P("area", "real"),
        P(None, "area", None),
        P("real", "area", None),
    )
    out_specs = (P("real", "area", None), P("area", "real"))
    return jax.shard_map(local, mesh=mesh, in_specs=in_specs, out_specs=out_specs, check_vma=False)
```

profile of v0, /device:TPU:0, one launch (start us, length us, event | category | flops | bytes accessed | tf_op | source)
XLA Modules:
  0.0 109.8 jit_solution(9703844302358870367)
XLA Ops:
  5.8 3.0 %place_rows.1 = (bf16[1024,1536]{1,0:T(8,128)(2,1)S(1)}, s32[1,1536]{1,0:T(1,128)S(1)}, f32[1,1536]{1,0:T(1,128)S(1)}, s32[16,128]{1,0:T(8,128)S(1)}, f32[16,20,...) custom-call(s32[1]{0:T(128)S(6)} %copy.15.counts_ref, s32[1,128]{1,0:T(1,128)S(1)} %bitcast.7, ...), custom_call_target="tpu_custom_call" | custom-call | bytes 15000000 | tf_op jit(solution)/shard_map/place_rows/pallas_call | solution.py:461
  9.5 7.4 %all-to-all-start = ((f32[16,20,128]{2,1,0:T(8,128)}), f32[16,20,128]{2,1,0:T(8,128)S(1)}, u32[]{:S(2)}, u32[]{:S(2)}) async-start(f32[16,20,128]{2,1,0:T(8,128)} %copy-done.33), calls=%async_computation | async-start | bytes 393216 | tf_op jit(solution)/shard_map/all_to_all | solution.py:509
  16.8 2.3 %collective-permute-start = (f32[8,1024]{1,0:T(8,128)S(1)}, f32[8,1024]{1,0:T(8,128)S(1)}, u32[]{:S(2)}, u32[]{:S(2)}) collective-permute-start(f32[8,1024]{1,0:T(8,128)S(1)} %get-tuple-element.37), channel_id=1, source_target_pairs={{0,1},{1,2},{2,3},{3,4},{4,5},{5,6},{6,7},{7,8},{8,9},{9,10},{10,1... | collective-permute-start | bytes 98312 | tf_op jit(solution)/shard_map/ppermute | solution.py:512
  19.2 1.3 %collective-permute-start.1 = (f32[8,1024]{1,0:T(8,128)S(1)}, f32[8,1024]{1,0:T(8,128)S(1)}, u32[]{:S(2)}, u32[]{:S(2)}) collective-permute-start(f32[8,1024]{1,0:T(8,128)S(1)} %get-tuple-element.38), channel_id=1, source_target_pairs={{1,0},{2,1},{3,2},{4,3},{5,4},{6,5},{7,6},{8,7},{9,8},{10,9},{11,1... | collective-permute-start | bytes 98312 | tf_op jit(solution)/shard_map/ppermute | solution.py:512
  20.5 2.9 %collective-permute-done.1.high_side_ref = f32[8,1024]{1,0:T(8,128)S(1)} collective-permute-done((f32[8,1024]{1,0:T(8,128)S(1)}, f32[8,1024]{1,0:T(8,128)S(1)}, u32[]{:S(2)}, u32[]{:S(2)}) %collective-permute-start.1) | collective-permute-done | bytes 32800 | tf_op jit(solution)/shard_map/ppermute | solution.py:512
  23.4 1.0 copy-done.8
  24.4 1.0 copy-done.13
  28.7 1.1 %stencil_first.1 = (f32[8,16,1024]{2,1,0:T(8,128)S(1)}, f32[8,16,1024]{2,1,0:T(8,128)S(1)}, f32[8,256]{1,0:T(8,128)S(1)}) custom-call(f32[8,16,1024]{2,1,0:T(8,128)S(1)} %copy-done.13, f32[8,1024]{1,0:T(8,128)S(1)} %collective-permute-done.low_side_ref, f32[8,1024]{1,0:T(8,128)S(1)} %collective-permute-done.1.high_side_ref, f32[8,16,1024]{2,1,0:T(8,128)S(1)} %copy-done.8, ...), custom_call_target="tpu_custom_call" | custom-call | bytes 12000000 | tf_op jit(solution)/shard_map/stencil_first/pallas_call | solution.py:461
  33.6 4.8 %couple_first.1 = (f32[8,16,1024]{2,1,0:T(8,128)S(1)}, f32[8,256]{1,0:T(8,128)S(1)}, f32[8,256]{1,0:T(8,128)S(1)}, s32[16,128]{1,0:T(8,128)S(1)}, f32[16,2,128]{...) custom-call(f32[16,20,128]{2,1,0:T(8,128)S(1)} %all-to-all-done.arrived_ref, ...), custom_call_target="tpu_custom_call" | custom-call | bytes 12000000 | tf_op jit(solution)/shard_map/couple_first/pallas_call | solution.py:461
  39.1 4.5 %collective-permute-start.2 = (f32[8,1024]{1,0:T(8,128)S(1)}, f32[8,1024]{1,0:T(8,128)S(1)}, u32[]{:S(2)}, u32[]{:S(2)}) collective-permute-start(f32[8,1024]{1,0:T(8,128)S(1)} %get-tuple-element.48), channel_id=1, source_target_pairs={{0,1},{1,2},{2,3},{3,4},{4,5},{5,6},{6,7},{7,8},{8,9},{9,10},{10,1... | collective-permute-start | bytes 98312 | tf_op jit(solution)/shard_map/ppermute | solution.py:512
  43.7 1.3 %collective-permute-start.3 = (f32[8,1024]{1,0:T(8,128)S(1)}, f32[8,1024]{1,0:T(8,128)S(1)}, u32[]{:S(2)}, u32[]{:S(2)}) collective-permute-start(f32[8,1024]{1,0:T(8,128)S(1)} %get-tuple-element.49), channel_id=1, source_target_pairs={{1,0},{2,1},{3,2},{4,3},{5,4},{6,5},{7,6},{8,7},{9,8},{10,9},{11,1... | collective-permute-start | bytes 98312 | tf_op jit(solution)/shard_map/ppermute | solution.py:512
  45.0 7.3 %all-to-all-start.1 = ((f32[16,2,128]{2,1,0:T(2,128)}), f32[16,2,128]{2,1,0:T(2,128)S(1)}, u32[]{:S(2)}, u32[]{:S(2)}) async-start(f32[16,2,128]{2,1,0:T(2,128)} %get-tuple-element.45), calls=%async_computation.1 | async-start | bytes 32768 | tf_op jit(solution)/shard_map/all_to_all | solution.py:509
  53.3 1.0 copy-done.9
  54.3 1.0 copy-done.25
  56.7 2.1 %all-to-all-done.1.arrived_ref = f32[16,2,128]{2,1,0:T(2,128)S(1)} async-done(((f32[16,2,128]{2,1,0:T(2,128)}), f32[16,2,128]{2,1,0:T(2,128)S(1)}, u32[]{:S(2)}, u32[]{:S(2)}) %all-to-all-start.1) | async-done | bytes 16416 | tf_op jit(solution)/shard_map/all_to_all | solution.py:509
  58.7 1.0 copy-done.3
  59.8 1.0 copy-done.21
  60.8 4.5 %couple.3 = (f32[8,16,1024]{2,1,0:T(8,128)S(1)}, f32[8,256]{1,0:T(8,128)S(1)}, f32[16,2,128]{2,1,0:T(2,128)}, f32[8,1024]{1,0:T(8,128)S(1)}, f32[8,1024]{1,0:T(8,128)S(1)}) custom-call(f32[16,2,128]{2,1,0:T(2,128)S(1)} %all-to-all-done.1.arrived_ref, s32[16,128]{1,0:T(8,128)S(1)} %get-tuple-element.46.node_code_ref, f32[8,16,1024]{2,1,0:T(8,128)S(1)} %copy-done.21, ...), custom_call_target="tpu_custom_call" | custom-call | bytes 9000000 | tf_op jit(solution)/shard_map/couple/pallas_call | solution.py:461
  66.1 1.6 %collective-permute-start.4 = (f32[8,1024]{1,0:T(8,128)S(1)}, f32[8,1024]{1,0:T(8,128)S(1)}, u32[]{:S(2)}, u32[]{:S(2)}) collective-permute-start(f32[8,1024]{1,0:T(8,128)S(1)} %get-tuple-element.56), channel_id=1, source_target_pairs={{0,1},{1,2},{2,3},{3,4},{4,5},{5,6},{6,7},{7,8},{8,9},{9,10},{10,1... | collective-permute-start | bytes 98312 | tf_op jit(solution)/shard_map/ppermute | solution.py:512
  67.8 1.3 %collective-permute-start.5 = (f32[8,1024]{1,0:T(8,128)S(1)}, f32[8,1024]{1,0:T(8,128)S(1)}, u32[]{:S(2)}, u32[]{:S(2)}) collective-permute-start(f32[8,1024]{1,0:T(8,128)S(1)} %get-tuple-element.57), channel_id=1, source_target_pairs={{1,0},{2,1},{3,2},{4,3},{5,4},{6,5},{7,6},{8,7},{9,8},{10,9},{11,1... | collective-permute-start | bytes 98312 | tf_op jit(solution)/shard_map/ppermute | solution.py:512
  69.1 6.6 %all-to-all-start.2 = ((f32[16,2,128]{2,1,0:T(2,128)}), f32[16,2,128]{2,1,0:T(2,128)S(1)}, u32[]{:S(2)}, u32[]{:S(2)}) async-start(f32[16,2,128]{2,1,0:T(2,128)} %get-tuple-element.54), calls=%async_computation.2 | async-start | bytes 32768 | tf_op jit(solution)/shard_map/all_to_all | solution.py:509
  76.7 1.0 copy-done.10
  80.1 2.1 %all-to-all-done.2.arrived_ref = f32[16,2,128]{2,1,0:T(2,128)S(1)} async-done(((f32[16,2,128]{2,1,0:T(2,128)}), f32[16,2,128]{2,1,0:T(2,128)S(1)}, u32[]{:S(2)}, u32[]{:S(2)}) %all-to-all-start.2) | async-done | bytes 16416 | tf_op jit(solution)/shard_map/all_to_all | solution.py:509
  82.2 1.0 copy-done.5
  83.2 1.0 copy-done.23
  84.2 4.5 %couple.4 = (f32[8,16,1024]{2,1,0:T(8,128)S(1)}, f32[8,256]{1,0:T(8,128)S(1)}, f32[16,2,128]{2,1,0:T(2,128)}, f32[8,1024]{1,0:T(8,128)S(1)}, f32[8,1024]{1,0:T(8,128)S(1)}) custom-call(f32[16,2,128]{2,1,0:T(2,128)S(1)} %all-to-all-done.2.arrived_ref, s32[16,128]{1,0:T(8,128)S(1)} %get-tuple-element.46.node_code_ref, f32[8,16,1024]{2,1,0:T(8,128)S(1)} %copy-done.23, ...), custom_call_target="tpu_custom_call" | custom-call | bytes 9000000 | tf_op jit(solution)/shard_map/couple/pallas_call | solution.py:461
  89.6 1.6 %collective-permute-start.6 = (f32[8,1024]{1,0:T(8,128)S(1)}, f32[8,1024]{1,0:T(8,128)S(1)}, u32[]{:S(2)}, u32[]{:S(2)}) collective-permute-start(f32[8,1024]{1,0:T(8,128)S(1)} %get-tuple-element.63), channel_id=1, source_target_pairs={{0,1},{1,2},{2,3},{3,4},{4,5},{5,6},{6,7},{7,8},{8,9},{9,10},{10,1... | collective-permute-start | bytes 98312 | tf_op jit(solution)/shard_map/ppermute | solution.py:512
  91.2 1.3 %collective-permute-start.7 = (f32[8,1024]{1,0:T(8,128)S(1)}, f32[8,1024]{1,0:T(8,128)S(1)}, u32[]{:S(2)}, u32[]{:S(2)}) collective-permute-start(f32[8,1024]{1,0:T(8,128)S(1)} %get-tuple-element.64), channel_id=1, source_target_pairs={{1,0},{2,1},{3,2},{4,3},{5,4},{6,5},{7,6},{8,7},{9,8},{10,9},{11,1... | collective-permute-start | bytes 98312 | tf_op jit(solution)/shard_map/ppermute | solution.py:512
  92.5 6.6 %all-to-all-start.3 = ((f32[16,2,128]{2,1,0:T(2,128)}), f32[16,2,128]{2,1,0:T(2,128)S(1)}, u32[]{:S(2)}, u32[]{:S(2)}) async-start(f32[16,2,128]{2,1,0:T(2,128)} %get-tuple-element.61), calls=%async_computation.3 | async-start | bytes 32768 | tf_op jit(solution)/shard_map/all_to_all | solution.py:509
  103.5 2.1 %all-to-all-done.3.arrived_ref = f32[16,2,128]{2,1,0:T(2,128)S(1)} async-done(((f32[16,2,128]{2,1,0:T(2,128)}), f32[16,2,128]{2,1,0:T(2,128)S(1)}, u32[]{:S(2)}, u32[]{:S(2)}) %all-to-all-start.3) | async-done | bytes 16416 | tf_op jit(solution)/shard_map/all_to_all | solution.py:509
  105.6 1.0 copy-done.7
  107.7 2.1 %couple.5 = (f32[8,16,1024]{2,1,0:T(8,128)}, f32[8,256]{1,0:T(8,128)}) custom-call(f32[16,2,128]{2,1,0:T(2,128)S(1)} %all-to-all-done.3.arrived_ref, s32[16,128]{1,0:T(8,128)S(1)} %get-tuple-element.46.node_code_ref, f32[8,16,1024]{2,1,0:T(8,128)S(1)} %copy-done.19, f32[8,16,1024]{2,1,0:T(8,128)S(1)} %copy-done.7, ...), custom_call_target="tpu_custom_call" | custom-call | bytes 9000000 | tf_op jit(solution)/shard_map/couple/pallas_call | solution.py:461
  (87 shorter events, 25.5 us)
Async XLA Ops:
  0.6 30.8 %copy-start.34 = (f32[8,256]{1,0:T(8,128)S(1)}, f32[8,256]{1,0:T(8,128)}, u32[]{:S(2)}) copy-start(f32[8,256]{1,0:T(8,128)} %fracture_source_ref.7) | copy-start | bytes 24580
  1.3 1.0 copy-start.12
  5.8 25.7 %copy-start.15 = (f32[4,8,256]{2,1,0:T(8,128)S(1)}, f32[4,8,256]{2,1,0:T(8,128)}, u32[]{:S(2)}) copy-start(f32[4,8,256]{2,1,0:T(8,128)} %link_weights_ref.9) | copy-start | bytes 98308
  5.8 25.7 %copy-start.37 = (f32[8,256]{1,0:T(8,128)S(1)}, f32[8,256]{1,0:T(8,128)}, u32[]{:S(2)}) copy-start(f32[8,256]{1,0:T(8,128)} %fracture_ref.5) | copy-start | bytes 24580
  5.8 25.7 %copy-start.38 = (f32[8,256]{1,0:T(8,128)S(1)}, f32[8,256]{1,0:T(8,128)}, u32[]{:S(2)}) copy-start(f32[8,256]{1,0:T(8,128)} %leak_ref.1) | copy-start | bytes 24580
  9.5 22.0 %all-to-all-start = ((f32[16,20,128]{2,1,0:T(8,128)}), f32[16,20,128]{2,1,0:T(8,128)S(1)}, u32[]{:S(2)}, u32[]{:S(2)}) async-start(f32[16,20,128]{2,1,0:T(8,128)} %copy-done.33), calls=%async_computation | async-start | bytes 393216 | tf_op jit(solution)/shard_map/all_to_all | solution.py:509
  16.8 3.6 %collective-permute-start = (f32[8,1024]{1,0:T(8,128)S(1)}, f32[8,1024]{1,0:T(8,128)S(1)}, u32[]{:S(2)}, u32[]{:S(2)}) collective-permute-start(f32[8,1024]{1,0:T(8,128)S(1)} %get-tuple-element.37), channel_id=1, source_target_pairs={{0,1},{1,2},{2,3},{3,4},{4,5},{5,6},{6,7},{7,8},{8,9},{9,10},{10,1... | collective-permute-start | bytes 98312 | tf_op jit(solution)/shard_map/ppermute | solution.py:512
  19.2 4.2 %collective-permute-start.1 = (f32[8,1024]{1,0:T(8,128)S(1)}, f32[8,1024]{1,0:T(8,128)S(1)}, u32[]{:S(2)}, u32[]{:S(2)}) collective-permute-start(f32[8,1024]{1,0:T(8,128)S(1)} %get-tuple-element.38), channel_id=1, source_target_pairs={{1,0},{2,1},{3,2},{4,3},{5,4},{6,5},{7,6},{8,7},{9,8},{10,9},{11,1... | collective-permute-start | bytes 98312 | tf_op jit(solution)/shard_map/ppermute | solution.py:512
  23.4 1.0 copy-start.8
  24.4 1.0 copy-start.13
  26.2 1.0 copy-start.30
  28.7 23.5 %copy-start.32 = (s32[4,8,256]{2,1,0:T(8,128)S(1)}, s32[4,8,256]{2,1,0:T(8,128)}, u32[]{:S(2)}) copy-start(s32[4,8,256]{2,1,0:T(8,128)} %links_ref.7) | copy-start | bytes 98308
  31.5 1.0 copy-start.1
  32.5 1.0 copy-start.17
  39.1 13.1 %collective-permute-start.2 = (f32[8,1024]{1,0:T(8,128)S(1)}, f32[8,1024]{1,0:T(8,128)S(1)}, u32[]{:S(2)}, u32[]{:S(2)}) collective-permute-start(f32[8,1024]{1,0:T(8,128)S(1)} %get-tuple-element.48), channel_id=1, source_target_pairs={{0,1},{1,2},{2,3},{3,4},{4,5},{5,6},{6,7},{7,8},{8,9},{9,10},{10,1... | collective-permute-start | bytes 98312 | tf_op jit(solution)/shard_map/ppermute | solution.py:512
  43.7 8.6 %collective-permute-start.3 = (f32[8,1024]{1,0:T(8,128)S(1)}, f32[8,1024]{1,0:T(8,128)S(1)}, u32[]{:S(2)}, u32[]{:S(2)}) collective-permute-start(f32[8,1024]{1,0:T(8,128)S(1)} %get-tuple-element.49), channel_id=1, source_target_pairs={{1,0},{2,1},{3,2},{4,3},{5,4},{6,5},{7,6},{8,7},{9,8},{10,9},{11,1... | collective-permute-start | bytes 98312 | tf_op jit(solution)/shard_map/ppermute | solution.py:512
  45.0 13.8 %all-to-all-start.1 = ((f32[16,2,128]{2,1,0:T(2,128)}), f32[16,2,128]{2,1,0:T(2,128)S(1)}, u32[]{:S(2)}, u32[]{:S(2)}) async-start(f32[16,2,128]{2,1,0:T(2,128)} %get-tuple-element.45), calls=%async_computation.1 | async-start | bytes 32768 | tf_op jit(solution)/shard_map/all_to_all | solution.py:509
  52.3 1.0 copy-start.2
  53.3 1.0 copy-start.9
  54.3 1.0 copy-start.25
  58.7 1.0 copy-start.3
  59.8 1.0 copy-start.21
  66.1 9.5 %collective-permute-start.4 = (f32[8,1024]{1,0:T(8,128)S(1)}, f32[8,1024]{1,0:T(8,128)S(1)}, u32[]{:S(2)}, u32[]{:S(2)}) collective-permute-start(f32[8,1024]{1,0:T(8,128)S(1)} %get-tuple-element.56), channel_id=1, source_target_pairs={{0,1},{1,2},{2,3},{3,4},{4,5},{5,6},{6,7},{7,8},{8,9},{9,10},{10,1... | collective-permute-start | bytes 98312 | tf_op jit(solution)/shard_map/ppermute | solution.py:512
  67.8 7.9 %collective-permute-start.5 = (f32[8,1024]{1,0:T(8,128)S(1)}, f32[8,1024]{1,0:T(8,128)S(1)}, u32[]{:S(2)}, u32[]{:S(2)}) collective-permute-start(f32[8,1024]{1,0:T(8,128)S(1)} %get-tuple-element.57), channel_id=1, source_target_pairs={{1,0},{2,1},{3,2},{4,3},{5,4},{6,5},{7,6},{8,7},{9,8},{10,9},{11,1... | collective-permute-start | bytes 98312 | tf_op jit(solution)/shard_map/ppermute | solution.py:512
  69.1 13.1 %all-to-all-start.2 = ((f32[16,2,128]{2,1,0:T(2,128)}), f32[16,2,128]{2,1,0:T(2,128)S(1)}, u32[]{:S(2)}, u32[]{:S(2)}) async-start(f32[16,2,128]{2,1,0:T(2,128)} %get-tuple-element.54), calls=%async_computation.2 | async-start | bytes 32768 | tf_op jit(solution)/shard_map/all_to_all | solution.py:509
  75.7 1.0 copy-start.4
  82.2 1.0 copy-start.5
  89.6 9.5 %collective-permute-start.6 = (f32[8,1024]{1,0:T(8,128)S(1)}, f32[8,1024]{1,0:T(8,128)S(1)}, u32[]{:S(2)}, u32[]{:S(2)}) collective-permute-start(f32[8,1024]{1,0:T(8,128)S(1)} %get-tuple-element.63), channel_id=1, source_target_pairs={{0,1},{1,2},{2,3},{3,4},{4,5},{5,6},{6,7},{7,8},{8,9},{9,10},{10,1... | collective-permute-start | bytes 98312 | tf_op jit(solution)/shard_map/ppermute | solution.py:512
  91.2 7.9 %collective-permute-start.7 = (f32[8,1024]{1,0:T(8,128)S(1)}, f32[8,1024]{1,0:T(8,128)S(1)}, u32[]{:S(2)}, u32[]{:S(2)}) collective-permute-start(f32[8,1024]{1,0:T(8,128)S(1)} %get-tuple-element.64), channel_id=1, source_target_pairs={{1,0},{2,1},{3,2},{4,3},{5,4},{6,5},{7,6},{8,7},{9,8},{10,9},{11,1... | collective-permute-start | bytes 98312 | tf_op jit(solution)/shard_map/ppermute | solution.py:512
  92.5 13.1 %all-to-all-start.3 = ((f32[16,2,128]{2,1,0:T(2,128)}), f32[16,2,128]{2,1,0:T(2,128)S(1)}, u32[]{:S(2)}, u32[]{:S(2)}) async-start(f32[16,2,128]{2,1,0:T(2,128)} %get-tuple-element.61), calls=%async_computation.3 | async-start | bytes 32768 | tf_op jit(solution)/shard_map/all_to_all | solution.py:509
  99.1 1.0 copy-start.6
  105.6 1.0 copy-start.7
  (23 other events, 18.9 us)
where the time goes:
time: 112 us; the launch traced here: 110 us
  starting transfers between devices  43.1 us (38%)
  local copies, waits for them, and re-layouts  34.5 us (31%)
  Pallas kernels  21.4 us (19%)
  waiting for transfers between devices  9.14 us (8%)
  between operations  1.63 us (1%)
    unnamed x86, local copies, waits for them, and re-layouts  34.5 us
    all_to_all x4, starting transfers between devices, exchange(): lax.all_to_all(message, 'area', split_axis=0, concat_axis=0, tiled=True)  27.8 us
    pallas_call x9, Pallas kernels, call(): pl.pallas_call(kernel, out_shape=[jax.ShapeDtypeStruct(shape, dtype) for...  21.4 us
    ppermute x4, starting transfers between devices, sides(): lax.ppermute(bottom, 'area', forward)  10.1 us
    all_to_all x4, waiting for transfers between devices, exchange(): lax.all_to_all(message, 'area', split_axis=0, concat_axis=0, tiled=True)  6.19 us
    ppermute x4, starting transfers between devices, sides(): lax.ppermute(top, 'area', backward)  5.17 us
    ppermute x4, waiting for transfers between devices, sides(): lax.ppermute(top, 'area', backward)  2.94 us
  transfers between devices with their start and end apart: 12, of which 4 were waited for; matrix products, arithmetic and copies ran while one was open for 0% of the time, Pallas kernels for 2%

commit v1 on v0

--- a/solution.py
+++ b/solution.py
@@ -9,6 +9,7 @@
 from jax.sharding import PartitionSpec as P
 
 ITERS = 4
+HALO = ITERS - 1
 LANES = 128
 F32 = jnp.float32
 BF16 = jnp.bfloat16
@@ -93,35 +94,35 @@
     columns_ref[LANES:, index * LANES : (index + 1) * LANES] = low
 
 
-def setup_kernel(
-    devices,
-    cap,
-    owned,
-    blk,
-    cols,
-    counts_ref,
-    owner_ref,
-    cells_ref,
-    nodes_ref,
-    weights_ref,
-    matrix_ref,
-    fracture_ref,
-    hot_ref,
-    slot_index_ref,
-    slot_weight_ref,
-    slot_code_ref,
-    message_ref,
-    top_ref,
-    bottom_ref,
-    columns_ref,
-):
+def fill_hot(hot_ref, slot_high):
+    for start in range(0, hot_ref.shape[0], LANES):
+        rows = iota((LANES, slot_high.shape[1]), 0) + start
+        hot_ref[start : start + LANES, :] = (rows == slot_high).astype(F32).astype(BF16)
+
+
+def setup_kernel(devices, cap, staged, *refs):
+    sources, refs = refs[:staged], refs[staged:]
+    slot_index_ref, slot_weight_ref, slot_code_ref, message_hbm, up_hbm, down_hbm = refs[:6]
+    targets, refs = refs[6 : 6 + staged], refs[6 + staged :]
+    message_ref, up_ref, down_ref, hot_ref, columns_ref, sems = refs
+    copies = [
+        pltpu.make_async_copy(sources[i], targets[i], sems.at[i]) for i in range(staged)
+    ]
+    for copy in copies:
+        copy.start()
+    for copy in copies[:5]:
+        copy.wait()
+    counts_ref, owner_ref, cells_ref, nodes_ref, weights_ref = targets[:5]
+    matrix_ref, fracture_ref, source_ref, storage_ref = targets[5:]
+    owned, blk = fracture_ref.shape
+    depth, area_rows, cols = matrix_ref.shape
     groups = cells_ref.shape[0]
     slots = devices * cap
     plane_rows = matrix_ref.shape[0] * matrix_ref.shape[1]
     col_groups = cols // LANES
     shape = (groups, LANES)
     nodes, cells = nodes_ref[...], cells_ref[...]
-    live = iota(shape, 0) * LANES + iota(shape, 1) < counts_ref[0]
+    live = iota(shape, 0) * LANES + iota(shape, 1) < counts_ref[...]
     weight = jnp.where(live, weights_ref[...], 0.0)
     block = nodes >> log2(blk)
     slot = jnp.zeros(shape, jnp.int32)
@@ -177,25 +178,53 @@
     slot_high = jnp.where(used, packed[4:5] * plane_rows + packed[3:4], -1.0).astype(jnp.int32)
     slot_low = packed[5:6].astype(jnp.int32)
     slot_weight = packed[6:7] + packed[7:8] + packed[8:9]
-    hot = (iota((col_groups * plane_rows, slots), 0) == slot_high).astype(F32).astype(BF16)
-    hot_ref[...] = hot
-    slot_index_ref[...] = slot_low
+    fill_hot(hot_ref, slot_high)
+    slot_index_ref[0:1] = slot_high
+    slot_index_ref[1:2] = slot_low
     slot_weight_ref[...] = slot_weight
-
+    padded_code = from_dense(code, devices, cap)
+    slot_code_ref[...] = padded_code.astype(jnp.int32)
+    message_ref[:, 0, :] = jnp.where(iota((devices, LANES), 1) < cap, padded_code, -1.0)
+    message_ref[:, 1, :] = from_dense(slot_weight, devices, cap)
+    message_ref[:, 3, :] = jnp.zeros((devices, LANES), F32)
+
+    row = slot_high & (area_rows - 1)
+    plane = (slot_high >> log2(area_rows)) & (depth - 1)
+    group = slot_high >> log2(plane_rows)
+    for far, side_ref in ((area_rows - 1 - row, up_ref), (row, down_ref)):
+        place = (group * HALO + far) * depth + plane
+        place = jnp.where(used & (far < HALO), place, -1).astype(F32)
+        half = slots // 2
+        for i, x in enumerate((place, packed[5:6], slot_weight, code)):
+            side_ref[3 * HALO + 1, 2 * i : 2 * i + 1, :half] = x[:, :half]
+            side_ref[3 * HALO + 1, 2 * i + 1 : 2 * i + 2, :half] = x[:, half:]
+
+    for copy in copies[5:]:
+        copy.wait()
+    table = stack_lanes(fracture_ref[...])
+    message_ref[:, 4:, :] = jnp.broadcast_to(table[None], (devices,) + table.shape)
     for c in range(col_groups):
         chunk = matrix_ref[:, :, c * LANES : (c + 1) * LANES].reshape(plane_rows, LANES)
         put_columns(chunk, c, columns_ref)
-    picked = pick_low(matmul(columns_ref[...], hot, (1, 0)), slot_low)
-    code = from_dense(code, devices, cap)
-    slot_code_ref[...] = code.astype(jnp.int32)
-    message_ref[:, 0, :] = jnp.where(iota((devices, LANES), 1) < cap, code, -1.0)
-    message_ref[:, 1, :] = from_dense(slot_weight, devices, cap)
+    for far in range(HALO + 1):
+        up_ref[far] = matrix_ref[:, area_rows - 1 - far, :]
+        down_ref[far] = matrix_ref[:, far, :]
+    for start, ref in ((HALO + 1, source_ref), (2 * HALO + 1, storage_ref)):
+        for far in range(HALO):
+            up_ref[start + far] = ref[:, area_rows - 1 - far, :]
+            down_ref[start + far] = ref[:, far, :]
+    outs = [
+        pltpu.make_async_copy(up_ref, up_hbm, sems.at[staged]),
+        pltpu.make_async_copy(down_ref, down_hbm, sems.at[staged + 1]),
+        pltpu.make_async_copy(message_ref, message_hbm, sems.at[staged + 2]),
+    ]
+    outs[0].start()
+    outs[1].start()
+    picked = pick_low(matmul(columns_ref[...], hot_ref[...], (1, 0)), slot_low)
     message_ref[:, 2, :] = from_dense(slot_weight * picked, devices, cap)
-    message_ref[:, 3, :] = jnp.zeros((devices, LANES), F32)
-    table = stack_lanes(fracture_ref[...])
-    message_ref[:, 4:, :] = jnp.broadcast_to(table[None], (devices,) + table.shape)
-    top_ref[...] = matrix_ref[:, 0, :]
-    bottom_ref[...] = matrix_ref[:, matrix_ref.shape[1] - 1, :]
+    outs[2].start()
+    for out in outs:
+        out.wait()
 
 
 def relaxed(now, source, inverse, low_side, high_side, relaxation):
@@ -210,7 +239,7 @@
     left = jnp.where(place == 0, 0.0, pltpu.roll(flat, 1, 1))
     right = jnp.where(place == cols - 1, 0.0, pltpu.roll(flat, cols - 1, 1))
     beside = beside + (left + right).reshape(now.shape)
-    return (1.0 - relaxation) * now + (relaxation * inverse) * (source + beside)
+    return (1.0 - relaxation) * now + relaxation * (source + inverse * beside)
 
 
 def linked(fracture, links_ref, link_weights_ref):
@@ -232,60 +261,178 @@
     return jnp.concatenate(sums, axis=1)
 
 
+def relaxed_side(now, beyond, edge, scaled, inverse, relaxation):
+    depth, cols = edge.shape
+    place = iota(edge.shape, 1)
+    zero_plane = jnp.zeros((1, cols), F32)
+    after = []
+    for far in range(HALO):
+        here = now[far]
+        beside = jnp.concatenate([here[1:], zero_plane], axis=0)
+        beside = beside + jnp.concatenate([zero_plane, here[:-1]], axis=0)
+        beside = beside + jnp.where(place == 0, 0.0, pltpu.roll(here, 1, 1))
+        beside = beside + jnp.where(place == cols - 1, 0.0, pltpu.roll(here, cols - 1, 1))
+        beside = beside + (edge if far == 0 else now[far - 1])
+        if far + 1 < HALO:
+            beside = beside + now[far + 1]
+        elif beyond is not None:
+            beside = beside + beyond
+        after.append(
+            (1.0 - relaxation) * here + relaxation * (scaled[far] + inverse[far] * beside)
+        )
+    return after
+
+
+def side_slots(side_ref, slots):
+    half = slots // 2
+    return [
+        jnp.concatenate(
+            [side_ref[3 * HALO + 1, i : i + 1, :half] for i in (2 * j, 2 * j + 1)], axis=1
+        )
+        for j in range(4)
+    ]
+
+
+def spread_side(place, low, values, depth, col_groups):
+    rows = iota((col_groups * HALO * depth, place.shape[1]), 0)
+    hot = (rows == place).astype(F32).astype(BF16)
+    added = fold(matmul(hot, masked_parts(low, values), (1, 1)), 0)
+    return [
+        jnp.concatenate(
+            [
+                added[(group * HALO + far) * depth : (group * HALO + far + 1) * depth]
+                for group in range(col_groups)
+            ],
+            axis=1,
+        )
+        for far in range(HALO)
+    ]
+
+
 def first_window_kernel(
     relaxation,
     matrix_ref,
-    low_side_ref,
-    high_side_ref,
+    low_ref,
+    high_ref,
     source_ref,
     storage_ref,
-    hot_ref,
     slot_index_ref,
     slot_weight_ref,
     fracture_ref,
     links_ref,
     link_weights_ref,
     partial_ref,
+    scaled_ref,
     inverse_ref,
+    side_partial_ref,
+    side_scaled_ref,
+    side_inverse_ref,
     link_sum_ref,
+    hot_ref,
 ):
-    plane_rows = matrix_ref.shape[0] * matrix_ref.shape[1]
-    parts = masked_parts(slot_index_ref[...], slot_weight_ref[...])
+    depth, area_rows, cols = matrix_ref.shape
+    plane_rows = depth * area_rows
+    slots = slot_index_ref.shape[1]
+    fill_hot(hot_ref, slot_index_ref[0:1])
+    parts = masked_parts(slot_index_ref[1:2], slot_weight_ref[...])
     added = fold(matmul(hot_ref[...], parts, (1, 1)), 0)
-    for c in range(matrix_ref.shape[2] // LANES):
+    for c in range(cols // LANES):
         lanes = slice(c * LANES, (c + 1) * LANES)
-        extra = added[c * plane_rows : (c + 1) * plane_rows].reshape(matrix_ref.shape[:2] + (LANES,))
-        inverse_ref[:, :, lanes] = 1.0 / (6.0 + storage_ref[:, :, lanes] + extra)
+        extra = added[c * plane_rows : (c + 1) * plane_rows].reshape(depth, area_rows, LANES)
+        inverse = 1.0 / (6.0 + storage_ref[:, :, lanes] + extra)
+        scaled_ref[:, :, lanes] = source_ref[:, :, lanes] * inverse
+        inverse_ref[:, :, lanes] = inverse
     partial_ref[...] = relaxed(
         matrix_ref[...],
-        source_ref[...],
+        scaled_ref[...],
         inverse_ref[...],
-        low_side_ref[...],
-        high_side_ref[...],
+        low_ref[0],
+        high_ref[0],
         relaxation,
     )
+    for side, (ref, edge) in enumerate(((low_ref, 0), (high_ref, area_rows - 1))):
+        place, low, weight, _ = side_slots(ref, slots)
+        added = spread_side(
+            place.astype(jnp.int32), low.astype(jnp.int32), weight, depth, cols // LANES
+        )
+        for far in range(HALO):
+            storage = ref[2 * HALO + 1 + far]
+            inverse = jnp.where(storage > 0.0, 1.0 / (6.0 + storage + added[far]), 0.0)
+            side_inverse_ref[side, far] = inverse
+            side_scaled_ref[side, far] = ref[HALO + 1 + far] * inverse
+        after = relaxed_side(
+            [ref[far] for far in range(HALO)],
+            ref[HALO],
+            matrix_ref[:, edge, :],
+            [side_scaled_ref[side, far] for far in range(HALO)],
+            [side_inverse_ref[side, far] for far in range(HALO)],
+            relaxation,
+        )
+        for far in range(HALO):
+            side_partial_ref[side, far] = after[far]
     link_sum_ref[...] = linked(fracture_ref[...], links_ref, link_weights_ref)
 
 
 def window_kernel(
     relaxation,
+    before,
+    cap,
+    first,
+    arrived_ref,
+    low_ref,
+    high_ref,
     matrix_ref,
-    low_side_ref,
-    high_side_ref,
-    source_ref,
+    scaled_ref,
     inverse_ref,
+    side_before_ref,
+    side_scaled_ref,
+    side_inverse_ref,
     fracture_ref,
     links_ref,
     link_weights_ref,
     partial_ref,
+    side_partial_ref,
     link_sum_ref,
 ):
+    depth, area_rows, cols = matrix_ref.shape
+    devices = arrived_ref.shape[0]
+    slots = devices * cap
+    edges = []
+    for side, (ref, edge) in enumerate(((low_ref, 0), (high_ref, area_rows - 1))):
+        place, low, weight, code = side_slots(ref, slots)
+        if first:
+            code = from_dense(code, devices, cap).astype(jnp.int32)
+            returned = device_values(arrived_ref, code)
+        else:
+            returned = arrived_ref[:, 2 + side, :]
+        added = spread_side(
+            place.astype(jnp.int32),
+            low.astype(jnp.int32),
+            weight * to_dense(returned, cap),
+            depth,
+            cols // LANES,
+        )
+        now = [
+            side_before_ref[side, far] + before * side_inverse_ref[side, far] * added[far]
+            for far in range(HALO)
+        ]
+        edges.append(now[0])
+        after = relaxed_side(
+            now,
+            None,
+            matrix_ref[:, edge, :],
+            [side_scaled_ref[side, far] for far in range(HALO)],
+            [side_inverse_ref[side, far] for far in range(HALO)],
+            relaxation,
+        )
+        for far in range(HALO):
+            side_partial_ref[side, far] = after[far]
     partial_ref[...] = relaxed(
         matrix_ref[...],
-        source_ref[...],
+        scaled_ref[...],
         inverse_ref[...],
-        low_side_ref[...],
-        high_side_ref[...],
+        edges[0],
+        edges[1],
         relaxation,
     )
     link_sum_ref[...] = linked(fracture_ref[...], links_ref, link_weights_ref)
@@ -304,7 +451,8 @@
     columns_ref,
 ):
     plane_rows = partial_ref.shape[0] * partial_ref.shape[1]
-    low = slot_index_ref[...]
+    fill_hot(hot_ref, slot_index_ref[0:1])
+    low = slot_index_ref[1:2]
     weight = slot_weight_ref[...]
     parts = masked_parts(low, weight * to_dense(returned, cap))
     added = fold(matmul(hot_ref[...], parts, (1, 1)), 0)
@@ -335,6 +483,22 @@
     return found
 
 
+def device_values(arrived_ref, code):
+    found = jnp.zeros(code.shape, F32)
+    low = code & (LANES - 1)
+    for row in range(arrived_ref.shape[1] - 4):
+        values = lane_gather(arrived_ref[:, 4 + row, :], low)
+        found = jnp.where(code >> log2(LANES) == row, values, found)
+    return found
+
+
+def put_requested(message_ref, values):
+    zero = jnp.zeros((1, LANES), F32)
+    message_ref[:, 1, :] = values
+    message_ref[:, 2, :] = jnp.concatenate([zero, values[:-1]], axis=0)
+    message_ref[:, 3, :] = jnp.concatenate([values[1:], zero], axis=0)
+
+
 def first_step_kernel(
     relaxation,
     cap,
@@ -342,7 +506,6 @@
     slot_code_ref,
     partial_ref,
     inverse_ref,
-    hot_ref,
     slot_index_ref,
     slot_weight_ref,
     fracture_ref,
@@ -354,20 +517,16 @@
     fracture_next_ref,
     fracture_inverse_ref,
     node_code_ref,
+    message_hbm,
+    hot_ref,
+    columns_ref,
     message_ref,
-    top_ref,
-    bottom_ref,
-    columns_ref,
+    sem,
 ):
     devices = arrived_ref.shape[0]
     owned = fracture_ref.shape[0]
-    slot_code = slot_code_ref[...]
-    low = slot_code & (LANES - 1)
-    returned = jnp.zeros(slot_code.shape, F32)
+    returned = device_values(arrived_ref, slot_code_ref[...])
     table_rows = arrived_ref.shape[1] - 4
-    for row in range(table_rows):
-        found = lane_gather(arrived_ref[:, 4 + row, :], low)
-        returned = jnp.where(slot_code >> log2(LANES) == row, found, returned)
     outgoing = couple(
         relaxation,
         cap,
@@ -399,9 +558,10 @@
     )
     fracture_next_ref[...] = fracture_next
     message_ref[:, 0, :] = from_dense(outgoing, devices, cap)
-    message_ref[:, 1, :] = node_values(stack_lanes(fracture_next), code)
-    top_ref[...] = matrix_ref[:, 0, :]
-    bottom_ref[...] = matrix_ref[:, matrix_ref.shape[1] - 1, :]
+    put_requested(message_ref, node_values(stack_lanes(fracture_next), code))
+    out = pltpu.make_async_copy(message_ref, message_hbm, sem)
+    out.start()
+    out.wait()
 
 
 def step_kernel(
@@ -412,7 +572,6 @@
     node_code_ref,
     partial_ref,
     inverse_ref,
-    hot_ref,
     slot_index_ref,
     slot_weight_ref,
     fracture_ref,
@@ -421,11 +580,13 @@
     fracture_inverse_ref,
     matrix_ref,
     fracture_next_ref,
-    message_ref=None,
-    top_ref=None,
-    bottom_ref=None,
-    columns_ref=None,
+    *refs,
 ):
+    if last:
+        (hot_ref,) = refs
+        columns_ref = None
+    else:
+        message_hbm, hot_ref, columns_ref, message_ref, sem = refs
     devices = arrived_ref.shape[0]
     owned, blk = fracture_ref.shape
     outgoing = couple(
@@ -451,24 +612,30 @@
     if last:
         return
     message_ref[:, 0, :] = from_dense(outgoing, devices, cap)
-    message_ref[:, 1, :] = node_values(stack_lanes(fracture_next), code)
-    top_ref[...] = matrix_ref[:, 0, :]
-    bottom_ref[...] = matrix_ref[:, matrix_ref.shape[1] - 1, :]
-
-
-def call(kernel, outs, ins, name, micros, smem=(), scratch=()):
-    bytes_accessed = int(micros * 3.0e6)
+    put_requested(message_ref, node_values(stack_lanes(fracture_next), code))
+    out = pltpu.make_async_copy(message_ref, message_hbm, sem)
+    out.start()
+    out.wait()
+
+
+def call(kernel, outs, ins, name, micros, hbm_in=(), hbm_out=(), scratch=(), aliases=None, limit=VMEM_LIMIT):
     return pl.pallas_call(
         kernel,
         out_shape=[jax.ShapeDtypeStruct(shape, dtype) for shape, dtype in outs],
         in_specs=[
-            pl.BlockSpec(memory_space=pltpu.SMEM if i in smem else pltpu.VMEM)
+            pl.BlockSpec(memory_space=pltpu.HBM if i in hbm_in else pltpu.VMEM)
             for i in range(len(ins))
         ],
-        out_specs=[pl.BlockSpec(memory_space=pltpu.VMEM) for _ in outs],
+        out_specs=[
+            pl.BlockSpec(memory_space=pltpu.HBM if i in hbm_out else pltpu.VMEM)
+            for i in range(len(outs))
+        ],
         scratch_shapes=list(scratch),
-        compiler_params=pltpu.CompilerParams(vmem_limit_bytes=VMEM_LIMIT),
-        cost_estimate=pl.CostEstimate(flops=0, bytes_accessed=bytes_accessed, transcendentals=0),
+        input_output_aliases=aliases or {},
+        compiler_params=pltpu.CompilerParams(vmem_limit_bytes=limit),
+        cost_estimate=pl.CostEstimate(
+            flops=0, bytes_accessed=int(micros * 3.0e6), transcendentals=0
+        ),
         name=name,
     )(*ins)
 
@@ -499,55 +666,68 @@
     relax = relax_weights(ITERS)
     grid = (matrix_start.shape, F32)
     fracture = (fracture_start.shape, F32)
-    side = ((depth, cols), F32)
+    side = ((3 * HALO + 2, depth, cols), F32)
+    sides = ((2, HALO, depth, cols), F32)
+    hot = pltpu.VMEM((cells, slots), BF16)
     columns = pltpu.VMEM((2 * LANES, cells), BF16)
     padded = (devices, LANES)
+    first_message = ((devices, 4 + table_rows, LANES), F32)
+    later_message = ((devices, 4, LANES), F32)
     forward = [(i, i + 1) for i in range(devices - 1)]
     backward = [(target, source) for source, target in forward]
 
     def exchange(message):
         return lax.all_to_all(message, "area", split_axis=0, concat_axis=0, tiled=True)
 
-    def sides(top, bottom):
-        return lax.ppermute(bottom, "area", forward), lax.ppermute(top, "area", backward)
-
-    hot, slot_index, slot_weight, slot_code, message, top, bottom = call(
-        functools.partial(setup_kernel, devices, cap, owned, blk, cols),
+    staged = [
+        row_counts.reshape(1, 1),
+        block_owner.reshape(-1, LANES),
+        transfer_cells.reshape(-1, LANES),
+        transfer_nodes.reshape(-1, LANES),
+        transfer_weights.reshape(-1, LANES),
+        matrix_start,
+        fracture_start,
+        matrix_source,
+        matrix_storage,
+    ]
+    slot_index, slot_weight, slot_code, message, up, down = call(
+        functools.partial(setup_kernel, devices, cap, len(staged)),
         [
-            ((cells, slots), BF16),
-            ((1, slots), jnp.int32),
+            ((2, slots), jnp.int32),
             ((1, slots), F32),
             (padded, jnp.int32),
-            ((devices, 4 + table_rows, LANES), F32),
+            first_message,
             side,
             side,
         ],
-        [
-            row_counts,
-            block_owner.reshape(-1, LANES),
-            transfer_cells.reshape(-1, LANES),
-            transfer_nodes.reshape(-1, LANES),
-            transfer_weights.reshape(-1, LANES),
-            matrix_start,
-            fracture_start,
-        ],
+        staged,
         "place_rows",
         5.0,
-        smem=(0,),
-        scratch=[columns],
+        hbm_in=range(len(staged)),
+        hbm_out=(3, 4, 5),
+        scratch=[pltpu.VMEM(x.shape, x.dtype) for x in staged]
+        + [
+            pltpu.VMEM(*first_message),
+            pltpu.VMEM(*side),
+            pltpu.VMEM(*side),
+            hot,
+            columns,
+            pltpu.SemaphoreType.DMA((len(staged) + 3,)),
+        ],
+        limit=63 * 1024 * 1024,
     )
     arrived = exchange(message)
-    low_side, high_side = sides(top, bottom)
-    partial, inverse, link_sum = call(
+    low = lax.ppermute(up, "area", forward)
+    high = lax.ppermute(down, "area", backward)
+    partial, scaled, inverse, side_partial, side_scaled, side_inverse, link_sum = call(
         functools.partial(first_window_kernel, relax[0]),
-        [grid, grid, fracture],
+        [grid, grid, grid, sides, sides, sides, fracture],
         [
             matrix_start,
-            low_side,
-            high_side,
+            low,
+            high,
             matrix_source,
             matrix_storage,
-            hot,
             slot_index,
             slot_weight,
             fracture_start,
@@ -556,19 +736,20 @@
         ],
         "stencil_first",
         4.0,
-    )
-    matrix, fracture_now, fracture_inverse, node_code, message, top, bottom = call(
+        scratch=[hot],
+    )
+    fracture_now = fracture_start
+    matrix, fracture_now, fracture_inverse, node_code, message = call(
         functools.partial(first_step_kernel, relax[0], cap),
-        [grid, fracture, fracture, (padded, jnp.int32), ((devices, 2, LANES), F32), side, side],
+        [grid, fracture, fracture, (padded, jnp.int32), later_message],
         [
             arrived,
             slot_code,
             partial,
             inverse,
-            hot,
             slot_index,
             slot_weight,
-            fracture_start,
+            fracture_now,
             link_sum,
             fracture_source,
             fracture_leak,
@@ -576,37 +757,41 @@
         ],
         "couple_first",
         4.0,
-        scratch=[columns],
+        hbm_out=(4,),
+        scratch=[hot, columns, pltpu.VMEM(*later_message), pltpu.SemaphoreType.DMA],
     )
     for index in range(1, ITERS):
         last = index == ITERS - 1
-        arrived = exchange(message)
-        low_side, high_side = sides(top, bottom)
-        partial, link_sum = call(
-            functools.partial(window_kernel, relax[index]),
-            [grid, fracture],
+        old, arrived = arrived, exchange(message)
+        partial, side_partial, link_sum = call(
+            functools.partial(window_kernel, relax[index], relax[index - 1], cap, index == 1),
+            [grid, sides, fracture],
             [
+                old,
+                low,
+                high,
                 matrix,
-                low_side,
-                high_side,
-                matrix_source,
+                scaled,
                 inverse,
+                side_partial,
+                side_scaled,
+                side_inverse,
                 fracture_now,
                 fracture_links,
                 link_weights,
             ],
             "stencil",
             3.0,
+            aliases={6: 1},
         )
         outs = call(
             functools.partial(step_kernel, relax[index], cap, last),
-            [grid, fracture] + ([] if last else [((devices, 2, LANES), F32), side, side]),
+            [grid, fracture] + ([] if last else [later_message]),
             [
                 arrived,
                 node_code,
                 partial,
                 inverse,
-                hot,
                 slot_index,
                 slot_weight,
                 fracture_now,
@@ -616,11 +801,13 @@
             ],
             "couple",
             3.0,
-            scratch=[] if last else [columns],
+            hbm_out=() if last else (2,),
+            scratch=[hot]
+            + ([] if last else [columns, pltpu.VMEM(*later_message), pltpu.SemaphoreType.DMA]),
         )
         matrix, fracture_now = outs[:2]
         if not last:
-            message, top, bottom = outs[2:]
+            message = outs[2]
     return (matrix, fracture_now)
 
 

time: 112 us -> 79.2 us (0.71); the launches traced: 110 us -> 78.4 us
  local copies, waits for them, and re-layouts: 34.5 us -> 9.42 us
  starting transfers between devices: 43.1 us -> 23.7 us
  waiting for transfers between devices: 9.14 us -> 16.5 us
  Pallas kernels: 21.4 us -> 27.1 us
    unnamed x86 -> x38, local copies, waits for them, and re-layouts: 34.5 us -> 9.42 us
    ppermute x8 -> x2, starting transfers between devices: 15.3 us -> 3.67 us  [the longest x1 2.38 us: local(): low = lax.ppermute(up, 'area', forward)]
    all_to_all x4, waiting for transfers between devices: 6.19 us -> 16.5 us  [exchange(): lax.all_to_all(message, 'area', split_axis=0, concat_axis=0, tiled=True)]
    all_to_all x4, starting transfers between devices: 27.8 us -> 20.1 us  [exchange(): lax.all_to_all(message, 'area', split_axis=0, concat_axis=0, tiled=True)]
    pallas_call x9, Pallas kernels: 21.4 us -> 27.1 us  [call(): pl.pallas_call(kernel, out_shape=[jax.ShapeDtypeStruct(shape, dtype) for...]
    ppermute x8 -> x2, waiting for transfers between devices: 2.95 us -> 0.01 us  [the longest x1 0.01 us: local(): high = lax.ppermute(down, 'area', backward)]
  transfers between devices with their start and end apart: 12 -> 6, of which waited for: 4 -> 4; matrix products, arithmetic and copies ran while one was open for 0% -> 0% of each run, Pallas kernels for 2% -> 8%
where the time goes in v1:
time: 79.2 us; the launch traced here: 78.4 us
  Pallas kernels  27.1 us (34%)
  starting transfers between devices  23.7 us (30%)
  waiting for transfers between devices  16.5 us (21%)
  local copies, waits for them, and re-layouts  9.42 us (12%)
  between operations  1.58 us (2%)
    pallas_call x9, Pallas kernels, call(): pl.pallas_call(kernel, out_shape=[jax.ShapeDtypeStruct(shape, dtype) for...  27.1 us
    all_to_all x4, starting transfers between devices, exchange(): lax.all_to_all(message, 'area', split_axis=0, concat_axis=0, tiled=True)  20.1 us
    all_to_all x4, waiting for transfers between devices, exchange(): lax.all_to_all(message, 'area', split_axis=0, concat_axis=0, tiled=True)  16.5 us
    unnamed x38, local copies, waits for them, and re-layouts  9.42 us
    ppermute x1, starting transfers between devices, local(): low = lax.ppermute(up, 'area', forward)  2.38 us
  transfers between devices with their start and end apart: 6, of which 4 were waited for; matrix products, arithmetic and copies ran while one was open for 0% of the time, Pallas kernels for 8%

profile of v1, /device:TPU:0, one launch (start us, length us, event | category | flops | bytes accessed | tf_op | source)
XLA Modules:
  0.0 78.4 jit_solution(927427926764847689)
XLA Ops:
  1.3 5.0 %place_rows.1 = (s32[2,1536]{1,0:T(2,128)}, f32[1,1536]{1,0:T(1,128)}, s32[16,128]{1,0:T(8,128)}, f32[16,20,128]{2,1,0:T(8,128)}, f32[11,8,1024]{2,1,0:T(8,128)}, /*index=5*/f32[11,8,1024]{2,1,0:T(8,128)}) custom-call(s32[1,1]{1,0:T(1,128)} %bitcast.5.refs_0_, s32[1,128]{1,0:T(1,128)} %bitcast.9, s32[8,128]{1,0:T(8,128)} %bitcast.6, s32[8,128]{1,0:T(8,128)} %bitcast.7, ...), custom_call_target="tpu_custom_call" | custom-call | bytes 15000000 | tf_op jit(solution)/shard_map/place_rows/pallas_call | solution.py:622
  6.3 2.4 %collective-permute-start = (f32[11,8,1024]{2,1,0:T(8,128)}, f32[11,8,1024]{2,1,0:T(8,128)S(1)}, u32[]{:S(2)}, u32[]{:S(2)}) collective-permute-start(f32[11,8,1024]{2,1,0:T(8,128)} %get-tuple-element.36), channel_id=1, source_target_pairs={{0,1},{1,2},{2,3},{3,4},{4,5},{5,6},{6,7},{7,8},{8,9},{9,10},{10,1... | collective-permute-start | bytes 1081352 | tf_op jit(solution)/shard_map/ppermute | solution.py:720
  8.6 1.3 %collective-permute-start.1 = (f32[11,8,1024]{2,1,0:T(8,128)}, f32[11,8,1024]{2,1,0:T(8,128)S(1)}, u32[]{:S(2)}, u32[]{:S(2)}) collective-permute-start(f32[11,8,1024]{2,1,0:T(8,128)} %get-tuple-element.37), channel_id=1, source_target_pairs={{1,0},{2,1},{3,2},{4,3},{5,4},{6,5},{7,6},{8,7},{9,8},{10,9},{11,1... | collective-permute-start | bytes 1081352 | tf_op jit(solution)/shard_map/ppermute | solution.py:721
  9.9 0.0 copy-start.3
  9.9 0.0 copy-start.4
  10.0 9.4 %all-to-all-start = ((f32[16,20,128]{2,1,0:T(8,128)}), f32[16,20,128]{2,1,0:T(8,128)S(1)}, u32[]{:S(2)}, u32[]{:S(2)}) async-start(f32[16,20,128]{2,1,0:T(8,128)} %get-tuple-element.34), calls=%async_computation | async-start | bytes 393216 | tf_op jit(solution)/shard_map/all_to_all | solution.py:680
  19.5 0.0 copy-start.1
  19.5 1.0 %copy-done.1 = f32[8,16,1024]{2,1,0:T(8,128)S(1)} copy-done((f32[8,16,1024]{2,1,0:T(8,128)S(1)}, f32[8,16,1024]{2,1,0:T(8,128)}, u32[]{:S(2)}) %copy-start.1) | copy-done | bytes 524312
  20.6 1.0 %copy-done.2 = f32[8,16,1024]{2,1,0:T(8,128)S(1)} copy-done((f32[8,16,1024]{2,1,0:T(8,128)S(1)}, f32[8,16,1024]{2,1,0:T(8,128)}, u32[]{:S(2)}) %copy-start.2) | copy-done | bytes 524312
  21.6 1.9 %stencil_first.1 = (f32[8,16,1024]{2,1,0:T(8,128)S(1)}, f32[8,16,1024]{2,1,0:T(8,128)S(1)}, f32[8,16,1024]{2,1,0:T(8,128)S(1)}, f32[2,3,8,1024]{3,2,1,0:T(8,128)...) custom-call(f32[8,16,1024]{2,1,0:T(8,128)S(1)} %copy-done, ...), custom_call_target="tpu_custom_call" | custom-call | bytes 12000000 | tf_op jit(solution)/shard_map/stencil_first/pallas_call | solution.py:622
  23.5 0.8 copy-done.5
  24.3 4.1 %all-to-all-done.arrived_ref = f32[16,20,128]{2,1,0:T(8,128)S(1)} async-done(((f32[16,20,128]{2,1,0:T(8,128)}), f32[16,20,128]{2,1,0:T(8,128)S(1)}, u32[]{:S(2)}, u32[]{:S(2)}) %all-to-all-start) | async-done | bytes 163872 | tf_op jit(solution)/shard_map/all_to_all | solution.py:680
  28.4 1.0 %copy-done.6 = f32[8,16,1024]{2,1,0:T(8,128)S(1)} copy-done((f32[8,16,1024]{2,1,0:T(8,128)S(1)}, f32[8,16,1024]{2,1,0:T(8,128)}, u32[]{:S(2)}) %copy-start.6) | copy-done | bytes 524312
  29.5 4.8 %couple_first.1 = (f32[8,16,1024]{2,1,0:T(8,128)S(1)}, f32[8,256]{1,0:T(8,128)S(1)}, f32[8,256]{1,0:T(8,128)S(1)}, s32[16,128]{1,0:T(8,128)S(1)}, f32[16,4,128]{2,1,0:T(4,128)}) custom-call(f32[16,20,128]{2,1,0:T(8,128)S(1)} %all-to-all-done.arrived_ref, s32[16,128]{1,0:T(8,128)S(1)} %copy-done.18, f32[8,16,1024]{2,1,0:T(8,128)S(1)} %copy-done.6, ...), custom_call_target="tpu_custom_call" | custom-call | bytes 12000000 | tf_op jit(solution)/shard_map/couple_first/pallas_call | solution.py:622
  34.3 0.8 copy-done.9
  35.1 3.5 %all-to-all-start.1 = ((f32[16,4,128]{2,1,0:T(4,128)}), f32[16,4,128]{2,1,0:T(4,128)S(1)}, u32[]{:S(2)}, u32[]{:S(2)}) async-start(f32[16,4,128]{2,1,0:T(4,128)} %get-tuple-element.43), calls=%async_computation.1 | async-start | bytes 65536 | tf_op jit(solution)/shard_map/all_to_all | solution.py:680
  38.6 1.0 %copy-done.10 = f32[8,16,1024]{2,1,0:T(8,128)S(1)} copy-done((f32[8,16,1024]{2,1,0:T(8,128)S(1)}, f32[8,16,1024]{2,1,0:T(8,128)}, u32[]{:S(2)}) %copy-start.10) | copy-done | bytes 524312
  39.6 1.6 %stencil.3 = (f32[8,16,1024]{2,1,0:T(8,128)S(1)}, f32[2,3,8,1024]{3,2,1,0:T(8,128)S(1)}, f32[8,256]{1,0:T(8,128)S(1)}) custom-call(f32[16,20,128]{2,1,0:T(8,128)S(1)} %all-to-all-done.arrived_ref, f32[11,8,1024]{2,1,0:T(8,128)S(1)} %collective-permute-done.low_ref, ...), custom_call_target="tpu_custom_call", output_to_operand_aliasing={{1}: (6, {})} | custom-call | bytes 9000000 | tf_op jit(solution)/shard_map/stencil/pallas_call | solution.py:622
  41.2 3.9 %all-to-all-done.1.arrived_ref = f32[16,4,128]{2,1,0:T(4,128)S(1)} async-done(((f32[16,4,128]{2,1,0:T(4,128)}), f32[16,4,128]{2,1,0:T(4,128)S(1)}, u32[]{:S(2)}, u32[]{:S(2)}) %all-to-all-start.1) | async-done | bytes 32800 | tf_op jit(solution)/shard_map/all_to_all | solution.py:680
  45.2 4.6 %couple.3 = (f32[8,16,1024]{2,1,0:T(8,128)S(1)}, f32[8,256]{1,0:T(8,128)S(1)}, f32[16,4,128]{2,1,0:T(4,128)}) custom-call(f32[16,4,128]{2,1,0:T(4,128)S(1)} %all-to-all-done.1.arrived_ref, s32[16,128]{1,0:T(8,128)S(1)} %get-tuple-element.44.node_code_ref, f32[8,16,1024]{2,1,0:T(8,128)S(1)} %get-tuple-element.51.partial_ref, ...), custom_call_target="tpu_custom_call" | custom-call | bytes 9000000 | tf_op jit(solution)/shard_map/couple/pallas_call | solution.py:622
  49.8 0.8 copy-done.11
  50.5 3.7 %all-to-all-start.2 = ((f32[16,4,128]{2,1,0:T(4,128)}), f32[16,4,128]{2,1,0:T(4,128)S(1)}, u32[]{:S(2)}, u32[]{:S(2)}) async-start(f32[16,4,128]{2,1,0:T(4,128)} %get-tuple-element.54), calls=%async_computation.2 | async-start | bytes 65536 | tf_op jit(solution)/shard_map/all_to_all | solution.py:680
  54.2 1.0 %copy-done.12 = f32[8,16,1024]{2,1,0:T(8,128)S(1)} copy-done((f32[8,16,1024]{2,1,0:T(8,128)S(1)}, f32[8,16,1024]{2,1,0:T(8,128)}, u32[]{:S(2)}) %copy-start.12) | copy-done | bytes 524312
  55.3 1.3 %stencil.4 = (f32[8,16,1024]{2,1,0:T(8,128)S(1)}, f32[2,3,8,1024]{3,2,1,0:T(8,128)S(1)}, f32[8,256]{1,0:T(8,128)S(1)}) custom-call(f32[16,4,128]{2,1,0:T(4,128)S(1)} %all-to-all-done.1.arrived_ref, f32[11,8,1024]{2,1,0:T(8,128)S(1)} %collective-permute-done.low_ref, ...), custom_call_target="tpu_custom_call", output_to_operand_aliasing={{1}: (6, {})} | custom-call | bytes 9000000 | tf_op jit(solution)/shard_map/stencil/pallas_call | solution.py:622
  56.6 4.2 %all-to-all-done.2.arrived_ref = f32[16,4,128]{2,1,0:T(4,128)S(1)} async-done(((f32[16,4,128]{2,1,0:T(4,128)}), f32[16,4,128]{2,1,0:T(4,128)S(1)}, u32[]{:S(2)}, u32[]{:S(2)}) %all-to-all-start.2) | async-done | bytes 32800 | tf_op jit(solution)/shard_map/all_to_all | solution.py:680
  60.8 4.6 %couple.4 = (f32[8,16,1024]{2,1,0:T(8,128)S(1)}, f32[8,256]{1,0:T(8,128)S(1)}, f32[16,4,128]{2,1,0:T(4,128)}) custom-call(f32[16,4,128]{2,1,0:T(4,128)S(1)} %all-to-all-done.2.arrived_ref, s32[16,128]{1,0:T(8,128)S(1)} %get-tuple-element.44.node_code_ref, f32[8,16,1024]{2,1,0:T(8,128)S(1)} %get-tuple-element.58.partial_ref, ...), custom_call_target="tpu_custom_call" | custom-call | bytes 9000000 | tf_op jit(solution)/shard_map/couple/pallas_call | solution.py:622
  65.4 0.8 copy-done.7
  66.2 3.5 %all-to-all-start.3 = ((f32[16,4,128]{2,1,0:T(4,128)}), f32[16,4,128]{2,1,0:T(4,128)S(1)}, u32[]{:S(2)}, u32[]{:S(2)}) async-start(f32[16,4,128]{2,1,0:T(4,128)} %get-tuple-element.60), calls=%async_computation.3 | async-start | bytes 65536 | tf_op jit(solution)/shard_map/all_to_all | solution.py:680
  69.7 1.0 %copy-done.8 = f32[8,16,1024]{2,1,0:T(8,128)S(1)} copy-done((f32[8,16,1024]{2,1,0:T(8,128)S(1)}, f32[8,16,1024]{2,1,0:T(8,128)}, u32[]{:S(2)}) %copy-start.8) | copy-done | bytes 524312
  70.7 1.3 %stencil.5 = (f32[8,16,1024]{2,1,0:T(8,128)S(1)}, f32[2,3,8,1024]{3,2,1,0:T(8,128)S(1)}, f32[8,256]{1,0:T(8,128)S(1)}) custom-call(f32[16,4,128]{2,1,0:T(4,128)S(1)} %all-to-all-done.2.arrived_ref, f32[11,8,1024]{2,1,0:T(8,128)S(1)} %collective-permute-done.low_ref, ...), custom_call_target="tpu_custom_call", output_to_operand_aliasing={{1}: (6, {})} | custom-call | bytes 9000000 | tf_op jit(solution)/shard_map/stencil/pallas_call | solution.py:622
  72.1 4.2 %all-to-all-done.3.arrived_ref = f32[16,4,128]{2,1,0:T(4,128)S(1)} async-done(((f32[16,4,128]{2,1,0:T(4,128)}), f32[16,4,128]{2,1,0:T(4,128)S(1)}, u32[]{:S(2)}, u32[]{:S(2)}) %all-to-all-start.3) | async-done | bytes 32800 | tf_op jit(solution)/shard_map/all_to_all | solution.py:680
  76.3 2.1 %couple.5 = (f32[8,16,1024]{2,1,0:T(8,128)}, f32[8,256]{1,0:T(8,128)}) custom-call(f32[16,4,128]{2,1,0:T(4,128)S(1)} %all-to-all-done.3.arrived_ref, s32[16,128]{1,0:T(8,128)S(1)} %get-tuple-element.44.node_code_ref, f32[8,16,1024]{2,1,0:T(8,128)S(1)} %get-tuple-element.64.partial_ref, f32[8,16,1024]{2,1,0:T(8,128)S(1)} %get-tuple-element.41.inverse_ref, ...), custom_call_target="tpu_custom_call" | custom-call | bytes 9000000 | tf_op jit(solution)/shard_map/couple/pallas_call | solution.py:622
  (27 shorter events, 0.1 us)
Async XLA Ops:
  1.3 18.2 %copy-start = (f32[8,16,1024]{2,1,0:T(8,128)S(1)}, f32[8,16,1024]{2,1,0:T(8,128)}, u32[]{:S(2)}) copy-start(f32[8,16,1024]{2,1,0:T(8,128)} %matrix_ref.1) | copy-start | bytes 1572868
  6.3 13.2 %collective-permute-start = (f32[11,8,1024]{2,1,0:T(8,128)}, f32[11,8,1024]{2,1,0:T(8,128)S(1)}, u32[]{:S(2)}, u32[]{:S(2)}) collective-permute-start(f32[11,8,1024]{2,1,0:T(8,128)} %get-tuple-element.36), channel_id=1, source_target_pairs={{0,1},{1,2},{2,3},{3,4},{4,5},{5,6},{6,7},{7,8},{8,9},{9,10},{10,1... | collective-permute-start | bytes 1081352 | tf_op jit(solution)/shard_map/ppermute | solution.py:720
  8.6 10.8 %collective-permute-start.1 = (f32[11,8,1024]{2,1,0:T(8,128)}, f32[11,8,1024]{2,1,0:T(8,128)S(1)}, u32[]{:S(2)}, u32[]{:S(2)}) collective-permute-start(f32[11,8,1024]{2,1,0:T(8,128)} %get-tuple-element.37), channel_id=1, source_target_pairs={{1,0},{2,1},{3,2},{4,3},{5,4},{6,5},{7,6},{8,7},{9,8},{10,9},{11,1... | collective-permute-start | bytes 1081352 | tf_op jit(solution)/shard_map/ppermute | solution.py:721
  9.9 9.5 %copy-start.3 = (f32[4,8,256]{2,1,0:T(8,128)S(1)}, f32[4,8,256]{2,1,0:T(8,128)}, u32[]{:S(2)}) copy-start(f32[4,8,256]{2,1,0:T(8,128)} %link_weights_ref.9) | copy-start | bytes 98308
  9.9 9.5 %copy-start.4 = (s32[4,8,256]{2,1,0:T(8,128)S(1)}, s32[4,8,256]{2,1,0:T(8,128)}, u32[]{:S(2)}) copy-start(s32[4,8,256]{2,1,0:T(8,128)} %links_ref.7) | copy-start | bytes 98308
  10.0 9.5 %copy-start.13 = (s32[2,1536]{1,0:T(2,128)S(1)}, s32[2,1536]{1,0:T(2,128)}, u32[]{:S(2)}) copy-start(s32[2,1536]{1,0:T(2,128)} %get-tuple-element.38.slot_index_ref) | copy-start | bytes 36868
  10.0 9.5 %copy-start.14 = (f32[1,1536]{1,0:T(1,128)S(1)}, f32[1,1536]{1,0:T(1,128)}, u32[]{:S(2)}) copy-start(f32[1,1536]{1,0:T(1,128)} %get-tuple-element.39.slot_weight_ref) | copy-start | bytes 18436
  10.0 9.5 %copy-start.16 = (f32[8,256]{1,0:T(8,128)S(1)}, f32[8,256]{1,0:T(8,128)}, u32[]{:S(2)}) copy-start(f32[8,256]{1,0:T(8,128)} %fracture_ref.3) | copy-start | bytes 24580
  10.0 18.4 %all-to-all-start = ((f32[16,20,128]{2,1,0:T(8,128)}), f32[16,20,128]{2,1,0:T(8,128)S(1)}, u32[]{:S(2)}, u32[]{:S(2)}) async-start(f32[16,20,128]{2,1,0:T(8,128)} %get-tuple-element.34), calls=%async_computation | async-start | bytes 393216 | tf_op jit(solution)/shard_map/all_to_all | solution.py:680
  19.5 1.0 %copy-start.1 = (f32[8,16,1024]{2,1,0:T(8,128)S(1)}, f32[8,16,1024]{2,1,0:T(8,128)}, u32[]{:S(2)}) copy-start(f32[8,16,1024]{2,1,0:T(8,128)} %source_ref.1) | copy-start | bytes 1572868
  20.5 1.0 %copy-start.2 = (f32[8,16,1024]{2,1,0:T(8,128)S(1)}, f32[8,16,1024]{2,1,0:T(8,128)}, u32[]{:S(2)}) copy-start(f32[8,16,1024]{2,1,0:T(8,128)} %storage_ref.1) | copy-start | bytes 1572868
  21.6 6.8 %copy-start.15 = (f32[8,256]{1,0:T(8,128)S(1)}, f32[8,256]{1,0:T(8,128)}, u32[]{:S(2)}) copy-start(f32[8,256]{1,0:T(8,128)} %fracture_source_ref.7) | copy-start | bytes 24580
  21.6 6.8 %copy-start.17 = (f32[8,256]{1,0:T(8,128)S(1)}, f32[8,256]{1,0:T(8,128)}, u32[]{:S(2)}) copy-start(f32[8,256]{1,0:T(8,128)} %leak_ref.1) | copy-start | bytes 24580
  21.6 6.8 %copy-start.18 = (s32[16,128]{1,0:T(8,128)S(1)}, s32[16,128]{1,0:T(8,128)}, u32[]{:S(2)}) copy-start(s32[16,128]{1,0:T(8,128)} %get-tuple-element.35.slot_code_ref) | copy-start | bytes 24580
  23.5 0.8 %copy-start.5 = (f32[8,16,1024]{2,1,0:T(8,128)}, f32[8,16,1024]{2,1,0:T(8,128)S(1)}, u32[]{:S(2)}) copy-start(f32[8,16,1024]{2,1,0:T(8,128)S(1)} %get-tuple-element.40.partial_ref) | copy-start | bytes 1572868
  28.4 1.0 %copy-start.6 = (f32[8,16,1024]{2,1,0:T(8,128)S(1)}, f32[8,16,1024]{2,1,0:T(8,128)}, u32[]{:S(2)}) copy-start(f32[8,16,1024]{2,1,0:T(8,128)} %copy-done.5) | copy-start | bytes 1572868
  34.3 0.8 %copy-start.9 = (f32[8,16,1024]{2,1,0:T(8,128)}, f32[8,16,1024]{2,1,0:T(8,128)S(1)}, u32[]{:S(2)}) copy-start(f32[8,16,1024]{2,1,0:T(8,128)S(1)} %get-tuple-element.45.matrix_ref) | copy-start | bytes 1572868
  35.1 10.1 %all-to-all-start.1 = ((f32[16,4,128]{2,1,0:T(4,128)}), f32[16,4,128]{2,1,0:T(4,128)S(1)}, u32[]{:S(2)}, u32[]{:S(2)}) async-start(f32[16,4,128]{2,1,0:T(4,128)} %get-tuple-element.43), calls=%async_computation.1 | async-start | bytes 65536 | tf_op jit(solution)/shard_map/all_to_all | solution.py:680
  38.6 1.0 %copy-start.10 = (f32[8,16,1024]{2,1,0:T(8,128)S(1)}, f32[8,16,1024]{2,1,0:T(8,128)}, u32[]{:S(2)}) copy-start(f32[8,16,1024]{2,1,0:T(8,128)} %copy-done.9) | copy-start | bytes 1572868
  49.7 0.8 %copy-start.11 = (f32[8,16,1024]{2,1,0:T(8,128)}, f32[8,16,1024]{2,1,0:T(8,128)S(1)}, u32[]{:S(2)}) copy-start(f32[8,16,1024]{2,1,0:T(8,128)S(1)} %get-tuple-element.55.matrix_ref) | copy-start | bytes 1572868
  50.5 10.3 %all-to-all-start.2 = ((f32[16,4,128]{2,1,0:T(4,128)}), f32[16,4,128]{2,1,0:T(4,128)S(1)}, u32[]{:S(2)}, u32[]{:S(2)}) async-start(f32[16,4,128]{2,1,0:T(4,128)} %get-tuple-element.54), calls=%async_computation.2 | async-start | bytes 65536 | tf_op jit(solution)/shard_map/all_to_all | solution.py:680
  54.2 1.0 %copy-start.12 = (f32[8,16,1024]{2,1,0:T(8,128)S(1)}, f32[8,16,1024]{2,1,0:T(8,128)}, u32[]{:S(2)}) copy-start(f32[8,16,1024]{2,1,0:T(8,128)} %copy-done.11) | copy-start | bytes 1572868
  65.4 0.8 %copy-start.7 = (f32[8,16,1024]{2,1,0:T(8,128)}, f32[8,16,1024]{2,1,0:T(8,128)S(1)}, u32[]{:S(2)}) copy-start(f32[8,16,1024]{2,1,0:T(8,128)S(1)} %get-tuple-element.61.matrix_ref) | copy-start | bytes 1572868
  66.2 10.1 %all-to-all-start.3 = ((f32[16,4,128]{2,1,0:T(4,128)}), f32[16,4,128]{2,1,0:T(4,128)S(1)}, u32[]{:S(2)}, u32[]{:S(2)}) async-start(f32[16,4,128]{2,1,0:T(4,128)} %get-tuple-element.60), calls=%async_computation.3 | async-start | bytes 65536 | tf_op jit(solution)/shard_map/all_to_all | solution.py:680
  69.7 1.0 %copy-start.8 = (f32[8,16,1024]{2,1,0:T(8,128)S(1)}, f32[8,16,1024]{2,1,0:T(8,128)}, u32[]{:S(2)}) copy-start(f32[8,16,1024]{2,1,0:T(8,128)} %copy-done.7) | copy-start | bytes 1572868

commit v2 on v1

--- a/solution.py
+++ b/solution.py
@@ -26,6 +26,11 @@
 def log2(value):
     assert value & (value - 1) == 0
     return value.bit_length() - 1
+
+
+def group_order(devices):
+    part = devices // 4
+    return [quarter * part + (i - 1) % part for quarter in (2, 0, 1, 3) for i in range(part)]
 
 
 def iota(shape, dim):
@@ -102,8 +107,9 @@
 
 def setup_kernel(devices, cap, staged, *refs):
     sources, refs = refs[:staged], refs[staged:]
-    slot_index_ref, slot_weight_ref, slot_code_ref, message_hbm, up_hbm, down_hbm = refs[:6]
-    targets, refs = refs[6 : 6 + staged], refs[6 + staged :]
+    slot_index_ref, slot_weight_ref, slot_code_ref, cell_rows_ref, cell_columns_ref = refs[:5]
+    message_hbm, up_hbm, down_hbm = refs[5:8]
+    targets, refs = refs[8 : 8 + staged], refs[8 + staged :]
     message_ref, up_ref, down_ref, hot_ref, columns_ref, sems = refs
     copies = [
         pltpu.make_async_copy(sources[i], targets[i], sems.at[i]) for i in range(staged)
@@ -130,7 +136,11 @@
         table = jnp.broadcast_to(owner_ref[part : part + 1, :], shape)
         found = lane_gather(table, block & (LANES - 1))
         slot = jnp.where(block >> log2(LANES) == part, found, slot)
-    target = jnp.where(live, slot >> log2(owned), -1)
+    device = slot >> log2(owned)
+    target = jnp.zeros(shape, jnp.int32)
+    for position, member in enumerate(group_order(devices)):
+        target = jnp.where(device == member, position, target)
+    target = jnp.where(live, target, -1)
     node_high = ((nodes & (blk - 1)) >> log2(LANES)) * owned + (slot & (owned - 1))
     node_low = nodes & (LANES - 1)
     cell_plane = cells >> log2(cols)
@@ -188,29 +198,32 @@
     message_ref[:, 1, :] = from_dense(slot_weight, devices, cap)
     message_ref[:, 3, :] = jnp.zeros((devices, LANES), F32)
 
+    cell = jnp.where(used, (slot_high * LANES + slot_low).astype(F32), -1.0)
+    rows = stack_lanes(cell)
+    cell_rows_ref[...] = rows
+    cell_columns_ref[...] = turned(rows)
+
     row = slot_high & (area_rows - 1)
     plane = (slot_high >> log2(area_rows)) & (depth - 1)
     group = slot_high >> log2(plane_rows)
+    half = slots // 2
     for far, side_ref in ((area_rows - 1 - row, up_ref), (row, down_ref)):
         place = (group * HALO + far) * depth + plane
         place = jnp.where(used & (far < HALO), place, -1).astype(F32)
-        half = slots // 2
         for i, x in enumerate((place, packed[5:6], slot_weight, code)):
             side_ref[3 * HALO + 1, 2 * i : 2 * i + 1, :half] = x[:, :half]
             side_ref[3 * HALO + 1, 2 * i + 1 : 2 * i + 2, :half] = x[:, half:]
 
     for copy in copies[5:]:
         copy.wait()
-    table = stack_lanes(fracture_ref[...])
-    message_ref[:, 4:, :] = jnp.broadcast_to(table[None], (devices,) + table.shape)
-    for c in range(col_groups):
-        chunk = matrix_ref[:, :, c * LANES : (c + 1) * LANES].reshape(plane_rows, LANES)
-        put_columns(chunk, c, columns_ref)
-    for far in range(HALO + 1):
-        up_ref[far] = matrix_ref[:, area_rows - 1 - far, :]
-        down_ref[far] = matrix_ref[:, far, :]
-    for start, ref in ((HALO + 1, source_ref), (2 * HALO + 1, storage_ref)):
-        for far in range(HALO):
+    nodes_table = stack_lanes(fracture_ref[...])
+    message_ref[:, 4:, :] = jnp.broadcast_to(nodes_table[None], (devices,) + nodes_table.shape)
+    for ref, start, count in (
+        (matrix_ref, 0, HALO + 1),
+        (source_ref, HALO + 1, HALO),
+        (storage_ref, 2 * HALO + 1, HALO),
+    ):
+        for far in range(count):
             up_ref[start + far] = ref[:, area_rows - 1 - far, :]
             down_ref[start + far] = ref[:, far, :]
     outs = [
@@ -220,11 +233,35 @@
     ]
     outs[0].start()
     outs[1].start()
+    for c in range(col_groups):
+        chunk = matrix_ref[:, :, c * LANES : (c + 1) * LANES].reshape(plane_rows, LANES)
+        put_columns(chunk, c, columns_ref)
     picked = pick_low(matmul(columns_ref[...], hot_ref[...], (1, 0)), slot_low)
     message_ref[:, 2, :] = from_dense(slot_weight * picked, devices, cap)
     outs[2].start()
     for out in outs:
         out.wait()
+
+
+def turned(rows):
+    count = rows.shape[0]
+    extra = -count % 8
+    if extra:
+        rows = jnp.concatenate([rows, jnp.zeros((extra, LANES), rows.dtype)], axis=0)
+    return rows.T
+
+
+def same_cell_sum(values, cell_rows, cell_columns):
+    value_columns = turned(stack_lanes(values))
+    blocks = cell_rows.shape[0]
+    sums = [jnp.zeros((8, LANES), F32) for _ in range(blocks)]
+    for j in range(blocks):
+        cell = jnp.broadcast_to(cell_columns[:, j : j + 1], (LANES, LANES))
+        value = jnp.broadcast_to(value_columns[:, j : j + 1], (LANES, LANES))
+        for i in range(blocks):
+            hit = jnp.where(cell == cell_rows[i : i + 1], value, 0.0)
+            sums[i] = sums[i] + jnp.sum(hit.reshape(LANES // 8, 8, LANES), axis=0)
+    return jnp.concatenate([jnp.sum(x, axis=0, keepdims=True) for x in sums], axis=1)
 
 
 def relaxed(now, source, inverse, low_side, high_side, relaxation):
@@ -309,39 +346,64 @@
     ]
 
 
+def pick_cells(table_ref, columns_ref, hot_ref, low):
+    depth, area_rows, cols = table_ref.shape
+    for c in range(cols // LANES):
+        chunk = table_ref[:, :, c * LANES : (c + 1) * LANES]
+        put_columns(chunk.reshape(depth * area_rows, LANES), c, columns_ref)
+    return pick_low(matmul(columns_ref[...], hot_ref[...], (1, 0)), low)
+
+
+def diagonal_kernel(
+    source_ref,
+    storage_ref,
+    slot_index_ref,
+    slot_weight_ref,
+    scaled_ref,
+    inverse_ref,
+    row_inverse_ref,
+    hot_ref,
+    columns_ref,
+):
+    depth, area_rows, cols = source_ref.shape
+    plane_rows = depth * area_rows
+    low = slot_index_ref[1:2]
+    weight = slot_weight_ref[...]
+    fill_hot(hot_ref, slot_index_ref[0:1])
+    added = fold(matmul(hot_ref[...], masked_parts(low, weight), (1, 1)), 0)
+    for c in range(cols // LANES):
+        lanes = slice(c * LANES, (c + 1) * LANES)
+        extra = added[c * plane_rows : (c + 1) * plane_rows].reshape(depth, area_rows, LANES)
+        inverse = 1.0 / (6.0 + storage_ref[:, :, lanes] + extra)
+        scaled_ref[:, :, lanes] = source_ref[:, :, lanes] * inverse
+        inverse_ref[:, :, lanes] = inverse
+    row_inverse_ref[...] = weight * pick_cells(inverse_ref, columns_ref, hot_ref, low)
+
+
 def first_window_kernel(
     relaxation,
     matrix_ref,
     low_ref,
     high_ref,
-    source_ref,
-    storage_ref,
+    scaled_ref,
+    inverse_ref,
     slot_index_ref,
     slot_weight_ref,
     fracture_ref,
     links_ref,
     link_weights_ref,
     partial_ref,
-    scaled_ref,
-    inverse_ref,
     side_partial_ref,
     side_scaled_ref,
     side_inverse_ref,
+    row_partial_ref,
     link_sum_ref,
     hot_ref,
+    columns_ref,
 ):
     depth, area_rows, cols = matrix_ref.shape
-    plane_rows = depth * area_rows
     slots = slot_index_ref.shape[1]
     fill_hot(hot_ref, slot_index_ref[0:1])
-    parts = masked_parts(slot_index_ref[1:2], slot_weight_ref[...])
-    added = fold(matmul(hot_ref[...], parts, (1, 1)), 0)
-    for c in range(cols // LANES):
-        lanes = slice(c * LANES, (c + 1) * LANES)
-        extra = added[c * plane_rows : (c + 1) * plane_rows].reshape(depth, area_rows, LANES)
-        inverse = 1.0 / (6.0 + storage_ref[:, :, lanes] + extra)
-        scaled_ref[:, :, lanes] = source_ref[:, :, lanes] * inverse
-        inverse_ref[:, :, lanes] = inverse
     partial_ref[...] = relaxed(
         matrix_ref[...],
         scaled_ref[...],
@@ -349,6 +411,9 @@
         low_ref[0],
         high_ref[0],
         relaxation,
+    )
+    row_partial_ref[...] = slot_weight_ref[...] * pick_cells(
+        partial_ref, columns_ref, hot_ref, slot_index_ref[1:2]
     )
     for side, (ref, edge) in enumerate(((low_ref, 0), (high_ref, area_rows - 1))):
         place, low, weight, _ = side_slots(ref, slots)
@@ -373,30 +438,55 @@
     link_sum_ref[...] = linked(fracture_ref[...], links_ref, link_weights_ref)
 
 
+def add_rows(relaxation, values, partial_ref, inverse_ref, slot_index_ref, hot_ref, matrix_ref):
+    depth, area_rows, cols = partial_ref.shape
+    plane_rows = depth * area_rows
+    fill_hot(hot_ref, slot_index_ref[0:1])
+    added = fold(matmul(hot_ref[...], masked_parts(slot_index_ref[1:2], values), (1, 1)), 0)
+    for c in range(cols // LANES):
+        lanes = slice(c * LANES, (c + 1) * LANES)
+        extra = added[c * plane_rows : (c + 1) * plane_rows].reshape(depth, area_rows, LANES)
+        matrix_ref[:, :, lanes] = (
+            partial_ref[:, :, lanes] + (relaxation * inverse_ref[:, :, lanes]) * extra
+        )
+
+
 def window_kernel(
     relaxation,
     before,
     cap,
     first,
+    last,
     arrived_ref,
     low_ref,
     high_ref,
-    matrix_ref,
+    partial_before_ref,
     scaled_ref,
     inverse_ref,
     side_before_ref,
     side_scaled_ref,
     side_inverse_ref,
+    slot_index_ref,
+    slot_weight_ref,
+    slot_code_ref,
     fracture_ref,
     links_ref,
     link_weights_ref,
     partial_ref,
     side_partial_ref,
     link_sum_ref,
+    *refs,
 ):
-    depth, area_rows, cols = matrix_ref.shape
+    if last:
+        matrix_ref, hot_ref = refs
+    else:
+        row_partial_ref, matrix_ref, hot_ref, columns_ref = refs
+    depth, area_rows, cols = scaled_ref.shape
     devices = arrived_ref.shape[0]
     slots = devices * cap
+    returned = device_values(arrived_ref, slot_code_ref[...]) if first else arrived_ref[:, 1, :]
+    values = slot_weight_ref[...] * to_dense(returned, cap)
+    add_rows(before, values, partial_before_ref, inverse_ref, slot_index_ref, hot_ref, matrix_ref)
     edges = []
     for side, (ref, edge) in enumerate(((low_ref, 0), (high_ref, area_rows - 1))):
         place, low, weight, code = side_slots(ref, slots)
@@ -435,39 +525,27 @@
         edges[1],
         relaxation,
     )
+    if not last:
+        row_partial_ref[...] = slot_weight_ref[...] * pick_cells(
+            partial_ref, columns_ref, hot_ref, slot_index_ref[1:2]
+        )
     link_sum_ref[...] = linked(fracture_ref[...], links_ref, link_weights_ref)
 
 
-def couple(
+def row_values(
     relaxation,
     cap,
     returned,
-    partial_ref,
-    inverse_ref,
-    hot_ref,
-    slot_index_ref,
     slot_weight_ref,
-    matrix_ref,
-    columns_ref,
+    row_partial_ref,
+    row_inverse_ref,
+    cell_rows_ref,
+    cell_columns_ref,
 ):
-    plane_rows = partial_ref.shape[0] * partial_ref.shape[1]
-    fill_hot(hot_ref, slot_index_ref[0:1])
-    low = slot_index_ref[1:2]
-    weight = slot_weight_ref[...]
-    parts = masked_parts(low, weight * to_dense(returned, cap))
-    added = fold(matmul(hot_ref[...], parts, (1, 1)), 0)
-    for c in range(partial_ref.shape[2] // LANES):
-        lanes = slice(c * LANES, (c + 1) * LANES)
-        extra = added[c * plane_rows : (c + 1) * plane_rows].reshape(
-            partial_ref.shape[:2] + (LANES,)
-        )
-        chunk = partial_ref[:, :, lanes] + (relaxation * inverse_ref[:, :, lanes]) * extra
-        matrix_ref[:, :, lanes] = chunk
-        if columns_ref is not None:
-            put_columns(chunk.reshape(plane_rows, LANES), c, columns_ref)
-    if columns_ref is None:
-        return None
-    return weight * pick_low(matmul(columns_ref[...], hot_ref[...], (1, 0)), low)
+    values = slot_weight_ref[...] * to_dense(returned, cap)
+    total = same_cell_sum(values, cell_rows_ref[...], cell_columns_ref[...])
+    outgoing = row_partial_ref[...] + (relaxation * row_inverse_ref[...]) * total
+    return from_dense(outgoing, returned.shape[0], cap)
 
 
 def node_hot(code, rows):
@@ -494,9 +572,13 @@
 
 def put_requested(message_ref, values):
     zero = jnp.zeros((1, LANES), F32)
+    order = group_order(values.shape[0])
+    rows = {device: values[i : i + 1] for i, device in enumerate(order)}
     message_ref[:, 1, :] = values
-    message_ref[:, 2, :] = jnp.concatenate([zero, values[:-1]], axis=0)
-    message_ref[:, 3, :] = jnp.concatenate([values[1:], zero], axis=0)
+    for place, step in ((2, -1), (3, 1)):
+        message_ref[:, place, :] = jnp.concatenate(
+            [rows.get(device + step, zero) for device in order], axis=0
+        )
 
 
 def first_step_kernel(
@@ -504,40 +586,33 @@
     cap,
     arrived_ref,
     slot_code_ref,
-    partial_ref,
-    inverse_ref,
-    slot_index_ref,
     slot_weight_ref,
+    row_partial_ref,
+    row_inverse_ref,
+    cell_rows_ref,
+    cell_columns_ref,
     fracture_ref,
     link_sum_ref,
     fracture_source_ref,
     leak_ref,
     link_weights_ref,
-    matrix_ref,
     fracture_next_ref,
     fracture_inverse_ref,
     node_code_ref,
     message_hbm,
-    hot_ref,
-    columns_ref,
     message_ref,
     sem,
 ):
-    devices = arrived_ref.shape[0]
     owned = fracture_ref.shape[0]
-    returned = device_values(arrived_ref, slot_code_ref[...])
-    table_rows = arrived_ref.shape[1] - 4
-    outgoing = couple(
+    message_ref[:, 0, :] = row_values(
         relaxation,
         cap,
-        returned,
-        partial_ref,
-        inverse_ref,
-        hot_ref,
-        slot_index_ref,
+        device_values(arrived_ref, slot_code_ref[...]),
         slot_weight_ref,
-        matrix_ref,
-        columns_ref,
+        row_partial_ref,
+        row_inverse_ref,
+        cell_rows_ref,
+        cell_columns_ref,
     )
     code = arrived_ref[:, 0, :].astype(jnp.int32)
     node_code_ref[...] = code
@@ -547,7 +622,7 @@
         to_dense(arrived_ref[:, 1, :], cap),
         to_dense(arrived_ref[:, 2, :], cap),
     )
-    sums = matmul(node_hot(dense, table_rows), parts, (1, 1))
+    sums = matmul(node_hot(dense, fracture_ref.shape[0] * fracture_ref.shape[1] // LANES), parts, (1, 1))
     diag = (
         leak_ref[...] + jnp.sum(link_weights_ref[...], axis=0) + unstack_lanes(fold(sums, 0), owned)
     )
@@ -557,17 +632,81 @@
         fracture_source_ref[...] + link_sum_ref[...] + unstack_lanes(fold(sums, 1), owned)
     )
     fracture_next_ref[...] = fracture_next
-    message_ref[:, 0, :] = from_dense(outgoing, devices, cap)
     put_requested(message_ref, node_values(stack_lanes(fracture_next), code))
     out = pltpu.make_async_copy(message_ref, message_hbm, sem)
     out.start()
     out.wait()
 
 
+def next_fracture(
+    relaxation,
+    cap,
+    arrived_ref,
+    code,
+    fracture_ref,
+    link_sum_ref,
+    fracture_source_ref,
+    fracture_inverse_ref,
+):
+    owned, blk = fracture_ref.shape
+    dense = to_dense(code, cap)
+    parts = masked_parts(dense & (LANES - 1), to_dense(arrived_ref[:, 0, :], cap))
+    sums = matmul(node_hot(dense, owned * blk // LANES), parts, (1, 1))
+    return (1.0 - relaxation) * fracture_ref[...] + (relaxation * fracture_inverse_ref[...]) * (
+        fracture_source_ref[...] + link_sum_ref[...] + unstack_lanes(fold(sums, 0), owned)
+    )
+
+
 def step_kernel(
     relaxation,
     cap,
-    last,
+    arrived_ref,
+    node_code_ref,
+    slot_weight_ref,
+    row_partial_ref,
+    row_inverse_ref,
+    cell_rows_ref,
+    cell_columns_ref,
+    fracture_ref,
+    link_sum_ref,
+    fracture_source_ref,
+    fracture_inverse_ref,
+    fracture_next_ref,
+    message_hbm,
+    message_ref,
+    sem,
+):
+    message_ref[:, 0, :] = row_values(
+        relaxation,
+        cap,
+        arrived_ref[:, 1, :],
+        slot_weight_ref,
+        row_partial_ref,
+        row_inverse_ref,
+        cell_rows_ref,
+        cell_columns_ref,
+    )
+    code = node_code_ref[...]
+    fracture_next = next_fracture(
+        relaxation,
+        cap,
+        arrived_ref,
+        code,
+        fracture_ref,
+        link_sum_ref,
+        fracture_source_ref,
+        fracture_inverse_ref,
+    )
+    fracture_next_ref[...] = fracture_next
+    put_requested(message_ref, node_values(stack_lanes(fracture_next), code))
+    out = pltpu.make_async_copy(message_ref, message_hbm, sem)
+    out.start()
+    out.wait()
+
+
+def last_step_kernel(
+    relaxation,
+    cap,
     arrived_ref,
     node_code_ref,
     partial_ref,
@@ -580,42 +719,20 @@
     fracture_inverse_ref,
     matrix_ref,
     fracture_next_ref,
-    *refs,
+    hot_ref,
 ):
-    if last:
-        (hot_ref,) = refs
-        columns_ref = None
-    else:
-        message_hbm, hot_ref, columns_ref, message_ref, sem = refs
-    devices = arrived_ref.shape[0]
-    owned, blk = fracture_ref.shape
-    outgoing = couple(
+    values = slot_weight_ref[...] * to_dense(arrived_ref[:, 1, :], cap)
+    add_rows(relaxation, values, partial_ref, inverse_ref, slot_index_ref, hot_ref, matrix_ref)
+    fracture_next_ref[...] = next_fracture(
         relaxation,
         cap,
-        arrived_ref[:, 1, :],
-        partial_ref,
-        inverse_ref,
-        hot_ref,
-        slot_index_ref,
-        slot_weight_ref,
-        matrix_ref,
-        columns_ref,
-    )
-    code = node_code_ref[...]
-    dense = to_dense(code, cap)
-    parts = masked_parts(dense & (LANES - 1), to_dense(arrived_ref[:, 0, :], cap))
-    sums = matmul(node_hot(dense, owned * blk // LANES), parts, (1, 1))
-    fracture_next = (1.0 - relaxation) * fracture_ref[...] + (
-        relaxation * fracture_inverse_ref[...]
-    ) * (fracture_source_ref[...] + link_sum_ref[...] + unstack_lanes(fold(sums, 0), owned))
-    fracture_next_ref[...] = fracture_next
-    if last:
-        return
-    message_ref[:, 0, :] = from_dense(outgoing, devices, cap)
-    put_requested(message_ref, node_values(stack_lanes(fracture_next), code))
-    out = pltpu.make_async_copy(message_ref, message_hbm, sem)
-    out.start()
-    out.wait()
+        arrived_ref,
+        node_code_ref[...],
+        fracture_ref,
+        link_sum_ref,
+        fracture_source_ref,
+        fracture_inverse_ref,
+    )
 
 
 def call(kernel, outs, ins, name, micros, hbm_in=(), hbm_out=(), scratch=(), aliases=None, limit=VMEM_LIMIT):
@@ -662,7 +779,6 @@
     cap = 3 * total_rows // (2 * devices)
     slots = devices * cap
     cells = depth * area_rows * cols // LANES
-    table_rows = owned * blk // LANES
     relax = relax_weights(ITERS)
     grid = (matrix_start.shape, F32)
     fracture = (fracture_start.shape, F32)
@@ -671,13 +787,20 @@
     hot = pltpu.VMEM((cells, slots), BF16)
     columns = pltpu.VMEM((2 * LANES, cells), BF16)
     padded = (devices, LANES)
-    first_message = ((devices, 4 + table_rows, LANES), F32)
-    later_message = ((devices, 4, LANES), F32)
+    first_message = ((devices, 4 + owned * blk // LANES, LANES), F32)
+    message_type = ((devices, 4, LANES), F32)
     forward = [(i, i + 1) for i in range(devices - 1)]
     backward = [(target, source) for source, target in forward]
 
     def exchange(message):
-        return lax.all_to_all(message, "area", split_axis=0, concat_axis=0, tiled=True)
+        return lax.all_to_all(
+            message,
+            "area",
+            split_axis=0,
+            concat_axis=0,
+            tiled=True,
+            axis_index_groups=[group_order(devices)],
+        )
 
     staged = [
         row_counts.reshape(1, 1),
@@ -690,12 +813,17 @@
         matrix_source,
         matrix_storage,
     ]
-    slot_index, slot_weight, slot_code, message, up, down = call(
+    slot_rows = ((slots // LANES, LANES), F32)
+    slot_columns = ((LANES, slots // LANES + -(slots // LANES) % 8), F32)
+    dense = ((1, slots), F32)
+    slot_index, slot_weight, slot_code, cell_rows, cell_columns, message, up, down = call(
         functools.partial(setup_kernel, devices, cap, len(staged)),
         [
             ((2, slots), jnp.int32),
-            ((1, slots), F32),
+            dense,
             (padded, jnp.int32),
+            slot_rows,
+            slot_columns,
             first_message,
             side,
             side,
@@ -704,7 +832,7 @@
         "place_rows",
         5.0,
         hbm_in=range(len(staged)),
-        hbm_out=(3, 4, 5),
+        hbm_out=(5, 6, 7),
         scratch=[pltpu.VMEM(x.shape, x.dtype) for x in staged]
         + [
             pltpu.VMEM(*first_message),
@@ -719,15 +847,23 @@
     arrived = exchange(message)
     low = lax.ppermute(up, "area", forward)
     high = lax.ppermute(down, "area", backward)
-    partial, scaled, inverse, side_partial, side_scaled, side_inverse, link_sum = call(
+    scaled, inverse, row_inverse = call(
+        diagonal_kernel,
+        [grid, grid, dense],
+        [matrix_source, matrix_storage, slot_index, slot_weight],
+        "diagonal",
+        2.0,
+        scratch=[hot, columns],
+    )
+    partial, side_partial, side_scaled, side_inverse, row_partial, link_sum = call(
         functools.partial(first_window_kernel, relax[0]),
-        [grid, grid, grid, sides, sides, sides, fracture],
+        [grid, sides, sides, sides, dense, fracture],
         [
             matrix_start,
             low,
             high,
-            matrix_source,
-            matrix_storage,
+            scaled,
+            inverse,
             slot_index,
             slot_weight,
             fracture_start,
@@ -735,80 +871,82 @@
             link_weights,
         ],
         "stencil_first",
-        4.0,
-        scratch=[hot],
-    )
-    fracture_now = fracture_start
-    matrix, fracture_now, fracture_inverse, node_code, message = call(
+        2.0,
+        scratch=[hot, columns],
+    )
+    message_scratch = [pltpu.VMEM(*message_type), pltpu.SemaphoreType.DMA]
+    fracture_now, fracture_inverse, node_code, message = call(
         functools.partial(first_step_kernel, relax[0], cap),
-        [grid, fracture, fracture, (padded, jnp.int32), later_message],
+        [fracture, fracture, (padded, jnp.int32), message_type],
         [
             arrived,
             slot_code,
-            partial,
-            inverse,
-            slot_index,
             slot_weight,
-            fracture_now,
+            row_partial,
+            row_inverse,
+            cell_rows,
+            cell_columns,
+            fracture_start,
             link_sum,
             fracture_source,
             fracture_leak,
             link_weights,
         ],
         "couple_first",
-        4.0,
-        hbm_out=(4,),
-        scratch=[hot, columns, pltpu.VMEM(*later_message), pltpu.SemaphoreType.DMA],
+        2.0,
+        hbm_out=(3,),
+        scratch=message_scratch,
     )
     for index in range(1, ITERS):
         last = index == ITERS - 1
         old, arrived = arrived, exchange(message)
-        partial, side_partial, link_sum = call(
-            functools.partial(window_kernel, relax[index], relax[index - 1], cap, index == 1),
-            [grid, sides, fracture],
+        outs = call(
+            functools.partial(window_kernel, relax[index], relax[index - 1], cap, index == 1, last),
+            [grid, sides, fracture] + ([] if last else [dense]),
             [
                 old,
                 low,
                 high,
-                matrix,
+                partial,
                 scaled,
                 inverse,
                 side_partial,
                 side_scaled,
                 side_inverse,
+                slot_index,
+                slot_weight,
+                slot_code,
                 fracture_now,
                 fracture_links,
                 link_weights,
             ],
             "stencil",
             3.0,
-            aliases={6: 1},
-        )
-        outs = call(
-            functools.partial(step_kernel, relax[index], cap, last),
-            [grid, fracture] + ([] if last else [later_message]),
-            [
-                arrived,
-                node_code,
-                partial,
-                inverse,
-                slot_index,
-                slot_weight,
-                fracture_now,
-                link_sum,
-                fracture_source,
-                fracture_inverse,
-            ],
+            aliases={3: 0, 6: 1},
+            scratch=[pltpu.VMEM(*grid), hot] + ([] if last else [columns]),
+        )
+        partial, side_partial, link_sum = outs[:3]
+        fractures = [fracture_now, link_sum, fracture_source, fracture_inverse]
+        if last:
+            return call(
+                functools.partial(last_step_kernel, relax[index], cap),
+                [grid, fracture],
+                [arrived, node_code, partial, inverse, slot_index, slot_weight] + fractures,
+                "couple_last",
+                2.0,
+                scratch=[hot],
+            )
+        row_partial = outs[3]
+        fracture_now, message = call(
+            functools.partial(step_kernel, relax[index], cap),
+            [fracture, message_type],
+            [arrived, node_code, slot_weight, row_partial, row_inverse, cell_rows, cell_columns]
+            + fractures,
             "couple",
-            3.0,
-            hbm_out=() if last else (2,),
-            scratch=[hot]
-            + ([] if last else [columns, pltpu.VMEM(*later_message), pltpu.SemaphoreType.DMA]),
-        )
-        matrix, fracture_now = outs[:2]
-        if not last:
-            message = outs[2]
-    return (matrix, fracture_now)
+            2.0,
+            hbm_out=(1,),
+            scratch=message_scratch,
+        )
 
 
 def solution(mesh):

time: 79.2 us -> 63.8 us (0.81)
  waiting for transfers between devices: 16.5 us -> 1.34 us
  local copies, waits for them, and re-layouts: 9.42 us -> 1.73 us
  starting transfers between devices: 23.7 us -> 28.7 us
  Pallas kernels: 27.1 us -> 29.9 us
    all_to_all x4, waiting for transfers between devices: 16.5 us -> 1.33 us  [exchange(): lax.all_to_all(message, 'area', split_axis=0, concat_axis=0, tiled=True,...]
    unnamed x38 -> x26, local copies, waits for them, and re-layouts: 9.42 us -> 1.73 us
    all_to_all x4, starting transfers between devices: 20.1 us -> 25 us  [exchange(): lax.all_to_all(message, 'area', split_axis=0, concat_axis=0, tiled=True,...]
    pallas_call x9 -> x10, Pallas kernels: 27.1 us -> 29.9 us  [call(): pl.pallas_call(kernel, out_shape=[jax.ShapeDtypeStruct(shape, dtype) for...]
  transfers between devices with their start and end apart: 6 -> 6, of which waited for: 4 -> 1; matrix products, arithmetic and copies ran while one was open for 0% -> 0% of each run, Pallas kernels for 8% -> 25%
where the time goes in v2:
time: 63.8 us; the launch traced here: 63.2 us
  Pallas kernels  29.9 us (47%)
  starting transfers between devices  28.7 us (45%)
  local copies, waits for them, and re-layouts  1.73 us (3%)
  between operations  1.56 us (2%)
  waiting for transfers between devices  1.34 us (2%)
    pallas_call x10, Pallas kernels, call(): pl.pallas_call(kernel, out_shape=[jax.ShapeDtypeStruct(shape, dtype) for...  29.9 us
    all_to_all x4, starting transfers between devices, exchange(): lax.all_to_all(message, 'area', split_axis=0, concat_axis=0, tiled=True,...  25 us
    ppermute x1, starting transfers between devices, local(): low = lax.ppermute(up, 'area', forward)  2.38 us
    unnamed x26, local copies, waits for them, and re-layouts  1.73 us
    all_to_all x4, waiting for transfers between devices, exchange(): lax.all_to_all(message, 'area', split_axis=0, concat_axis=0, tiled=True,...  1.33 us
    ppermute x1, starting transfers between devices, local(): high = lax.ppermute(down, 'area', backward)  1.29 us
  transfers between devices with their start and end apart: 6, of which 1 were waited for; matrix products, arithmetic and copies ran while one was open for 0% of the time, Pallas kernels for 25%

profile of v2, /device:TPU:0, one launch (start us, length us, event | category | flops | bytes accessed | tf_op | source)
XLA Modules:
  0.0 63.2 jit_solution(6898806316699552202)
XLA Ops:
  1.3 5.0 %place_rows.1 = (s32[2,1536]{1,0:T(2,128)}, f32[1,1536]{1,0:T(1,128)}, s32[16,128]{1,0:T(8,128)}, f32[12,128]{1,0:T(8,128)}, f32[128,16]{1,0:T(8,128)}, /*index=...) custom-call(s32[1,1]{1,0:T(1,128)} %bitcast.5.refs_0_, s32[1,128]{1,0:T(1,128)} %bitcast.9, ...), custom_call_target="tpu_custom_call" | custom-call | bytes 15000000 | tf_op jit(solution)/shard_map/place_rows/pallas_call | solution.py:739
  6.3 2.4 %collective-permute-start = (f32[11,8,1024]{2,1,0:T(8,128)}, f32[11,8,1024]{2,1,0:T(8,128)S(1)}, u32[]{:S(2)}, u32[]{:S(2)}) collective-permute-start(f32[11,8,1024]{2,1,0:T(8,128)} %get-tuple-element.40), channel_id=1, source_target_pairs={{0,1},{1,2},{2,3},{3,4},{4,5},{5,6},{6,7},{7,8},{8,9},{9,10},{10,1... | collective-permute-start | bytes 1081352 | tf_op jit(solution)/shard_map/ppermute | solution.py:848
  8.7 1.3 %collective-permute-start.1 = (f32[11,8,1024]{2,1,0:T(8,128)}, f32[11,8,1024]{2,1,0:T(8,128)S(1)}, u32[]{:S(2)}, u32[]{:S(2)}) collective-permute-start(f32[11,8,1024]{2,1,0:T(8,128)} %get-tuple-element.41), channel_id=1, source_target_pairs={{1,0},{2,1},{3,2},{4,3},{5,4},{6,5},{7,6},{8,7},{9,8},{10,9},{11,1... | collective-permute-start | bytes 1081352 | tf_op jit(solution)/shard_map/ppermute | solution.py:849
  10.0 0.0 copy-start.6
  10.0 0.0 copy-start.7
  10.0 10.5 %all-to-all-start = ((f32[16,20,128]{2,1,0:T(8,128)}), f32[16,20,128]{2,1,0:T(8,128)S(1)}, u32[]{:S(2)}, u32[]{:S(2)}) async-start(f32[16,20,128]{2,1,0:T(8,128)} %get-tuple-element.37), calls=%async_computation | async-start | bytes 393216 | tf_op jit(solution)/shard_map/all_to_all | solution.py:796
  20.5 0.0 copy-start.1
  20.5 1.0 %copy-done.1 = f32[8,16,1024]{2,1,0:T(8,128)S(1)} copy-done((f32[8,16,1024]{2,1,0:T(8,128)S(1)}, f32[8,16,1024]{2,1,0:T(8,128)}, u32[]{:S(2)}) %copy-start.1) | copy-done | bytes 524312
  21.6 3.5 %diagonal.1 = (f32[8,16,1024]{2,1,0:T(8,128)S(1)}, f32[8,16,1024]{2,1,0:T(8,128)S(1)}, f32[1,1536]{1,0:T(1,128)S(1)}) custom-call(f32[8,16,1024]{2,1,0:T(8,128)S(1)} %copy-done, f32[8,16,1024]{2,1,0:T(8,128)S(1)} %copy-done.1, s32[2,1536]{1,0:T(2,128)S(1)} %copy-done.7, f32[1,1536]{1,0:T(1,128)S(1)} %copy-done.6), custom_call_target="tpu_custom_call" | custom-call | bytes 6000000 | tf_op jit(solution)/shard_map/diagonal/pallas_call | solution.py:739
  25.0 0.0 collective-permute-done.low_ref
  25.1 0.0 collective-permute-done.1.high_ref
  25.1 0.0 copy-start.9
  25.1 0.0 copy-start.12
  25.2 2.2 %stencil_first.1 = (f32[8,16,1024]{2,1,0:T(8,128)S(1)}, f32[2,3,8,1024]{3,2,1,0:T(8,128)S(1)}, f32[2,3,8,1024]{3,2,1,0:T(8,128)S(1)}, f32[2,3,8,1024]{3,2,1,0:T(...) custom-call(f32[8,16,1024]{2,1,0:T(8,128)S(1)} %copy-done.2, f32[11,8,1024]{2,1,0:T(8,128)S(1)} %collective-permute-done.low_ref, ...), custom_call_target="tpu_custom_call" | custom-call | bytes 6000000 | tf_op jit(solution)/shard_map/stencil_first/pallas_call | solution.py:739
  27.3 0.0 copy-start.8
  27.4 0.0 all-to-all-done.arrived_ref
  27.4 0.0 copy-done.4
  27.4 0.0 copy-done.9
  27.4 0.6 %copy-done.8 = s32[16,128]{1,0:T(8,128)S(1)} copy-done((s32[16,128]{1,0:T(8,128)S(1)}, s32[16,128]{1,0:T(8,128)}, u32[]{:S(2)}) %copy-start.8) | copy-done | bytes 8216
  28.0 2.5 %couple_first.1 = (f32[8,256]{1,0:T(8,128)S(1)}, f32[8,256]{1,0:T(8,128)S(1)}, s32[16,128]{1,0:T(8,128)S(1)}, f32[16,4,128]{2,1,0:T(4,128)}) custom-call(f32[16,20,128]{2,1,0:T(8,128)S(1)} %all-to-all-done.arrived_ref, s32[16,128]{1,0:T(8,128)S(1)} %copy-done.8, f32[1,1536]{1,0:T(1,128)S(1)} %copy-done.6, f32[1,1536]{1,0:T(1,128)S(1)} %get-tuple-element.45.row_partial_ref, ...), custom_call_target="tpu_custom_call" | custom-call | bytes 6000000 | tf_op jit(solution)/shard_map/couple_first/pallas_call | solution.py:739
  30.6 4.8 %all-to-all-start.1 = ((f32[16,4,128]{2,1,0:T(4,128)}), f32[16,4,128]{2,1,0:T(4,128)S(1)}, u32[]{:S(2)}, u32[]{:S(2)}) async-start(f32[16,4,128]{2,1,0:T(4,128)} %get-tuple-element.50), calls=%async_computation.1 | async-start | bytes 65536 | tf_op jit(solution)/shard_map/all_to_all | solution.py:796
  35.4 4.1 %stencil.3 = (f32[8,16,1024]{2,1,0:T(8,128)S(1)}, f32[2,3,8,1024]{3,2,1,0:T(8,128)S(1)}, f32[8,256]{1,0:T(8,128)S(1)}, f32[1,1536]{1,0:T(1,128)S(1)}) custom-call(f32[16,20,128]{2,1,0:T(8,128)S(1)} %all-to-all-done.arrived_ref, f32[11,8,1024]{2,1,0:T(8,128)S(1)} %collective-permute-done.low_ref, ...), custom_call_target="tpu_custom_call", output_to_operand_aliasing={{0}: (3, {}), {1}: (6, {})} | custom-call | bytes 9000000 | tf_op jit(solution)/shard_map/stencil/pallas_call | solution.py:739
  39.5 0.0 all-to-all-done.1.arrived_ref
  39.5 2.3 %couple.2 = (f32[8,256]{1,0:T(8,128)S(1)}, f32[16,4,128]{2,1,0:T(4,128)}) custom-call(f32[16,4,128]{2,1,0:T(4,128)S(1)} %all-to-all-done.1.arrived_ref, s32[16,128]{1,0:T(8,128)S(1)} %get-tuple-element.51.node_code_ref, f32[1,1536]{1,0:T(1,128)S(1)} %copy-done.6, f32[1,1536]{1,0:T(1,128)S(1)} %get-tuple-element.57.row_partial_ref, ...), custom_call_target="tpu_custom_call" | custom-call | bytes 6000000 | tf_op jit(solution)/shard_map/couple/pallas_call | solution.py:739
  41.8 4.8 %all-to-all-start.2 = ((f32[16,4,128]{2,1,0:T(4,128)}), f32[16,4,128]{2,1,0:T(4,128)S(1)}, u32[]{:S(2)}, u32[]{:S(2)}) async-start(f32[16,4,128]{2,1,0:T(4,128)} %get-tuple-element.60), calls=%async_computation.2 | async-start | bytes 65536 | tf_op jit(solution)/shard_map/all_to_all | solution.py:796
  46.7 3.9 %stencil.4 = (f32[8,16,1024]{2,1,0:T(8,128)S(1)}, f32[2,3,8,1024]{3,2,1,0:T(8,128)S(1)}, f32[8,256]{1,0:T(8,128)S(1)}, f32[1,1536]{1,0:T(1,128)S(1)}) custom-call(f32[16,4,128]{2,1,0:T(4,128)S(1)} %all-to-all-done.1.arrived_ref, f32[11,8,1024]{2,1,0:T(8,128)S(1)} %collective-permute-done.low_ref, ...), custom_call_target="tpu_custom_call", output_to_operand_aliasing={{0}: (3, {}), {1}: (6, {})} | custom-call | bytes 9000000 | tf_op jit(solution)/shard_map/stencil/pallas_call | solution.py:739
  50.6 0.0 all-to-all-done.2.arrived_ref
  50.6 2.3 %couple.3 = (f32[8,256]{1,0:T(8,128)S(1)}, f32[16,4,128]{2,1,0:T(4,128)}) custom-call(f32[16,4,128]{2,1,0:T(4,128)S(1)} %all-to-all-done.2.arrived_ref, s32[16,128]{1,0:T(8,128)S(1)} %get-tuple-element.51.node_code_ref, f32[1,1536]{1,0:T(1,128)S(1)} %copy-done.6, f32[1,1536]{1,0:T(1,128)S(1)} %get-tuple-element.64.row_partial_ref, ...), custom_call_target="tpu_custom_call" | custom-call | bytes 6000000 | tf_op jit(solution)/shard_map/couple/pallas_call | solution.py:739
  52.9 4.8 %all-to-all-start.3 = ((f32[16,4,128]{2,1,0:T(4,128)}), f32[16,4,128]{2,1,0:T(4,128)S(1)}, u32[]{:S(2)}, u32[]{:S(2)}) async-start(f32[16,4,128]{2,1,0:T(4,128)} %get-tuple-element.66), calls=%async_computation.3 | async-start | bytes 65536 | tf_op jit(solution)/shard_map/all_to_all | solution.py:796
  57.8 2.0 %stencil.5 = (f32[8,16,1024]{2,1,0:T(8,128)S(1)}, f32[2,3,8,1024]{3,2,1,0:T(8,128)S(1)}, f32[8,256]{1,0:T(8,128)S(1)}) custom-call(f32[16,4,128]{2,1,0:T(4,128)S(1)} %all-to-all-done.2.arrived_ref, f32[11,8,1024]{2,1,0:T(8,128)S(1)} %collective-permute-done.low_ref, ...), custom_call_target="tpu_custom_call", output_to_operand_aliasing={{0}: (3, {}), {1}: (6, {})} | custom-call | bytes 9000000 | tf_op jit(solution)/shard_map/stencil/pallas_call | solution.py:739
  59.8 1.3 %all-to-all-done.3.arrived_ref = f32[16,4,128]{2,1,0:T(4,128)S(1)} async-done(((f32[16,4,128]{2,1,0:T(4,128)}), f32[16,4,128]{2,1,0:T(4,128)S(1)}, u32[]{:S(2)}, u32[]{:S(2)}) %all-to-all-start.3) | async-done | bytes 32800 | tf_op jit(solution)/shard_map/all_to_all | solution.py:796
  61.1 2.1 %couple_last.1 = (f32[8,16,1024]{2,1,0:T(8,128)}, f32[8,256]{1,0:T(8,128)}) custom-call(f32[16,4,128]{2,1,0:T(4,128)S(1)} %all-to-all-done.3.arrived_ref, s32[16,128]{1,0:T(8,128)S(1)} %get-tuple-element.51.node_code_ref, f32[8,16,1024]{2,1,0:T(8,128)S(1)} %get-tuple-element.70.partial_ref, f32[8,16,1024]{2,1,0:T(8,128)S(1)} %get-tuple-element.44.inverse_ref, ...), custom_call_target="tpu_custom_call" | custom-call | bytes 6000000 | tf_op jit(solution)/shard_map/couple_last/pallas_call | solution.py:739
  (16 shorter events, 0.0 us)
Async XLA Ops:
  1.3 19.2 %copy-start = (f32[8,16,1024]{2,1,0:T(8,128)S(1)}, f32[8,16,1024]{2,1,0:T(8,128)}, u32[]{:S(2)}) copy-start(f32[8,16,1024]{2,1,0:T(8,128)} %source_ref.1) | copy-start | bytes 1572868
  6.3 18.7 %collective-permute-start = (f32[11,8,1024]{2,1,0:T(8,128)}, f32[11,8,1024]{2,1,0:T(8,128)S(1)}, u32[]{:S(2)}, u32[]{:S(2)}) collective-permute-start(f32[11,8,1024]{2,1,0:T(8,128)} %get-tuple-element.40), channel_id=1, source_target_pairs={{0,1},{1,2},{2,3},{3,4},{4,5},{5,6},{6,7},{7,8},{8,9},{9,10},{10,1... | collective-permute-start | bytes 1081352 | tf_op jit(solution)/shard_map/ppermute | solution.py:848
  8.7 16.3 %collective-permute-start.1 = (f32[11,8,1024]{2,1,0:T(8,128)}, f32[11,8,1024]{2,1,0:T(8,128)S(1)}, u32[]{:S(2)}, u32[]{:S(2)}) collective-permute-start(f32[11,8,1024]{2,1,0:T(8,128)} %get-tuple-element.41), channel_id=1, source_target_pairs={{1,0},{2,1},{3,2},{4,3},{5,4},{6,5},{7,6},{8,7},{9,8},{10,9},{11,1... | collective-permute-start | bytes 1081352 | tf_op jit(solution)/shard_map/ppermute | solution.py:849
  10.0 10.5 %copy-start.6 = (f32[1,1536]{1,0:T(1,128)S(1)}, f32[1,1536]{1,0:T(1,128)}, u32[]{:S(2)}) copy-start(f32[1,1536]{1,0:T(1,128)} %get-tuple-element.39.slot_weight_ref) | copy-start | bytes 18436
  10.0 10.5 %copy-start.7 = (s32[2,1536]{1,0:T(2,128)S(1)}, s32[2,1536]{1,0:T(2,128)}, u32[]{:S(2)}) copy-start(s32[2,1536]{1,0:T(2,128)} %get-tuple-element.42.slot_index_ref) | copy-start | bytes 36868
  10.0 17.3 %all-to-all-start = ((f32[16,20,128]{2,1,0:T(8,128)}), f32[16,20,128]{2,1,0:T(8,128)S(1)}, u32[]{:S(2)}, u32[]{:S(2)}) async-start(f32[16,20,128]{2,1,0:T(8,128)} %get-tuple-element.37), calls=%async_computation | async-start | bytes 393216 | tf_op jit(solution)/shard_map/all_to_all | solution.py:796
  20.5 1.0 %copy-start.1 = (f32[8,16,1024]{2,1,0:T(8,128)S(1)}, f32[8,16,1024]{2,1,0:T(8,128)}, u32[]{:S(2)}) copy-start(f32[8,16,1024]{2,1,0:T(8,128)} %storage_ref.1) | copy-start | bytes 1572868
  21.6 3.5 %copy-start.2 = (f32[8,16,1024]{2,1,0:T(8,128)S(1)}, f32[8,16,1024]{2,1,0:T(8,128)}, u32[]{:S(2)}) copy-start(f32[8,16,1024]{2,1,0:T(8,128)} %matrix_ref.1) | copy-start | bytes 1572868
  21.6 3.5 %copy-start.3 = (f32[4,8,256]{2,1,0:T(8,128)S(1)}, f32[4,8,256]{2,1,0:T(8,128)}, u32[]{:S(2)}) copy-start(f32[4,8,256]{2,1,0:T(8,128)} %link_weights_ref.9) | copy-start | bytes 98308
  21.6 3.5 %copy-start.5 = (s32[4,8,256]{2,1,0:T(8,128)S(1)}, s32[4,8,256]{2,1,0:T(8,128)}, u32[]{:S(2)}) copy-start(s32[4,8,256]{2,1,0:T(8,128)} %links_ref.7) | copy-start | bytes 98308
  21.6 3.5 %copy-start.10 = (f32[8,256]{1,0:T(8,128)S(1)}, f32[8,256]{1,0:T(8,128)}, u32[]{:S(2)}) copy-start(f32[8,256]{1,0:T(8,128)} %fracture_ref.3) | copy-start | bytes 24580
  25.1 2.3 %copy-start.4 = (f32[128,16]{1,0:T(8,128)S(1)}, f32[128,16]{1,0:T(8,128)}, u32[]{:S(2)}) copy-start(f32[128,16]{1,0:T(8,128)} %get-tuple-element.48.cell_columns_ref) | copy-start | bytes 24580
  25.1 2.3 %copy-start.9 = (f32[8,256]{1,0:T(8,128)S(1)}, f32[8,256]{1,0:T(8,128)}, u32[]{:S(2)}) copy-start(f32[8,256]{1,0:T(8,128)} %fracture_source_ref.7) | copy-start | bytes 24580
  25.1 2.3 %copy-start.11 = (f32[12,128]{1,0:T(8,128)S(1)}, f32[12,128]{1,0:T(8,128)}, u32[]{:S(2)}) copy-start(f32[12,128]{1,0:T(8,128)} %get-tuple-element.47.cell_rows_ref) | copy-start | bytes 18436
  25.1 2.3 %copy-start.12 = (f32[8,256]{1,0:T(8,128)S(1)}, f32[8,256]{1,0:T(8,128)}, u32[]{:S(2)}) copy-start(f32[8,256]{1,0:T(8,128)} %leak_ref.1) | copy-start | bytes 24580
  27.3 0.7 %copy-start.8 = (s32[16,128]{1,0:T(8,128)S(1)}, s32[16,128]{1,0:T(8,128)}, u32[]{:S(2)}) copy-start(s32[16,128]{1,0:T(8,128)} %get-tuple-element.38.slot_code_ref) | copy-start | bytes 24580
  30.6 8.9 %all-to-all-start.1 = ((f32[16,4,128]{2,1,0:T(4,128)}), f32[16,4,128]{2,1,0:T(4,128)S(1)}, u32[]{:S(2)}, u32[]{:S(2)}) async-start(f32[16,4,128]{2,1,0:T(4,128)} %get-tuple-element.50), calls=%async_computation.1 | async-start | bytes 65536 | tf_op jit(solution)/shard_map/all_to_all | solution.py:796
  41.8 8.7 %all-to-all-start.2 = ((f32[16,4,128]{2,1,0:T(4,128)}), f32[16,4,128]{2,1,0:T(4,128)S(1)}, u32[]{:S(2)}, u32[]{:S(2)}) async-start(f32[16,4,128]{2,1,0:T(4,128)} %get-tuple-element.60), calls=%async_computation.2 | async-start | bytes 65536 | tf_op jit(solution)/shard_map/all_to_all | solution.py:796
  52.9 8.2 %all-to-all-start.3 = ((f32[16,4,128]{2,1,0:T(4,128)}), f32[16,4,128]{2,1,0:T(4,128)S(1)}, u32[]{:S(2)}, u32[]{:S(2)}) async-start(f32[16,4,128]{2,1,0:T(4,128)} %get-tuple-element.66), calls=%async_computation.3 | async-start | bytes 65536 | tf_op jit(solution)/shard_map/all_to_all | solution.py:796

commit v3 on v2

--- a/solution.py
+++ b/solution.py
@@ -10,6 +10,7 @@
 
 ITERS = 4
 HALO = ITERS - 1
+GRID_SLOTS = 72
 LANES = 128
 F32 = jnp.float32
 BF16 = jnp.bfloat16
@@ -99,20 +100,31 @@
     columns_ref[LANES:, index * LANES : (index + 1) * LANES] = low
 
 
-def fill_hot(hot_ref, slot_high):
+def fill_hot(hot_ref, high):
     for start in range(0, hot_ref.shape[0], LANES):
-        rows = iota((LANES, slot_high.shape[1]), 0) + start
-        hot_ref[start : start + LANES, :] = (rows == slot_high).astype(F32).astype(BF16)
+        rows = iota((LANES, high.shape[1]), 0) + start
+        hot_ref[start : start + LANES, :] = (rows == high).astype(F32).astype(BF16)
+
+
+def pick_entries(table, row, lane):
+    found = jnp.zeros(row.shape, table.dtype)
+    for i in range(table.shape[0]):
+        values = jnp.broadcast_to(table[i : i + 1], row.shape)
+        found = jnp.where(row == i, lane_gather(values, lane), found)
+    return found
 
 
 def setup_kernel(devices, cap, staged, *refs):
     sources, refs = refs[:staged], refs[staged:]
-    slot_index_ref, slot_weight_ref, slot_code_ref, cell_rows_ref, cell_columns_ref = refs[:5]
-    message_hbm, up_hbm, down_hbm = refs[5:8]
-    targets, refs = refs[8 : 8 + staged], refs[8 + staged :]
-    message_ref, up_ref, down_ref, hot_ref, columns_ref, sems = refs
+    rows_ref, slots_ref, message_hbm, pair_hbm, cross_hbm, grids_hbm = refs[:6]
+    targets, refs = refs[6 : 6 + staged], refs[6 + staged :]
+    message_ref, pair_ref, cross_ref, hot_ref, columns_ref, sems = refs
     copies = [
         pltpu.make_async_copy(sources[i], targets[i], sems.at[i]) for i in range(staged)
+    ]
+    kept = [
+        pltpu.make_async_copy(targets[i], grids_hbm.at[j], sems.at[staged + 3 + j])
+        for j, i in enumerate((5, 7, 8))
     ]
     for copy in copies:
         copy.start()
@@ -123,9 +135,7 @@
     owned, blk = fracture_ref.shape
     depth, area_rows, cols = matrix_ref.shape
     groups = cells_ref.shape[0]
-    slots = devices * cap
-    plane_rows = matrix_ref.shape[0] * matrix_ref.shape[1]
-    col_groups = cols // LANES
+    plane_rows = depth * area_rows
     shape = (groups, LANES)
     nodes, cells = nodes_ref[...], cells_ref[...]
     live = iota(shape, 0) * LANES + iota(shape, 1) < counts_ref[...]
@@ -138,108 +148,106 @@
         slot = jnp.where(block >> log2(LANES) == part, found, slot)
     device = slot >> log2(owned)
     target = jnp.zeros(shape, jnp.int32)
-    for position, member in enumerate(group_order(devices)):
-        target = jnp.where(device == member, position, target)
+    for position, place in enumerate(group_order(devices)):
+        target = jnp.where(device == place, position, target)
     target = jnp.where(live, target, -1)
     node_high = ((nodes & (blk - 1)) >> log2(LANES)) * owned + (slot & (owned - 1))
     node_low = nodes & (LANES - 1)
-    cell_plane = cells >> log2(cols)
+    plane_row = cells >> log2(cols)
     cell_group = (cells & (cols - 1)) >> log2(LANES)
+    cell_high = cell_group * plane_rows + plane_row
     cell_low = cells & (LANES - 1)
+    high, low = unstack_lanes(cell_high, 1), unstack_lanes(cell_low, 1)
+    row_weight = unstack_lanes(weight, 1)
+    fill_hot(hot_ref, high)
 
     device_rows = iota((devices, LANES), 0)
     member = [(device_rows == target[q : q + 1]).astype(F32) for q in range(groups)]
-    earlier = (iota((LANES, LANES), 0) < iota((LANES, LANES), 1)).astype(BF16)
+    earlier = (iota((LANES, LANES), 0) < iota((LANES, LANES), 1)).astype(F32).astype(BF16)
     counted = matmul(jnp.concatenate(member, axis=0).astype(BF16), earlier, (1, 0))
     before = jnp.zeros((devices, 1), F32)
-    placed = []
+    rank = []
     for q in range(groups):
-        rank = jnp.sum(
-            member[q] * (counted[q * devices : (q + 1) * devices] + before), axis=0, keepdims=True
-        ).astype(jnp.int32)
+        inside = counted[q * devices : (q + 1) * devices] + before
+        rank.append(jnp.sum(member[q] * inside, axis=0, keepdims=True).astype(jnp.int32))
         before = before + jnp.sum(member[q], axis=1, keepdims=True)
-        where = target[q : q + 1]
-        placed.append(jnp.where(where >= 0, where * cap + rank, -1))
-    placed = jnp.concatenate(placed, axis=1)
-
-    high = weight.astype(BF16).astype(F32)
-    middle = (weight - high).astype(BF16).astype(F32)
-    low = weight - high - middle
+    rank_row = jnp.concatenate(rank, axis=1)
+    rank = jnp.concatenate(rank, axis=0)
+    member = jnp.concatenate(member, axis=1)
+
+    first = weight.astype(BF16).astype(F32)
+    second = (weight - first).astype(BF16).astype(F32)
     features = [
-        jnp.where(live, 1.0, 0.0),
+        jnp.ones(shape, F32),
         node_high.astype(F32),
         node_low.astype(F32),
-        cell_plane.astype(F32),
-        cell_group.astype(F32),
-        cell_low.astype(F32),
-        high,
-        middle,
-        low,
+        first,
+        second,
+        weight - first - second,
+        iota(shape, 0).astype(F32),
+        iota(shape, 1).astype(F32),
     ]
-    features = [jnp.concatenate([x[q : q + 1] for q in range(groups)], axis=1) for x in features]
-    features = jnp.concatenate(
-        features + [jnp.zeros((16 - len(features), groups * LANES), F32)], axis=0
-    ).astype(BF16)
-    placing = (iota((slots, groups * LANES), 0) == placed).astype(F32).astype(BF16)
-    packed = matmul(features, placing, (1, 1))
-    used = packed[0:1] > 0.5
-    code = packed[1:2] * LANES + packed[2:3]
-    code = jnp.where(used, code, -1.0)
-    slot_high = jnp.where(used, packed[4:5] * plane_rows + packed[3:4], -1.0).astype(jnp.int32)
-    slot_low = packed[5:6].astype(jnp.int32)
-    slot_weight = packed[6:7] + packed[7:8] + packed[8:9]
-    fill_hot(hot_ref, slot_high)
-    slot_index_ref[0:1] = slot_high
-    slot_index_ref[1:2] = slot_low
-    slot_weight_ref[...] = slot_weight
-    padded_code = from_dense(code, devices, cap)
-    slot_code_ref[...] = padded_code.astype(jnp.int32)
-    message_ref[:, 0, :] = jnp.where(iota((devices, LANES), 1) < cap, padded_code, -1.0)
-    message_ref[:, 1, :] = from_dense(slot_weight, devices, cap)
+    features = [member * unstack_lanes(x, 1) for x in features]
+    ranked = (iota((LANES, groups * LANES), 0) == rank_row).astype(F32).astype(BF16)
+    packed = matmul(jnp.concatenate(features, axis=0).astype(BF16), ranked, (1, 1))
+    packed = [packed[i * devices : (i + 1) * devices] for i in range(len(features))]
+    code = jnp.where(packed[0] > 0.5, packed[1] * LANES + packed[2], -1.0)
+    slot_row, slot_lane = packed[6].astype(jnp.int32), packed[7].astype(jnp.int32)
+    slots_ref[0], slots_ref[1], slots_ref[2] = packed[6], packed[7], code
+    for i, x in enumerate((weight, target, rank, cells, cell_high, cell_low)):
+        rows_ref[i] = x.astype(F32)
+    message_ref[:, 0, :] = code
+    message_ref[:, 1, :] = packed[3] + packed[4] + packed[5]
     message_ref[:, 3, :] = jnp.zeros((devices, LANES), F32)
 
-    cell = jnp.where(used, (slot_high * LANES + slot_low).astype(F32), -1.0)
-    rows = stack_lanes(cell)
-    cell_rows_ref[...] = rows
-    cell_columns_ref[...] = turned(rows)
-
-    row = slot_high & (area_rows - 1)
-    plane = (slot_high >> log2(area_rows)) & (depth - 1)
-    group = slot_high >> log2(plane_rows)
-    half = slots // 2
-    for far, side_ref in ((area_rows - 1 - row, up_ref), (row, down_ref)):
-        place = (group * HALO + far) * depth + plane
-        place = jnp.where(used & (far < HALO), place, -1).astype(F32)
-        for i, x in enumerate((place, packed[5:6], slot_weight, code)):
-            side_ref[3 * HALO + 1, 2 * i : 2 * i + 1, :half] = x[:, :half]
-            side_ref[3 * HALO + 1, 2 * i + 1 : 2 * i + 2, :half] = x[:, half:]
+    odd = (lax.axis_index("area") & 1) == 1
+    plane = plane_row >> log2(area_rows)
+    row = plane_row & (area_rows - 1)
+    places = []
+    for far in (area_rows - 1 - row, row):
+        place = (cell_group * HALO + far) * depth + plane
+        places.append(jnp.where(live & (far < HALO), place, -1).astype(F32))
+    info = [low, row_weight, unstack_lanes(target, 1), unstack_lanes(rank, 1)]
+    info = [x.astype(F32) for x in info]
+    dense = to_dense(code, cap)
+    half = dense.shape[1] // 2
+    for ref, place in (
+        (pair_ref, jnp.where(odd, places[1], places[0])),
+        (cross_ref, jnp.where(odd, places[0], places[1])),
+    ):
+        tile = ref.at[3 * HALO + 1]
+        for i, x in enumerate([unstack_lanes(place, 1)] + info):
+            tile[i : i + 1, :] = x
+        tile[5:6, :half] = dense[:, :half]
+        tile[6:7, :half] = dense[:, half:]
 
     for copy in copies[5:]:
         copy.wait()
-    nodes_table = stack_lanes(fracture_ref[...])
-    message_ref[:, 4:, :] = jnp.broadcast_to(nodes_table[None], (devices,) + nodes_table.shape)
+    for copy in kept:
+        copy.start()
+    node_table = stack_lanes(fracture_ref[...])
+    message_ref[:, 4:, :] = jnp.broadcast_to(node_table[None], (devices,) + node_table.shape)
     for ref, start, count in (
         (matrix_ref, 0, HALO + 1),
         (source_ref, HALO + 1, HALO),
         (storage_ref, 2 * HALO + 1, HALO),
     ):
         for far in range(count):
-            up_ref[start + far] = ref[:, area_rows - 1 - far, :]
-            down_ref[start + far] = ref[:, far, :]
+            up = ref[:, area_rows - 1 - far, :]
+            down = ref[:, far, :]
+            pair_ref[start + far] = jnp.where(odd, down, up)
+            cross_ref[start + far] = jnp.where(odd, up, down)
     outs = [
-        pltpu.make_async_copy(up_ref, up_hbm, sems.at[staged]),
-        pltpu.make_async_copy(down_ref, down_hbm, sems.at[staged + 1]),
+        pltpu.make_async_copy(pair_ref, pair_hbm, sems.at[staged]),
+        pltpu.make_async_copy(cross_ref, cross_hbm, sems.at[staged + 1]),
         pltpu.make_async_copy(message_ref, message_hbm, sems.at[staged + 2]),
     ]
     outs[0].start()
     outs[1].start()
-    for c in range(col_groups):
-        chunk = matrix_ref[:, :, c * LANES : (c + 1) * LANES].reshape(plane_rows, LANES)
-        put_columns(chunk, c, columns_ref)
-    picked = pick_low(matmul(columns_ref[...], hot_ref[...], (1, 0)), slot_low)
-    message_ref[:, 2, :] = from_dense(slot_weight * picked, devices, cap)
+    picked = stack_lanes(pick_cells(matrix_ref, columns_ref, hot_ref, low))
+    message_ref[:, 2, :] = pick_entries(weight * picked, slot_row, slot_lane)
     outs[2].start()
-    for out in outs:
+    for out in outs + kept:
         out.wait()
 
 
@@ -252,7 +260,7 @@
 
 
 def same_cell_sum(values, cell_rows, cell_columns):
-    value_columns = turned(stack_lanes(values))
+    value_columns = turned(values)
     blocks = cell_rows.shape[0]
     sums = [jnp.zeros((8, LANES), F32) for _ in range(blocks)]
     for j in range(blocks):
@@ -261,7 +269,7 @@
         for i in range(blocks):
             hit = jnp.where(cell == cell_rows[i : i + 1], value, 0.0)
             sums[i] = sums[i] + jnp.sum(hit.reshape(LANES // 8, 8, LANES), axis=0)
-    return jnp.concatenate([jnp.sum(x, axis=0, keepdims=True) for x in sums], axis=1)
+    return jnp.concatenate([jnp.sum(x, axis=0, keepdims=True) for x in sums], axis=0)
 
 
 def relaxed(now, source, inverse, low_side, high_side, relaxation):
@@ -320,16 +328,6 @@
     return after
 
 
-def side_slots(side_ref, slots):
-    half = slots // 2
-    return [
-        jnp.concatenate(
-            [side_ref[3 * HALO + 1, i : i + 1, :half] for i in (2 * j, 2 * j + 1)], axis=1
-        )
-        for j in range(4)
-    ]
-
-
 def spread_side(place, low, values, depth, col_groups):
     rows = iota((col_groups * HALO * depth, place.shape[1]), 0)
     hot = (rows == place).astype(F32).astype(BF16)
@@ -354,41 +352,68 @@
     return pick_low(matmul(columns_ref[...], hot_ref[...], (1, 0)), low)
 
 
+def side_kernel_inputs(info_ref, side):
+    rows = [info_ref[side, i : i + 1, :] for i in range(5)]
+    whole = [x.astype(jnp.int32) for x in rows]
+    return whole[0], whole[1], rows[2], whole[3], whole[4]
+
+
+def row_integer(rows_ref, index):
+    return rows_ref[index].astype(jnp.int32)
+
+
+def row_cells(rows_ref):
+    return [unstack_lanes(row_integer(rows_ref, index), 1) for index in (4, 5)]
+
+
 def diagonal_kernel(
-    source_ref,
-    storage_ref,
-    slot_index_ref,
-    slot_weight_ref,
+    grids_hbm,
+    rows_ref,
+    matrix_ref,
     scaled_ref,
     inverse_ref,
     row_inverse_ref,
+    source_ref,
+    storage_ref,
     hot_ref,
     columns_ref,
+    sems,
 ):
+    copies = [
+        pltpu.make_async_copy(grids_hbm.at[1], source_ref, sems.at[0]),
+        pltpu.make_async_copy(grids_hbm.at[2], storage_ref, sems.at[1]),
+    ]
+    matrix_copy = pltpu.make_async_copy(grids_hbm.at[0], matrix_ref, sems.at[2])
+    for copy in copies + [matrix_copy]:
+        copy.start()
     depth, area_rows, cols = source_ref.shape
     plane_rows = depth * area_rows
-    low = slot_index_ref[1:2]
-    weight = slot_weight_ref[...]
-    fill_hot(hot_ref, slot_index_ref[0:1])
-    added = fold(matmul(hot_ref[...], masked_parts(low, weight), (1, 1)), 0)
+    high, low = row_cells(rows_ref)
+    weight = rows_ref[0]
+    fill_hot(hot_ref, high)
+    added = fold(matmul(hot_ref[...], masked_parts(low, unstack_lanes(weight, 1)), (1, 1)), 0)
+    for copy in copies:
+        copy.wait()
     for c in range(cols // LANES):
         lanes = slice(c * LANES, (c + 1) * LANES)
         extra = added[c * plane_rows : (c + 1) * plane_rows].reshape(depth, area_rows, LANES)
         inverse = 1.0 / (6.0 + storage_ref[:, :, lanes] + extra)
         scaled_ref[:, :, lanes] = source_ref[:, :, lanes] * inverse
         inverse_ref[:, :, lanes] = inverse
-    row_inverse_ref[...] = weight * pick_cells(inverse_ref, columns_ref, hot_ref, low)
+    row_inverse_ref[...] = weight * stack_lanes(
+        pick_cells(inverse_ref, columns_ref, hot_ref, low)
+    )
+    matrix_copy.wait()
 
 
 def first_window_kernel(
     relaxation,
     matrix_ref,
-    low_ref,
-    high_ref,
     scaled_ref,
     inverse_ref,
-    slot_index_ref,
-    slot_weight_ref,
+    pair_ref,
+    cross_ref,
+    rows_ref,
     fracture_ref,
     links_ref,
     link_weights_ref,
@@ -396,39 +421,44 @@
     side_partial_ref,
     side_scaled_ref,
     side_inverse_ref,
+    side_info_ref,
     row_partial_ref,
     link_sum_ref,
     hot_ref,
     columns_ref,
 ):
     depth, area_rows, cols = matrix_ref.shape
-    slots = slot_index_ref.shape[1]
-    fill_hot(hot_ref, slot_index_ref[0:1])
+    high, low = row_cells(rows_ref)
+    fill_hot(hot_ref, high)
+    odd = (lax.axis_index("area") & 1) == 1
+    tiles = pair_ref.shape[0]
+    lower = [jnp.where(odd, pair_ref[i], cross_ref[i]) for i in range(tiles)]
+    upper = [jnp.where(odd, cross_ref[i], pair_ref[i]) for i in range(tiles)]
+    whole = matrix_ref[...]
     partial_ref[...] = relaxed(
-        matrix_ref[...],
+        whole,
         scaled_ref[...],
         inverse_ref[...],
-        low_ref[0],
-        high_ref[0],
+        lower[0],
+        upper[0],
         relaxation,
     )
-    row_partial_ref[...] = slot_weight_ref[...] * pick_cells(
-        partial_ref, columns_ref, hot_ref, slot_index_ref[1:2]
-    )
-    for side, (ref, edge) in enumerate(((low_ref, 0), (high_ref, area_rows - 1))):
-        place, low, weight, _ = side_slots(ref, slots)
-        added = spread_side(
-            place.astype(jnp.int32), low.astype(jnp.int32), weight, depth, cols // LANES
-        )
+    row_partial_ref[...] = rows_ref[0] * stack_lanes(
+        pick_cells(partial_ref, columns_ref, hot_ref, low)
+    )
+    for side, (tiles, edge) in enumerate(((lower, 0), (upper, area_rows - 1))):
+        side_info_ref[side] = tiles[3 * HALO + 1]
+        place, side_low, side_weight, _, _ = side_kernel_inputs(side_info_ref, side)
+        added = spread_side(place, side_low, side_weight, depth, cols // LANES)
         for far in range(HALO):
-            storage = ref[2 * HALO + 1 + far]
+            storage = tiles[2 * HALO + 1 + far]
             inverse = jnp.where(storage > 0.0, 1.0 / (6.0 + storage + added[far]), 0.0)
             side_inverse_ref[side, far] = inverse
-            side_scaled_ref[side, far] = ref[HALO + 1 + far] * inverse
+            side_scaled_ref[side, far] = tiles[HALO + 1 + far] * inverse
         after = relaxed_side(
-            [ref[far] for far in range(HALO)],
-            ref[HALO],
-            matrix_ref[:, edge, :],
+            tiles[:HALO],
+            tiles[HALO],
+            whole[:, edge, :],
             [side_scaled_ref[side, far] for far in range(HALO)],
             [side_inverse_ref[side, far] for far in range(HALO)],
             relaxation,
@@ -438,17 +468,24 @@
     link_sum_ref[...] = linked(fracture_ref[...], links_ref, link_weights_ref)
 
 
-def add_rows(relaxation, values, partial_ref, inverse_ref, slot_index_ref, hot_ref, matrix_ref):
+def add_rows(relaxation, values, partial_ref, inverse_ref, rows_ref, hot_ref, matrix_ref):
     depth, area_rows, cols = partial_ref.shape
     plane_rows = depth * area_rows
-    fill_hot(hot_ref, slot_index_ref[0:1])
-    added = fold(matmul(hot_ref[...], masked_parts(slot_index_ref[1:2], values), (1, 1)), 0)
+    high, low = row_cells(rows_ref)
+    fill_hot(hot_ref, high)
+    parts = masked_parts(low, unstack_lanes(values, 1))
+    added = fold(matmul(hot_ref[...], parts, (1, 1)), 0)
     for c in range(cols // LANES):
         lanes = slice(c * LANES, (c + 1) * LANES)
         extra = added[c * plane_rows : (c + 1) * plane_rows].reshape(depth, area_rows, LANES)
         matrix_ref[:, :, lanes] = (
             partial_ref[:, :, lanes] + (relaxation * inverse_ref[:, :, lanes]) * extra
         )
+
+
+def returned_values(returned, rows_ref):
+    target, rank = row_integer(rows_ref, 1), row_integer(rows_ref, 2)
+    return rows_ref[0] * pick_entries(returned, target, rank)
 
 
 def window_kernel(
@@ -458,17 +495,15 @@
     first,
     last,
     arrived_ref,
-    low_ref,
-    high_ref,
     partial_before_ref,
     scaled_ref,
     inverse_ref,
     side_before_ref,
     side_scaled_ref,
     side_inverse_ref,
-    slot_index_ref,
-    slot_weight_ref,
-    slot_code_ref,
+    side_info_ref,
+    rows_ref,
+    slots_ref,
     fracture_ref,
     links_ref,
     link_weights_ref,
@@ -483,25 +518,24 @@
         row_partial_ref, matrix_ref, hot_ref, columns_ref = refs
     depth, area_rows, cols = scaled_ref.shape
     devices = arrived_ref.shape[0]
-    slots = devices * cap
-    returned = device_values(arrived_ref, slot_code_ref[...]) if first else arrived_ref[:, 1, :]
-    values = slot_weight_ref[...] * to_dense(returned, cap)
-    add_rows(before, values, partial_before_ref, inverse_ref, slot_index_ref, hot_ref, matrix_ref)
+    half = devices * cap // 2
+    returned = device_values(arrived_ref, row_integer(slots_ref, 2)) if first else arrived_ref[:, 1, :]
+    values = returned_values(returned, rows_ref)
+    add_rows(before, values, partial_before_ref, inverse_ref, rows_ref, hot_ref, matrix_ref)
     edges = []
-    for side, (ref, edge) in enumerate(((low_ref, 0), (high_ref, area_rows - 1))):
-        place, low, weight, code = side_slots(ref, slots)
+    for side, edge in enumerate((0, area_rows - 1)):
+        place, low, weight, target, rank = side_kernel_inputs(side_info_ref, side)
         if first:
+            code = jnp.concatenate(
+                [side_info_ref[side, i : i + 1, :half] for i in (5, 6)], axis=1
+            )
             code = from_dense(code, devices, cap).astype(jnp.int32)
             returned = device_values(arrived_ref, code)
         else:
             returned = arrived_ref[:, 2 + side, :]
-        added = spread_side(
-            place.astype(jnp.int32),
-            low.astype(jnp.int32),
-            weight * to_dense(returned, cap),
-            depth,
-            cols // LANES,
-        )
+        values = pick_entries(returned, stack_lanes(target), stack_lanes(rank))
+        values = weight * unstack_lanes(values, 1)
+        added = spread_side(place, low, values, depth, cols // LANES)
         now = [
             side_before_ref[side, far] + before * side_inverse_ref[side, far] * added[far]
             for far in range(HALO)
@@ -526,26 +560,17 @@
         relaxation,
     )
     if not last:
-        row_partial_ref[...] = slot_weight_ref[...] * pick_cells(
-            partial_ref, columns_ref, hot_ref, slot_index_ref[1:2]
+        row_partial_ref[...] = rows_ref[0] * stack_lanes(
+            pick_cells(partial_ref, columns_ref, hot_ref, row_cells(rows_ref)[1])
         )
     link_sum_ref[...] = linked(fracture_ref[...], links_ref, link_weights_ref)
 
 
-def row_values(
-    relaxation,
-    cap,
-    returned,
-    slot_weight_ref,
-    row_partial_ref,
-    row_inverse_ref,
-    cell_rows_ref,
-    cell_columns_ref,
-):
-    values = slot_weight_ref[...] * to_dense(returned, cap)
-    total = same_cell_sum(values, cell_rows_ref[...], cell_columns_ref[...])
+def row_values(relaxation, returned, slots_ref, rows_ref, row_partial_ref, row_inverse_ref):
+    cells = rows_ref[3]
+    total = same_cell_sum(returned_values(returned, rows_ref), cells, turned(cells))
     outgoing = row_partial_ref[...] + (relaxation * row_inverse_ref[...]) * total
-    return from_dense(outgoing, returned.shape[0], cap)
+    return pick_entries(outgoing, row_integer(slots_ref, 0), row_integer(slots_ref, 1))
 
 
 def node_hot(code, rows):
@@ -585,12 +610,10 @@
     relaxation,
     cap,
     arrived_ref,
-    slot_code_ref,
-    slot_weight_ref,
+    slots_ref,
+    rows_ref,
     row_partial_ref,
     row_inverse_ref,
-    cell_rows_ref,
-    cell_columns_ref,
     fracture_ref,
     link_sum_ref,
     fracture_source_ref,
@@ -606,13 +629,11 @@
     owned = fracture_ref.shape[0]
     message_ref[:, 0, :] = row_values(
         relaxation,
-        cap,
-        device_values(arrived_ref, slot_code_ref[...]),
-        slot_weight_ref,
+        device_values(arrived_ref, row_integer(slots_ref, 2)),
+        slots_ref,
+        rows_ref,
         row_partial_ref,
         row_inverse_ref,
-        cell_rows_ref,
-        cell_columns_ref,
     )
     code = arrived_ref[:, 0, :].astype(jnp.int32)
     node_code_ref[...] = code
@@ -662,11 +683,10 @@
     cap,
     arrived_ref,
     node_code_ref,
-    slot_weight_ref,
+    slots_ref,
+    rows_ref,
     row_partial_ref,
     row_inverse_ref,
-    cell_rows_ref,
-    cell_columns_ref,
     fracture_ref,
     link_sum_ref,
     fracture_source_ref,
@@ -678,13 +698,11 @@
 ):
     message_ref[:, 0, :] = row_values(
         relaxation,
-        cap,
         arrived_ref[:, 1, :],
-        slot_weight_ref,
+        slots_ref,
+        rows_ref,
         row_partial_ref,
         row_inverse_ref,
-        cell_rows_ref,
-        cell_columns_ref,
     )
     code = node_code_ref[...]
     fracture_next = next_fracture(
@@ -711,8 +729,7 @@
     node_code_ref,
     partial_ref,
     inverse_ref,
-    slot_index_ref,
-    slot_weight_ref,
+    rows_ref,
     fracture_ref,
     link_sum_ref,
     fracture_source_ref,
@@ -721,8 +738,8 @@
     fracture_next_ref,
     hot_ref,
 ):
-    values = slot_weight_ref[...] * to_dense(arrived_ref[:, 1, :], cap)
-    add_rows(relaxation, values, partial_ref, inverse_ref, slot_index_ref, hot_ref, matrix_ref)
+    values = returned_values(arrived_ref[:, 1, :], rows_ref)
+    add_rows(relaxation, values, partial_ref, inverse_ref, rows_ref, hot_ref, matrix_ref)
     fracture_next_ref[...] = next_fracture(
         relaxation,
         cap,
@@ -777,20 +794,22 @@
     owned, blk = fracture_start.shape
     total_rows = transfer_cells.shape[0]
     cap = 3 * total_rows // (2 * devices)
-    slots = devices * cap
     cells = depth * area_rows * cols // LANES
     relax = relax_weights(ITERS)
     grid = (matrix_start.shape, F32)
+    grids = ((GRID_SLOTS,) + matrix_start.shape, F32)
     fracture = (fracture_start.shape, F32)
     side = ((3 * HALO + 2, depth, cols), F32)
     sides = ((2, HALO, depth, cols), F32)
-    hot = pltpu.VMEM((cells, slots), BF16)
+    hot = pltpu.VMEM((cells, total_rows), BF16)
     columns = pltpu.VMEM((2 * LANES, cells), BF16)
     padded = (devices, LANES)
     first_message = ((devices, 4 + owned * blk // LANES, LANES), F32)
     message_type = ((devices, 4, LANES), F32)
-    forward = [(i, i + 1) for i in range(devices - 1)]
-    backward = [(target, source) for source, target in forward]
+    pairs, crossings = [
+        [(i + a, i + b) for i in range(start, devices - 1, 2) for a, b in ((0, 1), (1, 0))]
+        for start in (0, 1)
+    ]
 
     def exchange(message):
         return lax.all_to_all(
@@ -813,26 +832,16 @@
         matrix_source,
         matrix_storage,
     ]
-    slot_rows = ((slots // LANES, LANES), F32)
-    slot_columns = ((LANES, slots // LANES + -(slots // LANES) % 8), F32)
-    dense = ((1, slots), F32)
-    slot_index, slot_weight, slot_code, cell_rows, cell_columns, message, up, down = call(
+    row_shape = (total_rows // LANES, LANES)
+    rows = (row_shape, F32)
+    row_info, slot_info, message, pair, cross, grids_start = call(
         functools.partial(setup_kernel, devices, cap, len(staged)),
-        [
-            ((2, slots), jnp.int32),
-            dense,
-            (padded, jnp.int32),
-            slot_rows,
-            slot_columns,
-            first_message,
-            side,
-            side,
-        ],
+        [((6,) + row_shape, F32), ((3,) + padded, F32), first_message, side, side, grids],
         staged,
         "place_rows",
         5.0,
         hbm_in=range(len(staged)),
-        hbm_out=(5, 6, 7),
+        hbm_out=(2, 3, 4, 5),
         scratch=[pltpu.VMEM(x.shape, x.dtype) for x in staged]
         + [
             pltpu.VMEM(*first_message),
@@ -840,32 +849,32 @@
             pltpu.VMEM(*side),
             hot,
             columns,
-            pltpu.SemaphoreType.DMA((len(staged) + 3,)),
+            pltpu.SemaphoreType.DMA((len(staged) + 6,)),
         ],
         limit=63 * 1024 * 1024,
     )
     arrived = exchange(message)
-    low = lax.ppermute(up, "area", forward)
-    high = lax.ppermute(down, "area", backward)
-    scaled, inverse, row_inverse = call(
+    pair = lax.ppermute(pair, "area", pairs)
+    cross = lax.ppermute(cross, "area", crossings)
+    matrix, scaled, inverse, row_inverse = call(
         diagonal_kernel,
-        [grid, grid, dense],
-        [matrix_source, matrix_storage, slot_index, slot_weight],
+        [grid, grid, grid, rows],
+        [grids_start, row_info],
         "diagonal",
         2.0,
-        scratch=[hot, columns],
-    )
-    partial, side_partial, side_scaled, side_inverse, row_partial, link_sum = call(
+        hbm_in=(0,),
+        scratch=[pltpu.VMEM(*grid)] * 2 + [hot, columns, pltpu.SemaphoreType.DMA((3,))],
+    )
+    partial, side_partial, side_scaled, side_inverse, side_info, row_partial, link_sum = call(
         functools.partial(first_window_kernel, relax[0]),
-        [grid, sides, sides, sides, dense, fracture],
+        [grid, sides, sides, sides, ((2, depth, cols), F32), rows, fracture],
         [
-            matrix_start,
-            low,
-            high,
+            matrix,
             scaled,
             inverse,
-            slot_index,
-            slot_weight,
+            pair,
+            cross,
+            row_info,
             fracture_start,
             fracture_links,
             link_weights,
@@ -874,19 +883,18 @@
         2.0,
         scratch=[hot, columns],
     )
+    fracture_now = fracture_start
     message_scratch = [pltpu.VMEM(*message_type), pltpu.SemaphoreType.DMA]
     fracture_now, fracture_inverse, node_code, message = call(
         functools.partial(first_step_kernel, relax[0], cap),
         [fracture, fracture, (padded, jnp.int32), message_type],
         [
             arrived,
-            slot_code,
-            slot_weight,
+            slot_info,
+            row_info,
             row_partial,
             row_inverse,
-            cell_rows,
-            cell_columns,
-            fracture_start,
+            fracture_now,
             link_sum,
             fracture_source,
             fracture_leak,
@@ -902,27 +910,25 @@
         old, arrived = arrived, exchange(message)
         outs = call(
             functools.partial(window_kernel, relax[index], relax[index - 1], cap, index == 1, last),
-            [grid, sides, fracture] + ([] if last else [dense]),
+            [grid, sides, fracture] + ([] if last else [rows]),
             [
                 old,
-                low,
-                high,
                 partial,
                 scaled,
                 inverse,
                 side_partial,
                 side_scaled,
                 side_inverse,
-                slot_index,
-                slot_weight,
-                slot_code,
+                side_info,
+                row_info,
+                slot_info,
                 fracture_now,
                 fracture_links,
                 link_weights,
             ],
             "stencil",
             3.0,
-            aliases={3: 0, 6: 1},
+            aliases={1: 0, 4: 1},
             scratch=[pltpu.VMEM(*grid), hot] + ([] if last else [columns]),
         )
         partial, side_partial, link_sum = outs[:3]
@@ -931,7 +937,7 @@
             return call(
                 functools.partial(last_step_kernel, relax[index], cap),
                 [grid, fracture],
-                [arrived, node_code, partial, inverse, slot_index, slot_weight] + fractures,
+                [arrived, node_code, partial, inverse, row_info] + fractures,
                 "couple_last",
                 2.0,
                 scratch=[hot],
@@ -940,8 +946,7 @@
         fracture_now, message = call(
             functools.partial(step_kernel, relax[index], cap),
             [fracture, message_type],
-            [arrived, node_code, slot_weight, row_partial, row_inverse, cell_rows, cell_columns]
-            + fractures,
+            [arrived, node_code, slot_info, row_info, row_partial, row_inverse] + fractures,
             "couple",
             2.0,
             hbm_out=(1,),

time: 63.8 us -> 58.6 us (0.918)
  Pallas kernels: 29.9 us -> 23.8 us
  waiting for transfers between devices: 1.34 us -> 2.58 us
  local copies, waits for them, and re-layouts: 1.73 us -> 0.76 us
    pallas_call x10, Pallas kernels: 29.9 us -> 23.8 us  [call(): pl.pallas_call(kernel, out_shape=[jax.ShapeDtypeStruct(shape, dtype) for...]
    all_to_all x4, starting transfers between devices: 25 us -> 28.1 us  [exchange(): lax.all_to_all(message, 'area', split_axis=0, concat_axis=0, tiled=True,...]
    ppermute x2, starting transfers between devices: 3.67 us -> 1.19 us  [the longest x1 0.67 us: local(): cross = lax.ppermute(cross, 'area', crossings)]
    all_to_all x4, waiting for transfers between devices: 1.33 us -> 2.57 us  [exchange(): lax.all_to_all(message, 'area', split_axis=0, concat_axis=0, tiled=True,...]
    unnamed x26 -> x16, local copies, waits for them, and re-layouts: 1.73 us -> 0.76 us
  transfers between devices with their start and end apart: 6 -> 6, of which waited for: 1 -> 4; matrix products, arithmetic and copies ran while one was open for 0% -> 0% of each run, Pallas kernels for 25% -> 21%
where the time goes in v3:
time: 58.6 us; the launch traced here: 58 us
  starting transfers between devices  29.3 us (50%)
  Pallas kernels  23.8 us (41%)
  waiting for transfers between devices  2.58 us (4%)
  between operations  1.51 us (3%)
  local copies, waits for them, and re-layouts  0.76 us (1%)
    all_to_all x4, starting transfers between devices, exchange(): lax.all_to_all(message, 'area', split_axis=0, concat_axis=0, tiled=True,...  28.1 us
    pallas_call x10, Pallas kernels, call(): pl.pallas_call(kernel, out_shape=[jax.ShapeDtypeStruct(shape, dtype) for...  23.8 us
    all_to_all x4, waiting for transfers between devices, exchange(): lax.all_to_all(message, 'area', split_axis=0, concat_axis=0, tiled=True,...  2.57 us
  transfers between devices with their start and end apart: 6, of which 4 were waited for; matrix products, arithmetic and copies ran while one was open for 0% of the time, Pallas kernels for 21%

profile of v3, /device:TPU:0, one launch (start us, length us, event | category | flops | bytes accessed | tf_op | source)
XLA Modules:
  0.0 58.0 jit_solution(8753801724233994855)
XLA Ops:
  0.6 0.0 copy-start.6
  0.6 0.0 copy-start.3
  0.7 0.0 copy-start.4
  0.7 0.0 copy-start.5
  0.7 0.0 copy-start.7
  1.4 4.1 %place_rows.1 = (f32[6,8,128]{2,1,0:T(8,128)}, f32[3,16,128]{2,1,0:T(8,128)}, f32[16,20,128]{2,1,0:T(8,128)}, f32[11,8,1024]{2,1,0:T(8,128)}, f32[11,8,1024]{2,1,0:T(8,128)}, /*index=5*/f32[72,8,16,1024]{3,2,1,0:T(8,128)}) custom-call(s32[1,1]{1,0:T(1,128)} %bitcast.5.refs_0_, s32[1,128]{1,0:T(1,128)} %bitcast.9, s32[8,128]{1,0:T(8,128)} %bitcast.6, ...), custom_call_target="tpu_custom_call" | custom-call | bytes 15000000 | tf_op jit(solution)/shard_map/place_rows/pallas_call | solution.py:756
  5.5 0.0 copy-start.1
  5.5 0.0 copy-start.2
  5.5 0.5 collective-permute-start
  6.0 0.7 %collective-permute-start.1 = (f32[11,8,1024]{2,1,0:T(8,128)}, f32[11,8,1024]{2,1,0:T(8,128)S(1)}, u32[]{:S(2)}, u32[]{:S(2)}) collective-permute-start(f32[11,8,1024]{2,1,0:T(8,128)} %get-tuple-element.45), channel_id=1, source_target_pairs={{1,2},{2,1},{3,4},{4,3},{5,6},{6,5},{7,8},{8,7},{9,10},{10,9},{11,... | collective-permute-start | bytes 1081352 | tf_op jit(solution)/shard_map/ppermute | solution.py:858
  6.7 10.4 %all-to-all-start = ((f32[16,20,128]{2,1,0:T(8,128)}), f32[16,20,128]{2,1,0:T(8,128)S(1)}, u32[]{:S(2)}, u32[]{:S(2)}) async-start(f32[16,20,128]{2,1,0:T(8,128)} %get-tuple-element.37), calls=%async_computation | async-start | bytes 393216 | tf_op jit(solution)/shard_map/all_to_all | solution.py:815
  17.1 0.7 %copy-done = f32[6,8,128]{2,1,0:T(8,128)S(1)} copy-done((f32[6,8,128]{2,1,0:T(8,128)S(1)}, f32[6,8,128]{2,1,0:T(8,128)}, u32[]{:S(2)}) %copy-start) | copy-done | bytes 24600
  17.8 3.1 %diagonal.1 = (f32[8,16,1024]{2,1,0:T(8,128)S(1)}, f32[8,16,1024]{2,1,0:T(8,128)S(1)}, f32[8,16,1024]{2,1,0:T(8,128)S(1)}, f32[8,128]{1,0:T(8,128)S(1)}) custom-call(f32[72,8,16,1024]{3,2,1,0:T(8,128)} %get-tuple-element.40.grids_hbm, f32[6,8,128]{2,1,0:T(8,128)S(1)} %copy-done), custom_call_target="tpu_custom_call" | custom-call | bytes 6000000 | tf_op jit(solution)/shard_map/diagonal/pallas_call | solution.py:756
  20.9 0.0 collective-permute-done.pair_ref
  20.9 0.0 collective-permute-done.1.cross_ref
  20.9 0.0 copy-done.6
  21.0 1.8 %stencil_first.1 = (f32[8,16,1024]{2,1,0:T(8,128)S(1)}, f32[2,3,8,1024]{3,2,1,0:T(8,128)S(1)}, f32[2,3,8,1024]{3,2,1,0:T(8,128)S(1)}, f32[2,3,8,1024]{3,2,1,0:T(...) custom-call(f32[8,16,1024]{2,1,0:T(8,128)S(1)} %get-tuple-element.41.matrix_ref, ...), custom_call_target="tpu_custom_call" | custom-call | bytes 6000000 | tf_op jit(solution)/shard_map/stencil_first/pallas_call | solution.py:756
  22.8 0.1 all-to-all-done.arrived_ref
  22.8 0.0 copy-done.7
  22.8 1.9 %couple_first.1 = (f32[8,256]{1,0:T(8,128)S(1)}, f32[8,256]{1,0:T(8,128)S(1)}, s32[16,128]{1,0:T(8,128)S(1)}, f32[16,4,128]{2,1,0:T(4,128)}) custom-call(f32[16,20,128]{2,1,0:T(8,128)S(1)} %all-to-all-done.arrived_ref, f32[3,16,128]{2,1,0:T(8,128)S(1)} %copy-done.2, f32[6,8,128]{2,1,0:T(8,128)S(1)} %copy-done.1, ...), custom_call_target="tpu_custom_call" | custom-call | bytes 6000000 | tf_op jit(solution)/shard_map/couple_first/pallas_call | solution.py:756
  24.8 6.9 %all-to-all-start.1 = ((f32[16,4,128]{2,1,0:T(4,128)}), f32[16,4,128]{2,1,0:T(4,128)S(1)}, u32[]{:S(2)}, u32[]{:S(2)}) async-start(f32[16,4,128]{2,1,0:T(4,128)} %get-tuple-element.49), calls=%async_computation.1 | async-start | bytes 65536 | tf_op jit(solution)/shard_map/all_to_all | solution.py:815
  31.7 3.0 %stencil.3 = (f32[8,16,1024]{2,1,0:T(8,128)S(1)}, f32[2,3,8,1024]{3,2,1,0:T(8,128)S(1)}, f32[8,256]{1,0:T(8,128)S(1)}, f32[8,128]{1,0:T(8,128)S(1)}) custom-call(f32[16,20,128]{2,1,0:T(8,128)S(1)} %all-to-all-done.arrived_ref, f32[8,16,1024]{2,1,0:T(8,128)S(1)} %get-tuple-element.51.partial_before_ref, ...), custom_call_target="tpu_custom_call", output_to_operand_aliasing={{0}: (1, {}), {1}: (4, {})} | custom-call | bytes 9000000 | tf_op jit(solution)/shard_map/stencil/pallas_call | solution.py:756
  34.7 0.2 all-to-all-done.1.arrived_ref
  35.0 1.8 %couple.2 = (f32[8,256]{1,0:T(8,128)S(1)}, f32[16,4,128]{2,1,0:T(4,128)}) custom-call(f32[16,4,128]{2,1,0:T(4,128)S(1)} %all-to-all-done.1.arrived_ref, s32[16,128]{1,0:T(8,128)S(1)} %get-tuple-element.50.node_code_ref, f32[3,16,128]{2,1,0:T(8,128)S(1)} %copy-done.2, f32[6,8,128]{2,1,0:T(8,128)S(1)} %copy-done.1, ...), custom_call_target="tpu_custom_call" | custom-call | bytes 6000000 | tf_op jit(solution)/shard_map/couple/pallas_call | solution.py:756
  36.8 5.5 %all-to-all-start.2 = ((f32[16,4,128]{2,1,0:T(4,128)}), f32[16,4,128]{2,1,0:T(4,128)S(1)}, u32[]{:S(2)}, u32[]{:S(2)}) async-start(f32[16,4,128]{2,1,0:T(4,128)} %get-tuple-element.60), calls=%async_computation.2 | async-start | bytes 65536 | tf_op jit(solution)/shard_map/all_to_all | solution.py:815
  42.2 2.8 %stencil.4 = (f32[8,16,1024]{2,1,0:T(8,128)S(1)}, f32[2,3,8,1024]{3,2,1,0:T(8,128)S(1)}, f32[8,256]{1,0:T(8,128)S(1)}, f32[8,128]{1,0:T(8,128)S(1)}) custom-call(f32[16,4,128]{2,1,0:T(4,128)S(1)} %all-to-all-done.1.arrived_ref, f32[8,16,1024]{2,1,0:T(8,128)S(1)} %get-tuple-element.61.partial_before_ref, ...), custom_call_target="tpu_custom_call", output_to_operand_aliasing={{0}: (1, {}), {1}: (4, {})} | custom-call | bytes 9000000 | tf_op jit(solution)/shard_map/stencil/pallas_call | solution.py:756
  45.0 0.6 all-to-all-done.2.arrived_ref
  45.6 1.8 %couple.3 = (f32[8,256]{1,0:T(8,128)S(1)}, f32[16,4,128]{2,1,0:T(4,128)}) custom-call(f32[16,4,128]{2,1,0:T(4,128)S(1)} %all-to-all-done.2.arrived_ref, s32[16,128]{1,0:T(8,128)S(1)} %get-tuple-element.50.node_code_ref, f32[3,16,128]{2,1,0:T(8,128)S(1)} %copy-done.2, f32[6,8,128]{2,1,0:T(8,128)S(1)} %copy-done.1, ...), custom_call_target="tpu_custom_call" | custom-call | bytes 6000000 | tf_op jit(solution)/shard_map/couple/pallas_call | solution.py:756
  47.4 5.4 %all-to-all-start.3 = ((f32[16,4,128]{2,1,0:T(4,128)}), f32[16,4,128]{2,1,0:T(4,128)S(1)}, u32[]{:S(2)}, u32[]{:S(2)}) async-start(f32[16,4,128]{2,1,0:T(4,128)} %get-tuple-element.66), calls=%async_computation.3 | async-start | bytes 65536 | tf_op jit(solution)/shard_map/all_to_all | solution.py:815
  52.8 1.6 %stencil.5 = (f32[8,16,1024]{2,1,0:T(8,128)S(1)}, f32[2,3,8,1024]{3,2,1,0:T(8,128)S(1)}, f32[8,256]{1,0:T(8,128)S(1)}) custom-call(f32[16,4,128]{2,1,0:T(4,128)S(1)} %all-to-all-done.2.arrived_ref, f32[8,16,1024]{2,1,0:T(8,128)S(1)} %get-tuple-element.67.partial_before_ref, ...), custom_call_target="tpu_custom_call", output_to_operand_aliasing={{0}: (1, {}), {1}: (4, {})} | custom-call | bytes 9000000 | tf_op jit(solution)/shard_map/stencil/pallas_call | solution.py:756
  54.5 1.7 %all-to-all-done.3.arrived_ref = f32[16,4,128]{2,1,0:T(4,128)S(1)} async-done(((f32[16,4,128]{2,1,0:T(4,128)}), f32[16,4,128]{2,1,0:T(4,128)S(1)}, u32[]{:S(2)}, u32[]{:S(2)}) %all-to-all-start.3) | async-done | bytes 32800 | tf_op jit(solution)/shard_map/all_to_all | solution.py:815
  56.2 1.8 %couple_last.1 = (f32[8,16,1024]{2,1,0:T(8,128)}, f32[8,256]{1,0:T(8,128)}) custom-call(f32[16,4,128]{2,1,0:T(4,128)S(1)} %all-to-all-done.3.arrived_ref, s32[16,128]{1,0:T(8,128)S(1)} %get-tuple-element.50.node_code_ref, f32[8,16,1024]{2,1,0:T(8,128)S(1)} %get-tuple-element.70.partial_ref, f32[8,16,1024]{2,1,0:T(8,128)S(1)} %get-tuple-element.43.inverse_ref, ...), custom_call_target="tpu_custom_call" | custom-call | bytes 6000000 | tf_op jit(solution)/shard_map/couple_last/pallas_call | solution.py:756
  (6 shorter events, 0.0 us)
Async XLA Ops:
  0.6 20.3 %copy-start.6 = (f32[8,256]{1,0:T(8,128)S(1)}, f32[8,256]{1,0:T(8,128)}, u32[]{:S(2)}) copy-start(f32[8,256]{1,0:T(8,128)} %fracture_ref.3) | copy-start | bytes 24580
  0.6 20.3 %copy-start.3 = (f32[4,8,256]{2,1,0:T(8,128)S(1)}, f32[4,8,256]{2,1,0:T(8,128)}, u32[]{:S(2)}) copy-start(f32[4,8,256]{2,1,0:T(8,128)} %link_weights_ref.9) | copy-start | bytes 98308
  0.7 20.3 %copy-start.4 = (s32[4,8,256]{2,1,0:T(8,128)S(1)}, s32[4,8,256]{2,1,0:T(8,128)}, u32[]{:S(2)}) copy-start(s32[4,8,256]{2,1,0:T(8,128)} %links_ref.7) | copy-start | bytes 98308
  0.7 22.2 %copy-start.5 = (f32[8,256]{1,0:T(8,128)S(1)}, f32[8,256]{1,0:T(8,128)}, u32[]{:S(2)}) copy-start(f32[8,256]{1,0:T(8,128)} %fracture_source_ref.7) | copy-start | bytes 24580
  0.7 22.2 %copy-start.7 = (f32[8,256]{1,0:T(8,128)S(1)}, f32[8,256]{1,0:T(8,128)}, u32[]{:S(2)}) copy-start(f32[8,256]{1,0:T(8,128)} %leak_ref.1) | copy-start | bytes 24580
  5.5 15.5 %copy-start.1 = (f32[6,8,128]{2,1,0:T(8,128)S(1)}, f32[6,8,128]{2,1,0:T(8,128)}, u32[]{:S(2)}) copy-start(f32[6,8,128]{2,1,0:T(8,128)} %get-tuple-element.39.rows_ref) | copy-start | bytes 73732
  5.5 17.3 %copy-start.2 = (f32[3,16,128]{2,1,0:T(8,128)S(1)}, f32[3,16,128]{2,1,0:T(8,128)}, u32[]{:S(2)}) copy-start(f32[3,16,128]{2,1,0:T(8,128)} %get-tuple-element.38.slots_ref) | copy-start | bytes 73732
  5.5 15.4 %collective-permute-start = (f32[11,8,1024]{2,1,0:T(8,128)}, f32[11,8,1024]{2,1,0:T(8,128)S(1)}, u32[]{:S(2)}, u32[]{:S(2)}) collective-permute-start(f32[11,8,1024]{2,1,0:T(8,128)} %get-tuple-element.44), channel_id=1, source_target_pairs={{0,1},{1,0},{2,3},{3,2},{4,5},{5,4},{6,7},{7,6},{8,9},{9,8},{10,11... | collective-permute-start | bytes 1081352 | tf_op jit(solution)/shard_map/ppermute | solution.py:857
  6.0 14.9 %collective-permute-start.1 = (f32[11,8,1024]{2,1,0:T(8,128)}, f32[11,8,1024]{2,1,0:T(8,128)S(1)}, u32[]{:S(2)}, u32[]{:S(2)}) collective-permute-start(f32[11,8,1024]{2,1,0:T(8,128)} %get-tuple-element.45), channel_id=1, source_target_pairs={{1,2},{2,1},{3,4},{4,3},{5,6},{6,5},{7,8},{8,7},{9,10},{10,9},{11,... | collective-permute-start | bytes 1081352 | tf_op jit(solution)/shard_map/ppermute | solution.py:858
  6.7 16.1 %all-to-all-start = ((f32[16,20,128]{2,1,0:T(8,128)}), f32[16,20,128]{2,1,0:T(8,128)S(1)}, u32[]{:S(2)}, u32[]{:S(2)}) async-start(f32[16,20,128]{2,1,0:T(8,128)} %get-tuple-element.37), calls=%async_computation | async-start | bytes 393216 | tf_op jit(solution)/shard_map/all_to_all | solution.py:815
  17.1 0.7 %copy-start = (f32[6,8,128]{2,1,0:T(8,128)S(1)}, f32[6,8,128]{2,1,0:T(8,128)}, u32[]{:S(2)}) copy-start(f32[6,8,128]{2,1,0:T(8,128)} %get-tuple-element.39.rows_ref) | copy-start | bytes 73732
  24.8 10.1 %all-to-all-start.1 = ((f32[16,4,128]{2,1,0:T(4,128)}), f32[16,4,128]{2,1,0:T(4,128)S(1)}, u32[]{:S(2)}, u32[]{:S(2)}) async-start(f32[16,4,128]{2,1,0:T(4,128)} %get-tuple-element.49), calls=%async_computation.1 | async-start | bytes 65536 | tf_op jit(solution)/shard_map/all_to_all | solution.py:815
  36.8 8.8 %all-to-all-start.2 = ((f32[16,4,128]{2,1,0:T(4,128)}), f32[16,4,128]{2,1,0:T(4,128)S(1)}, u32[]{:S(2)}, u32[]{:S(2)}) async-start(f32[16,4,128]{2,1,0:T(4,128)} %get-tuple-element.60), calls=%async_computation.2 | async-start | bytes 65536 | tf_op jit(solution)/shard_map/all_to_all | solution.py:815
  47.4 8.7 %all-to-all-start.3 = ((f32[16,4,128]{2,1,0:T(4,128)}), f32[16,4,128]{2,1,0:T(4,128)S(1)}, u32[]{:S(2)}, u32[]{:S(2)}) async-start(f32[16,4,128]{2,1,0:T(4,128)} %get-tuple-element.66), calls=%async_computation.3 | async-start | bytes 65536 | tf_op jit(solution)/shard_map/all_to_all | solution.py:815

commit v4 on v3

--- a/solution.py
+++ b/solution.py
@@ -114,11 +114,16 @@
     return found
 
 
+def row_slice(grids_hbm, rows_ref):
+    count, groups, lanes = rows_ref.shape
+    return grids_hbm.at[3, :count, :groups, :lanes]
+
+
 def setup_kernel(devices, cap, staged, *refs):
     sources, refs = refs[:staged], refs[staged:]
-    rows_ref, slots_ref, message_hbm, pair_hbm, cross_hbm, grids_hbm = refs[:6]
+    slots_ref, message_hbm, pair_hbm, cross_hbm, grids_hbm, link_sum_ref = refs[:6]
     targets, refs = refs[6 : 6 + staged], refs[6 + staged :]
-    message_ref, pair_ref, cross_ref, hot_ref, columns_ref, sems = refs
+    rows_ref, message_ref, pair_ref, cross_ref, hot_ref, columns_ref, sems = refs
     copies = [
         pltpu.make_async_copy(sources[i], targets[i], sems.at[i]) for i in range(staged)
     ]
@@ -126,12 +131,13 @@
         pltpu.make_async_copy(targets[i], grids_hbm.at[j], sems.at[staged + 3 + j])
         for j, i in enumerate((5, 7, 8))
     ]
+    kept.append(pltpu.make_async_copy(rows_ref, row_slice(grids_hbm, rows_ref), sems.at[staged + 6]))
     for copy in copies:
         copy.start()
     for copy in copies[:5]:
         copy.wait()
     counts_ref, owner_ref, cells_ref, nodes_ref, weights_ref = targets[:5]
-    matrix_ref, fracture_ref, source_ref, storage_ref = targets[5:]
+    matrix_ref, fracture_ref, source_ref, storage_ref, links_ref, link_weights_ref = targets[5:]
     owned, blk = fracture_ref.shape
     depth, area_rows, cols = matrix_ref.shape
     groups = cells_ref.shape[0]
@@ -196,9 +202,10 @@
     slots_ref[0], slots_ref[1], slots_ref[2] = packed[6], packed[7], code
     for i, x in enumerate((weight, target, rank, cells, cell_high, cell_low)):
         rows_ref[i] = x.astype(F32)
-    message_ref[:, 0, :] = code
-    message_ref[:, 1, :] = packed[3] + packed[4] + packed[5]
-    message_ref[:, 3, :] = jnp.zeros((devices, LANES), F32)
+    kept[3].start()
+    message_ref[:, 0, 0, :] = code
+    message_ref[:, 0, 1, :] = packed[3] + packed[4] + packed[5]
+    message_ref[:, 0, 3, :] = jnp.zeros((devices, LANES), F32)
 
     odd = (lax.axis_index("area") & 1) == 1
     plane = plane_row >> log2(area_rows)
@@ -223,10 +230,14 @@
 
     for copy in copies[5:]:
         copy.wait()
-    for copy in kept:
+    for copy in kept[:3]:
         copy.start()
+    link_sum_ref[...] = linked(fracture_ref[...], links_ref, link_weights_ref)
     node_table = stack_lanes(fracture_ref[...])
-    message_ref[:, 4:, :] = jnp.broadcast_to(node_table[None], (devices,) + node_table.shape)
+    for i in range(node_table.shape[0]):
+        message_ref[:, 1 + i // 4, i % 4, :] = jnp.broadcast_to(
+            node_table[i : i + 1], (devices, LANES)
+        )
     for ref, start, count in (
         (matrix_ref, 0, HALO + 1),
         (source_ref, HALO + 1, HALO),
@@ -245,7 +256,7 @@
     outs[0].start()
     outs[1].start()
     picked = stack_lanes(pick_cells(matrix_ref, columns_ref, hot_ref, low))
-    message_ref[:, 2, :] = pick_entries(weight * picked, slot_row, slot_lane)
+    message_ref[:, 0, 2, :] = pick_entries(weight * picked, slot_row, slot_lane)
     outs[2].start()
     for out in outs + kept:
         out.wait()
@@ -277,8 +288,11 @@
     zero_plane = jnp.zeros((1, rows, cols), F32)
     beside = jnp.concatenate([now[1:], zero_plane], axis=0)
     beside = beside + jnp.concatenate([zero_plane, now[:-1]], axis=0)
-    beside = beside + jnp.concatenate([now[:, 1:], high_side[:, None]], axis=1)
-    beside = beside + jnp.concatenate([low_side[:, None], now[:, :-1]], axis=1)
+    zero_row = jnp.zeros((depth, 1, cols), F32)
+    above = zero_row if high_side is None else high_side[:, None]
+    below = zero_row if low_side is None else low_side[:, None]
+    beside = beside + jnp.concatenate([now[:, 1:], above], axis=1)
+    beside = beside + jnp.concatenate([below, now[:, :-1]], axis=1)
     flat = now.reshape(depth * rows, cols)
     place = iota(flat.shape, 1)
     left = jnp.where(place == 0, 0.0, pltpu.roll(flat, 1, 1))
@@ -366,13 +380,17 @@
     return [unstack_lanes(row_integer(rows_ref, index), 1) for index in (4, 5)]
 
 
-def diagonal_kernel(
+def first_window_kernel(
+    relaxation,
     grids_hbm,
     rows_ref,
-    matrix_ref,
+    partial_ref,
     scaled_ref,
     inverse_ref,
+    edges_ref,
+    row_partial_ref,
     row_inverse_ref,
+    matrix_ref,
     source_ref,
     storage_ref,
     hot_ref,
@@ -380,20 +398,21 @@
     sems,
 ):
     copies = [
-        pltpu.make_async_copy(grids_hbm.at[1], source_ref, sems.at[0]),
-        pltpu.make_async_copy(grids_hbm.at[2], storage_ref, sems.at[1]),
+        pltpu.make_async_copy(row_slice(grids_hbm, rows_ref), rows_ref, sems.at[3]),
+        pltpu.make_async_copy(grids_hbm.at[2], storage_ref, sems.at[2]),
+        pltpu.make_async_copy(grids_hbm.at[1], source_ref, sems.at[1]),
+        pltpu.make_async_copy(grids_hbm.at[0], matrix_ref, sems.at[0]),
     ]
-    matrix_copy = pltpu.make_async_copy(grids_hbm.at[0], matrix_ref, sems.at[2])
-    for copy in copies + [matrix_copy]:
+    for copy in copies:
         copy.start()
-    depth, area_rows, cols = source_ref.shape
+    for copy in copies:
+        copy.wait()
+    depth, area_rows, cols = matrix_ref.shape
     plane_rows = depth * area_rows
     high, low = row_cells(rows_ref)
     weight = rows_ref[0]
     fill_hot(hot_ref, high)
     added = fold(matmul(hot_ref[...], masked_parts(low, unstack_lanes(weight, 1)), (1, 1)), 0)
-    for copy in copies:
-        copy.wait()
     for c in range(cols // LANES):
         lanes = slice(c * LANES, (c + 1) * LANES)
         extra = added[c * plane_rows : (c + 1) * plane_rows].reshape(depth, area_rows, LANES)
@@ -403,69 +422,42 @@
     row_inverse_ref[...] = weight * stack_lanes(
         pick_cells(inverse_ref, columns_ref, hot_ref, low)
     )
-    matrix_copy.wait()
-
-
-def first_window_kernel(
-    relaxation,
-    matrix_ref,
-    scaled_ref,
-    inverse_ref,
-    pair_ref,
-    cross_ref,
-    rows_ref,
-    fracture_ref,
-    links_ref,
-    link_weights_ref,
-    partial_ref,
-    side_partial_ref,
-    side_scaled_ref,
-    side_inverse_ref,
-    side_info_ref,
-    row_partial_ref,
-    link_sum_ref,
-    hot_ref,
-    columns_ref,
-):
-    depth, area_rows, cols = matrix_ref.shape
+    partial_ref[...] = relaxed(
+        matrix_ref[...], scaled_ref[...], inverse_ref[...], None, None, relaxation
+    )
+    row_partial_ref[...] = weight * stack_lanes(pick_cells(partial_ref, columns_ref, hot_ref, low))
+    edges_ref[0] = matrix_ref[:, 0, :]
+    edges_ref[1] = matrix_ref[:, area_rows - 1, :]
+
+
+def row_integer(rows_ref, index):
+    return rows_ref[index].astype(jnp.int32)
+
+
+def row_cells(rows_ref):
+    return [unstack_lanes(row_integer(rows_ref, index), 1) for index in (4, 5)]
+
+
+def both_sides(pair_ref, cross_ref, tiles):
+    odd = (lax.axis_index("area") & 1) == 1
+    lower = [jnp.where(odd, pair_ref[i], cross_ref[i]) for i in tiles]
+    upper = [jnp.where(odd, cross_ref[i], pair_ref[i]) for i in tiles]
+    return lower, upper
+
+
+def beside_rows(pair_ref, cross_ref, rows_ref, area_rows):
+    (lower,), (upper,) = both_sides(pair_ref, cross_ref, (0,))
+    depth = lower.shape[0]
     high, low = row_cells(rows_ref)
-    fill_hot(hot_ref, high)
-    odd = (lax.axis_index("area") & 1) == 1
-    tiles = pair_ref.shape[0]
-    lower = [jnp.where(odd, pair_ref[i], cross_ref[i]) for i in range(tiles)]
-    upper = [jnp.where(odd, cross_ref[i], pair_ref[i]) for i in range(tiles)]
-    whole = matrix_ref[...]
-    partial_ref[...] = relaxed(
-        whole,
-        scaled_ref[...],
-        inverse_ref[...],
-        lower[0],
-        upper[0],
-        relaxation,
-    )
-    row_partial_ref[...] = rows_ref[0] * stack_lanes(
-        pick_cells(partial_ref, columns_ref, hot_ref, low)
-    )
-    for side, (tiles, edge) in enumerate(((lower, 0), (upper, area_rows - 1))):
-        side_info_ref[side] = tiles[3 * HALO + 1]
-        place, side_low, side_weight, _, _ = side_kernel_inputs(side_info_ref, side)
-        added = spread_side(place, side_low, side_weight, depth, cols // LANES)
-        for far in range(HALO):
-            storage = tiles[2 * HALO + 1 + far]
-            inverse = jnp.where(storage > 0.0, 1.0 / (6.0 + storage + added[far]), 0.0)
-            side_inverse_ref[side, far] = inverse
-            side_scaled_ref[side, far] = tiles[HALO + 1 + far] * inverse
-        after = relaxed_side(
-            tiles[:HALO],
-            tiles[HALO],
-            whole[:, edge, :],
-            [side_scaled_ref[side, far] for far in range(HALO)],
-            [side_inverse_ref[side, far] for far in range(HALO)],
-            relaxation,
-        )
-        for far in range(HALO):
-            side_partial_ref[side, far] = after[far]
-    link_sum_ref[...] = linked(fracture_ref[...], links_ref, link_weights_ref)
+    row = high & (area_rows - 1)
+    plane = (high >> log2(area_rows)) & (depth - 1)
+    place = (high >> log2(depth * area_rows)) * depth + plane
+    table = jnp.concatenate([stack_lanes(lower), stack_lanes(upper)], axis=0)
+    place = jnp.where(row == 0, place, place + table.shape[0] // 2)
+    place = jnp.where((row == 0) | (row == area_rows - 1), place, -1)
+    hot = (iota((table.shape[0], place.shape[1]), 0) == place).astype(F32).astype(BF16)
+    columns = jnp.concatenate(halves(table.T), axis=0)
+    return stack_lanes(pick_low(matmul(columns, hot, (1, 0)), low))
 
 
 def add_rows(relaxation, values, partial_ref, inverse_ref, rows_ref, hot_ref, matrix_ref):
@@ -488,6 +480,28 @@
     return rows_ref[0] * pick_entries(returned, target, rank)
 
 
+def first_sides(relaxation, pair_ref, cross_ref, edges_ref, scaled_ref, inverse_ref, info_ref):
+    depth, cols = edges_ref.shape[1:]
+    partial = []
+    for side, tiles in enumerate(both_sides(pair_ref, cross_ref, range(3 * HALO + 2))):
+        info_ref[side] = tiles[3 * HALO + 1]
+        place, low, weight, _, _ = side_kernel_inputs(info_ref, side)
+        added = spread_side(place, low, weight, depth, cols // LANES)
+        scaled, inverse = [], []
+        for far in range(HALO):
+            storage = tiles[2 * HALO + 1 + far]
+            inverse.append(jnp.where(storage > 0.0, 1.0 / (6.0 + storage + added[far]), 0.0))
+            scaled.append(tiles[HALO + 1 + far] * inverse[far])
+            scaled_ref[side, far] = scaled[far]
+            inverse_ref[side, far] = inverse[far]
+        partial.append(
+            relaxed_side(
+                tiles[:HALO], tiles[HALO], edges_ref[side], scaled, inverse, relaxation
+            )
+        )
+    return partial
+
+
 def window_kernel(
     relaxation,
     before,
@@ -498,30 +512,41 @@
     partial_before_ref,
     scaled_ref,
     inverse_ref,
-    side_before_ref,
-    side_scaled_ref,
-    side_inverse_ref,
-    side_info_ref,
     rows_ref,
     slots_ref,
     fracture_ref,
     links_ref,
     link_weights_ref,
-    partial_ref,
-    side_partial_ref,
-    link_sum_ref,
     *refs,
 ):
+    depth, area_rows, cols = scaled_ref.shape
+    devices = arrived_ref.shape[0]
+    half = devices * cap // 2
+    if first:
+        pair_ref, cross_ref, edges_ref, *refs = refs
+        partial_ref, side_partial_ref, link_sum_ref, *refs = refs
+        side_scaled_ref, side_inverse_ref, side_info_ref, *refs = refs
+    else:
+        side_before_ref, side_scaled_ref, side_inverse_ref, side_info_ref, *refs = refs
+        partial_ref, side_partial_ref, link_sum_ref, *refs = refs
     if last:
         matrix_ref, hot_ref = refs
     else:
         row_partial_ref, matrix_ref, hot_ref, columns_ref = refs
-    depth, area_rows, cols = scaled_ref.shape
-    devices = arrived_ref.shape[0]
-    half = devices * cap // 2
     returned = device_values(arrived_ref, row_integer(slots_ref, 2)) if first else arrived_ref[:, 1, :]
     values = returned_values(returned, rows_ref)
     add_rows(before, values, partial_before_ref, inverse_ref, rows_ref, hot_ref, matrix_ref)
+    if first:
+        lower, upper = both_sides(pair_ref, cross_ref, (0,))
+        for edge, tile in ((0, lower[0]), (area_rows - 1, upper[0])):
+            matrix_ref[:, edge, :] = (
+                matrix_ref[:, edge, :] + (before * inverse_ref[:, edge, :]) * tile
+            )
+        side_before = first_sides(
+            before, pair_ref, cross_ref, edges_ref, side_scaled_ref, side_inverse_ref, side_info_ref
+        )
+    else:
+        side_before = [[side_before_ref[side, far] for far in range(HALO)] for side in range(2)]
     edges = []
     for side, edge in enumerate((0, area_rows - 1)):
         place, low, weight, target, rank = side_kernel_inputs(side_info_ref, side)
@@ -537,7 +562,7 @@
         values = weight * unstack_lanes(values, 1)
         added = spread_side(place, low, values, depth, cols // LANES)
         now = [
-            side_before_ref[side, far] + before * side_inverse_ref[side, far] * added[far]
+            side_before[side][far] + before * side_inverse_ref[side, far] * added[far]
             for far in range(HALO)
         ]
         edges.append(now[0])
@@ -566,15 +591,36 @@
     link_sum_ref[...] = linked(fracture_ref[...], links_ref, link_weights_ref)
 
 
-def row_values(relaxation, returned, slots_ref, rows_ref, row_partial_ref, row_inverse_ref):
+def returned_values(returned, rows_ref):
+    target, rank = row_integer(rows_ref, 1), row_integer(rows_ref, 2)
+    return rows_ref[0] * pick_entries(returned, target, rank)
+
+
+def row_values(
+    relaxation, returned, slots_ref, rows_ref, row_partial_ref, row_inverse_ref, beside=None
+):
     cells = rows_ref[3]
     total = same_cell_sum(returned_values(returned, rows_ref), cells, turned(cells))
+    if beside is not None:
+        total = total + beside
     outgoing = row_partial_ref[...] + (relaxation * row_inverse_ref[...]) * total
     return pick_entries(outgoing, row_integer(slots_ref, 0), row_integer(slots_ref, 1))
 
 
-def node_hot(code, rows):
-    return (iota((rows, code.shape[1]), 0) == code >> log2(LANES)).astype(F32).astype(BF16)
+def node_sums(code, shape, *values):
+    owned, blk = shape
+    rows = owned * blk // LANES
+    member = iota((rows, code.shape[1]), 0) == code >> log2(LANES)
+    low = (iota((LANES, code.shape[1]), 0) == code & (LANES - 1)).astype(F32).astype(BF16)
+    parts = []
+    for value in values:
+        high = value.astype(BF16).astype(F32)
+        parts += [jnp.where(member, high, 0.0), jnp.where(member, value - high, 0.0)]
+    sums = matmul(jnp.concatenate(parts, axis=0).astype(BF16), low, (1, 1))
+    sums = [sums[i : i + rows] for i in range(0, sums.shape[0], rows)]
+    return [
+        unstack_lanes(sums[2 * i] + sums[2 * i + 1], owned) for i in range(len(values))
+    ]
 
 
 def node_values(table, code):
@@ -589,8 +635,8 @@
 def device_values(arrived_ref, code):
     found = jnp.zeros(code.shape, F32)
     low = code & (LANES - 1)
-    for row in range(arrived_ref.shape[1] - 4):
-        values = lane_gather(arrived_ref[:, 4 + row, :], low)
+    for row in range(4 * (arrived_ref.shape[1] - 1)):
+        values = lane_gather(arrived_ref[:, 1 + row // 4, row % 4, :], low)
         found = jnp.where(code >> log2(LANES) == row, values, found)
     return found
 
@@ -609,7 +655,10 @@
 def first_step_kernel(
     relaxation,
     cap,
+    area_rows,
     arrived_ref,
+    pair_ref,
+    cross_ref,
     slots_ref,
     rows_ref,
     row_partial_ref,
@@ -626,7 +675,6 @@
     message_ref,
     sem,
 ):
-    owned = fracture_ref.shape[0]
     message_ref[:, 0, :] = row_values(
         relaxation,
         device_values(arrived_ref, row_integer(slots_ref, 2)),
@@ -634,23 +682,22 @@
         rows_ref,
         row_partial_ref,
         row_inverse_ref,
-    )
-    code = arrived_ref[:, 0, :].astype(jnp.int32)
+        beside_rows(pair_ref, cross_ref, rows_ref, area_rows),
+    )
+    code = arrived_ref[:, 0, 0, :].astype(jnp.int32)
     node_code_ref[...] = code
     dense = to_dense(code, cap)
-    parts = masked_parts(
-        dense & (LANES - 1),
-        to_dense(arrived_ref[:, 1, :], cap),
-        to_dense(arrived_ref[:, 2, :], cap),
-    )
-    sums = matmul(node_hot(dense, fracture_ref.shape[0] * fracture_ref.shape[1] // LANES), parts, (1, 1))
-    diag = (
-        leak_ref[...] + jnp.sum(link_weights_ref[...], axis=0) + unstack_lanes(fold(sums, 0), owned)
-    )
+    weight_sum, value_sum = node_sums(
+        dense,
+        fracture_ref.shape,
+        to_dense(arrived_ref[:, 0, 1, :], cap),
+        to_dense(arrived_ref[:, 0, 2, :], cap),
+    )
+    diag = leak_ref[...] + jnp.sum(link_weights_ref[...], axis=0) + weight_sum
     inverse = 1.0 / diag
     fracture_inverse_ref[...] = inverse
     fracture_next = (1.0 - relaxation) * fracture_ref[...] + (relaxation * inverse) * (
-        fracture_source_ref[...] + link_sum_ref[...] + unstack_lanes(fold(sums, 1), owned)
+        fracture_source_ref[...] + link_sum_ref[...] + value_sum
     )
     fracture_next_ref[...] = fracture_next
     put_requested(message_ref, node_values(stack_lanes(fracture_next), code))
@@ -669,12 +716,11 @@
     fracture_source_ref,
     fracture_inverse_ref,
 ):
-    owned, blk = fracture_ref.shape
-    dense = to_dense(code, cap)
-    parts = masked_parts(dense & (LANES - 1), to_dense(arrived_ref[:, 0, :], cap))
-    sums = matmul(node_hot(dense, owned * blk // LANES), parts, (1, 1))
+    (value_sum,) = node_sums(
+        to_dense(code, cap), fracture_ref.shape, to_dense(arrived_ref[:, 0, :], cap)
+    )
     return (1.0 - relaxation) * fracture_ref[...] + (relaxation * fracture_inverse_ref[...]) * (
-        fracture_source_ref[...] + link_sum_ref[...] + unstack_lanes(fold(sums, 0), owned)
+        fracture_source_ref[...] + link_sum_ref[...] + value_sum
     )
 
 
@@ -804,7 +850,7 @@
     hot = pltpu.VMEM((cells, total_rows), BF16)
     columns = pltpu.VMEM((2 * LANES, cells), BF16)
     padded = (devices, LANES)
-    first_message = ((devices, 4 + owned * blk // LANES, LANES), F32)
+    first_message = ((devices, 1 + owned * blk // LANES // 4, 4, LANES), F32)
     message_type = ((devices, 4, LANES), F32)
     pairs, crossings = [
         [(i + a, i + b) for i in range(start, devices - 1, 2) for a, b in ((0, 1), (1, 0))]
@@ -831,65 +877,54 @@
         fracture_start,
         matrix_source,
         matrix_storage,
+        fracture_links,
+        link_weights,
     ]
     row_shape = (total_rows // LANES, LANES)
     rows = (row_shape, F32)
-    row_info, slot_info, message, pair, cross, grids_start = call(
+    info = ((6,) + row_shape, F32)
+    edges = ((2, depth, cols), F32)
+    slot_info, message, pair, cross, grids_start, link_sum = call(
         functools.partial(setup_kernel, devices, cap, len(staged)),
-        [((6,) + row_shape, F32), ((3,) + padded, F32), first_message, side, side, grids],
+        [((3,) + padded, F32), first_message, side, side, grids, fracture],
         staged,
         "place_rows",
         5.0,
         hbm_in=range(len(staged)),
-        hbm_out=(2, 3, 4, 5),
+        hbm_out=(1, 2, 3, 4),
         scratch=[pltpu.VMEM(x.shape, x.dtype) for x in staged]
         + [
+            pltpu.VMEM(*info),
             pltpu.VMEM(*first_message),
             pltpu.VMEM(*side),
             pltpu.VMEM(*side),
             hot,
             columns,
-            pltpu.SemaphoreType.DMA((len(staged) + 6,)),
+            pltpu.SemaphoreType.DMA((len(staged) + 7,)),
         ],
         limit=63 * 1024 * 1024,
     )
     arrived = exchange(message)
     pair = lax.ppermute(pair, "area", pairs)
     cross = lax.ppermute(cross, "area", crossings)
-    matrix, scaled, inverse, row_inverse = call(
-        diagonal_kernel,
-        [grid, grid, grid, rows],
-        [grids_start, row_info],
-        "diagonal",
-        2.0,
+    row_info, partial, scaled, inverse, edge_rows, row_partial, row_inverse = call(
+        functools.partial(first_window_kernel, relax[0]),
+        [info, grid, grid, grid, edges, rows, rows],
+        [grids_start],
+        "stencil_first",
+        4.0,
         hbm_in=(0,),
-        scratch=[pltpu.VMEM(*grid)] * 2 + [hot, columns, pltpu.SemaphoreType.DMA((3,))],
-    )
-    partial, side_partial, side_scaled, side_inverse, side_info, row_partial, link_sum = call(
-        functools.partial(first_window_kernel, relax[0]),
-        [grid, sides, sides, sides, ((2, depth, cols), F32), rows, fracture],
-        [
-            matrix,
-            scaled,
-            inverse,
-            pair,
-            cross,
-            row_info,
-            fracture_start,
-            fracture_links,
-            link_weights,
-        ],
-        "stencil_first",
-        2.0,
-        scratch=[hot, columns],
+        scratch=[pltpu.VMEM(*grid)] * 3 + [hot, columns, pltpu.SemaphoreType.DMA((4,))],
     )
     fracture_now = fracture_start
     message_scratch = [pltpu.VMEM(*message_type), pltpu.SemaphoreType.DMA]
     fracture_now, fracture_inverse, node_code, message = call(
-        functools.partial(first_step_kernel, relax[0], cap),
+        functools.partial(first_step_kernel, relax[0], cap, area_rows),
         [fracture, fracture, (padded, jnp.int32), message_type],
         [
             arrived,
+            pair,
+            cross,
             slot_info,
             row_info,
             row_partial,
@@ -908,30 +943,27 @@
     for index in range(1, ITERS):
         last = index == ITERS - 1
         old, arrived = arrived, exchange(message)
+        first = index == 1
+        inputs = [old, partial, scaled, inverse, row_info, slot_info, fracture_now]
+        inputs += [fracture_links, link_weights]
+        if first:
+            inputs += [pair, cross, edge_rows]
+        else:
+            inputs += [side_partial, side_scaled, side_inverse, side_info]
         outs = call(
-            functools.partial(window_kernel, relax[index], relax[index - 1], cap, index == 1, last),
-            [grid, sides, fracture] + ([] if last else [rows]),
-            [
-                old,
-                partial,
-                scaled,
-                inverse,
-                side_partial,
-                side_scaled,
-                side_inverse,
-                side_info,
-                row_info,
-                slot_info,
-                fracture_now,
-                fracture_links,
-                link_weights,
-            ],
+            functools.partial(window_kernel, relax[index], relax[index - 1], cap, first, last),
+            [grid, sides, fracture]
+            + ([sides, sides, edges] if first else [])
+            + ([] if last else [rows]),
+            inputs,
             "stencil",
             3.0,
-            aliases={1: 0, 4: 1},
+            aliases={1: 0} if first else {1: 0, 9: 1},
             scratch=[pltpu.VMEM(*grid), hot] + ([] if last else [columns]),
         )
         partial, side_partial, link_sum = outs[:3]
+        if first:
+            side_scaled, side_inverse, side_info = outs[3:6]
         fractures = [fracture_now, link_sum, fracture_source, fracture_inverse]
         if last:
             return call(
@@ -942,7 +974,7 @@
                 2.0,
                 scratch=[hot],
             )
-        row_partial = outs[3]
+        row_partial = outs[-1]
         fracture_now, message = call(
             functools.partial(step_kernel, relax[index], cap),
             [fracture, message_type],

time: 58.6 us -> 56.9 us (0.971)
  local copies, waits for them, and re-layouts: 0.76 us -> 0.03 us
    unnamed x16 -> x14, local copies, waits for them, and re-layouts: 0.76 us -> 0.03 us
    pallas_call x10 -> x9, Pallas kernels: 23.8 us -> 23.3 us  [call(): pl.pallas_call(kernel, out_shape=[jax.ShapeDtypeStruct(shape, dtype) for...]
  transfers between devices with their start and end apart: 6 -> 6, of which waited for: 4 -> 3; matrix products, arithmetic and copies ran while one was open for 0% -> 0% of each run, Pallas kernels for 21% -> 21%
where the time goes in v4:
time: 56.9 us; the launch traced here: 56.4 us
  starting transfers between devices  29.1 us (51%)
  Pallas kernels  23.3 us (41%)
  waiting for transfers between devices  2.42 us (4%)
  between operations  1.52 us (3%)
    all_to_all x4, starting transfers between devices, exchange(): lax.all_to_all(message, 'area', split_axis=0, concat_axis=0, tiled=True,...  27.9 us
    pallas_call x9, Pallas kernels, call(): pl.pallas_call(kernel, out_shape=[jax.ShapeDtypeStruct(shape, dtype) for...  23.3 us
    all_to_all x4, waiting for transfers between devices, exchange(): lax.all_to_all(message, 'area', split_axis=0, concat_axis=0, tiled=True,...  2.41 us
  transfers between devices with their start and end apart: 6, of which 3 were waited for; matrix products, arithmetic and copies ran while one was open for 0% of the time, Pallas kernels for 21%

profile of v4, /device:TPU:0, one launch (start us, length us, event | category | flops | bytes accessed | tf_op | source)
XLA Modules:
  0.0 56.4 jit_solution(362342862041949267)
XLA Ops:
  0.6 0.0 copy-start.1
  0.6 0.0 copy-start.2
  0.7 0.0 copy-start.4
  0.7 0.0 copy-start.3
  0.7 0.0 copy-start.5
  1.4 4.2 %place_rows.1 = (f32[3,16,128]{2,1,0:T(8,128)}, f32[16,5,4,128]{3,2,1,0:T(4,128)}, f32[11,8,1024]{2,1,0:T(8,128)}, f32[11,8,1024]{2,1,0:T(8,128)}, f32[72,8,16,1024]{3,2,1,0:T(8,128)}, /*index=5*/f32[8,256]{1,0:T(8,128)}) custom-call(s32[1,1]{1,0:T(1,128)} %bitcast.5.refs_0_, s32[1,128]{1,0:T(1,128)} %bitcast.9, s32[8,128]{1,0:T(8,128)} %bitcast.6, ...), custom_call_target="tpu_custom_call" | custom-call | bytes 15000000 | tf_op jit(solution)/shard_map/place_rows/pallas_call | solution.py:802
  5.6 0.0 copy-start
  5.6 0.0 copy-start.6
  5.6 0.5 collective-permute-start
  6.1 0.7 %collective-permute-start.1 = (f32[11,8,1024]{2,1,0:T(8,128)}, f32[11,8,1024]{2,1,0:T(8,128)S(1)}, u32[]{:S(2)}, u32[]{:S(2)}) collective-permute-start(f32[11,8,1024]{2,1,0:T(8,128)} %get-tuple-element.38), channel_id=1, source_target_pairs={{1,2},{2,1},{3,4},{4,3},{5,6},{6,5},{7,8},{8,7},{9,10},{10,9},{11,... | collective-permute-start | bytes 1081352 | tf_op jit(solution)/shard_map/ppermute | solution.py:909
  6.8 10.4 %all-to-all-start = ((f32[16,5,4,128]{3,2,1,0:T(4,128)}), f32[16,5,4,128]{3,2,1,0:T(4,128)S(1)}, u32[]{:S(2)}, u32[]{:S(2)}) async-start(f32[16,5,4,128]{3,2,1,0:T(4,128)} %get-tuple-element.36), calls=%async_computation | async-start | bytes 327680 | tf_op jit(solution)/shard_map/all_to_all | solution.py:861
  17.2 4.4 %stencil_first.1 = (f32[6,8,128]{2,1,0:T(8,128)S(1)}, f32[8,16,1024]{2,1,0:T(8,128)S(1)}, f32[8,16,1024]{2,1,0:T(8,128)S(1)}, f32[8,16,1024]{2,1,0:T(8,128)S(1)}...) custom-call(f32[72,8,16,1024]{3,2,1,0:T(8,128)} %get-tuple-element.40.grids_hbm), custom_call_target="tpu_custom_call" | custom-call | bytes 12000000 | tf_op jit(solution)/shard_map/stencil_first/pallas_call | solution.py:802
  21.6 0.0 all-to-all-done.arrived_ref
  21.6 0.0 collective-permute-done.pair_ref.refs_0_
  21.7 0.0 collective-permute-done.1.cross_ref.refs_1_
  21.7 0.0 copy-done.1
  21.7 0.0 copy-done.4
  21.7 0.0 copy-done.3
  21.7 0.0 copy-done.5
  21.7 2.0 %couple_first.1 = (f32[8,256]{1,0:T(8,128)S(1)}, f32[8,256]{1,0:T(8,128)S(1)}, s32[16,128]{1,0:T(8,128)S(1)}, f32[16,4,128]{2,1,0:T(4,128)}) custom-call(f32[16,5,4,128]{3,2,1,0:T(4,128)S(1)} %all-to-all-done.arrived_ref, f32[11,8,1024]{2,1,0:T(8,128)S(1)} %collective-permute-done.pair_ref.refs_0_, ...), custom_call_target="tpu_custom_call" | custom-call | bytes 6000000 | tf_op jit(solution)/shard_map/couple_first/pallas_call | solution.py:802
  23.7 6.7 %all-to-all-start.1 = ((f32[16,4,128]{2,1,0:T(4,128)}), f32[16,4,128]{2,1,0:T(4,128)S(1)}, u32[]{:S(2)}, u32[]{:S(2)}) async-start(f32[16,4,128]{2,1,0:T(4,128)} %get-tuple-element.45), calls=%async_computation.1 | async-start | bytes 65536 | tf_op jit(solution)/shard_map/all_to_all | solution.py:861
  30.4 3.1 %stencil.3 = (f32[8,16,1024]{2,1,0:T(8,128)S(1)}, f32[2,3,8,1024]{3,2,1,0:T(8,128)S(1)}, f32[8,256]{1,0:T(8,128)S(1)}, f32[2,3,8,1024]{3,2,1,0:T(8,128)S(1)}, f3...) custom-call(f32[16,5,4,128]{3,2,1,0:T(4,128)S(1)} %all-to-all-done.a, ...), custom_call_target="tpu_custom_call", output_to_operand_aliasing={{0}: (1, {})} | custom-call | bytes 9000000 | tf_op jit(solution)/shard_map/stencil/pallas_call | solution.py:802
  33.5 0.1 all-to-all-done.1.arrived_ref
  33.7 1.7 %couple.2 = (f32[8,256]{1,0:T(8,128)S(1)}, f32[16,4,128]{2,1,0:T(4,128)}) custom-call(f32[16,4,128]{2,1,0:T(4,128)S(1)} %all-to-all-done.1.arrived_ref, s32[16,128]{1,0:T(8,128)S(1)} %get-tuple-element.46.node_code_ref, f32[3,16,128]{2,1,0:T(8,128)S(1)} %copy-done, f32[6,8,128]{2,1,0:T(8,128)S(1)} %get-tuple-element.41.rows_ref, ...), custom_call_target="tpu_custom_call" | custom-call | bytes 6000000 | tf_op jit(solution)/shard_map/couple/pallas_call | solution.py:802
  35.4 5.5 %all-to-all-start.2 = ((f32[16,4,128]{2,1,0:T(4,128)}), f32[16,4,128]{2,1,0:T(4,128)S(1)}, u32[]{:S(2)}, u32[]{:S(2)}) async-start(f32[16,4,128]{2,1,0:T(4,128)} %get-tuple-element.55), calls=%async_computation.2 | async-start | bytes 65536 | tf_op jit(solution)/shard_map/all_to_all | solution.py:861
  40.9 2.7 %stencil.4 = (f32[8,16,1024]{2,1,0:T(8,128)S(1)}, f32[2,3,8,1024]{3,2,1,0:T(8,128)S(1)}, f32[8,256]{1,0:T(8,128)S(1)}, f32[8,128]{1,0:T(8,128)S(1)}) custom-call(f32[16,4,128]{2,1,0:T(4,128)S(1)} %all-to-all-done.1.arrived_ref, f32[8,16,1024]{2,1,0:T(8,128)S(1)} %get-tuple-element.56.partial_before_ref, ...), custom_call_target="tpu_custom_call", output_to_operand_aliasing={{0}: (1, {}), {1}: (9, {})} | custom-call | bytes 9000000 | tf_op jit(solution)/shard_map/stencil/pallas_call | solution.py:802
  43.6 0.6 %all-to-all-done.2.arrived_ref = f32[16,4,128]{2,1,0:T(4,128)S(1)} async-done(((f32[16,4,128]{2,1,0:T(4,128)}), f32[16,4,128]{2,1,0:T(4,128)S(1)}, u32[]{:S(2)}, u32[]{:S(2)}) %all-to-all-start.2) | async-done | bytes 32800 | tf_op jit(solution)/shard_map/all_to_all | solution.py:861
  44.2 1.7 %couple.3 = (f32[8,256]{1,0:T(8,128)S(1)}, f32[16,4,128]{2,1,0:T(4,128)}) custom-call(f32[16,4,128]{2,1,0:T(4,128)S(1)} %all-to-all-done.2.arrived_ref, s32[16,128]{1,0:T(8,128)S(1)} %get-tuple-element.46.node_code_ref, f32[3,16,128]{2,1,0:T(8,128)S(1)} %copy-done, f32[6,8,128]{2,1,0:T(8,128)S(1)} %get-tuple-element.41.rows_ref, ...), custom_call_target="tpu_custom_call" | custom-call | bytes 6000000 | tf_op jit(solution)/shard_map/couple/pallas_call | solution.py:802
  45.9 5.4 %all-to-all-start.3 = ((f32[16,4,128]{2,1,0:T(4,128)}), f32[16,4,128]{2,1,0:T(4,128)S(1)}, u32[]{:S(2)}, u32[]{:S(2)}) async-start(f32[16,4,128]{2,1,0:T(4,128)} %get-tuple-element.64), calls=%async_computation.3 | async-start | bytes 65536 | tf_op jit(solution)/shard_map/all_to_all | solution.py:861
  51.3 1.6 %stencil.5 = (f32[8,16,1024]{2,1,0:T(8,128)S(1)}, f32[2,3,8,1024]{3,2,1,0:T(8,128)S(1)}, f32[8,256]{1,0:T(8,128)S(1)}) custom-call(f32[16,4,128]{2,1,0:T(4,128)S(1)} %all-to-all-done.2.arrived_ref, f32[8,16,1024]{2,1,0:T(8,128)S(1)} %get-tuple-element.65.partial_before_ref, ...), custom_call_target="tpu_custom_call", output_to_operand_aliasing={{0}: (1, {}), {1}: (9, {})} | custom-call | bytes 9000000 | tf_op jit(solution)/shard_map/stencil/pallas_call | solution.py:802
  53.0 1.7 %all-to-all-done.3.arrived_ref = f32[16,4,128]{2,1,0:T(4,128)S(1)} async-done(((f32[16,4,128]{2,1,0:T(4,128)}), f32[16,4,128]{2,1,0:T(4,128)S(1)}, u32[]{:S(2)}, u32[]{:S(2)}) %all-to-all-start.3) | async-done | bytes 32800 | tf_op jit(solution)/shard_map/all_to_all | solution.py:861
  54.7 1.7 %couple_last.1 = (f32[8,16,1024]{2,1,0:T(8,128)}, f32[8,256]{1,0:T(8,128)}) custom-call(f32[16,4,128]{2,1,0:T(4,128)S(1)} %all-to-all-done.3.arrived_ref, s32[16,128]{1,0:T(8,128)S(1)} %get-tuple-element.46.node_code_ref, f32[8,16,1024]{2,1,0:T(8,128)S(1)} %get-tuple-element.68.partial_ref, f32[8,16,1024]{2,1,0:T(8,128)S(1)} %get-tuple-element.49.inverse_ref, ...), custom_call_target="tpu_custom_call" | custom-call | bytes 6000000 | tf_op jit(solution)/shard_map/couple_last/pallas_call | solution.py:802
  (3 shorter events, 0.0 us)
Async XLA Ops:
  0.6 21.0 %copy-start.1 = (f32[4,8,256]{2,1,0:T(8,128)S(1)}, f32[4,8,256]{2,1,0:T(8,128)}, u32[]{:S(2)}) copy-start(f32[4,8,256]{2,1,0:T(8,128)} %link_weights_ref.7) | copy-start | bytes 98308
  0.6 29.7 %copy-start.2 = (s32[4,8,256]{2,1,0:T(8,128)S(1)}, s32[4,8,256]{2,1,0:T(8,128)}, u32[]{:S(2)}) copy-start(s32[4,8,256]{2,1,0:T(8,128)} %links_ref.5) | copy-start | bytes 98308
  0.7 21.0 %copy-start.4 = (f32[8,256]{1,0:T(8,128)S(1)}, f32[8,256]{1,0:T(8,128)}, u32[]{:S(2)}) copy-start(f32[8,256]{1,0:T(8,128)} %fracture_ref.1) | copy-start | bytes 24580
  0.7 21.0 %copy-start.3 = (f32[8,256]{1,0:T(8,128)S(1)}, f32[8,256]{1,0:T(8,128)}, u32[]{:S(2)}) copy-start(f32[8,256]{1,0:T(8,128)} %fracture_source_ref.7) | copy-start | bytes 24580
  0.7 21.0 %copy-start.5 = (f32[8,256]{1,0:T(8,128)S(1)}, f32[8,256]{1,0:T(8,128)}, u32[]{:S(2)}) copy-start(f32[8,256]{1,0:T(8,128)} %leak_ref.1) | copy-start | bytes 24580
  5.6 16.1 %copy-start = (f32[3,16,128]{2,1,0:T(8,128)S(1)}, f32[3,16,128]{2,1,0:T(8,128)}, u32[]{:S(2)}) copy-start(f32[3,16,128]{2,1,0:T(8,128)} %get-tuple-element.39.slots_ref) | copy-start | bytes 73732
  5.6 16.1 %copy-start.6 = (f32[8,256]{1,0:T(8,128)S(1)}, f32[8,256]{1,0:T(8,128)}, u32[]{:S(2)}) copy-start(f32[8,256]{1,0:T(8,128)} %get-tuple-element.44.link_sum_ref) | copy-start | bytes 24580
  5.6 16.0 %collective-permute-start = (f32[11,8,1024]{2,1,0:T(8,128)}, f32[11,8,1024]{2,1,0:T(8,128)S(1)}, u32[]{:S(2)}, u32[]{:S(2)}) collective-permute-start(f32[11,8,1024]{2,1,0:T(8,128)} %get-tuple-element.37), channel_id=1, source_target_pairs={{0,1},{1,0},{2,3},{3,2},{4,5},{5,4},{6,7},{7,6},{8,9},{9,8},{10,11... | collective-permute-start | bytes 1081352 | tf_op jit(solution)/shard_map/ppermute | solution.py:908
  6.1 15.5 %collective-permute-start.1 = (f32[11,8,1024]{2,1,0:T(8,128)}, f32[11,8,1024]{2,1,0:T(8,128)S(1)}, u32[]{:S(2)}, u32[]{:S(2)}) collective-permute-start(f32[11,8,1024]{2,1,0:T(8,128)} %get-tuple-element.38), channel_id=1, source_target_pairs={{1,2},{2,1},{3,4},{4,3},{5,6},{6,5},{7,8},{8,7},{9,10},{10,9},{11,... | collective-permute-start | bytes 1081352 | tf_op jit(solution)/shard_map/ppermute | solution.py:909
  6.8 14.8 %all-to-all-start = ((f32[16,5,4,128]{3,2,1,0:T(4,128)}), f32[16,5,4,128]{3,2,1,0:T(4,128)S(1)}, u32[]{:S(2)}, u32[]{:S(2)}) async-start(f32[16,5,4,128]{3,2,1,0:T(4,128)} %get-tuple-element.36), calls=%async_computation | async-start | bytes 327680 | tf_op jit(solution)/shard_map/all_to_all | solution.py:861
  23.7 10.0 %all-to-all-start.1 = ((f32[16,4,128]{2,1,0:T(4,128)}), f32[16,4,128]{2,1,0:T(4,128)S(1)}, u32[]{:S(2)}, u32[]{:S(2)}) async-start(f32[16,4,128]{2,1,0:T(4,128)} %get-tuple-element.45), calls=%async_computation.1 | async-start | bytes 65536 | tf_op jit(solution)/shard_map/all_to_all | solution.py:861
  35.4 8.8 %all-to-all-start.2 = ((f32[16,4,128]{2,1,0:T(4,128)}), f32[16,4,128]{2,1,0:T(4,128)S(1)}, u32[]{:S(2)}, u32[]{:S(2)}) async-start(f32[16,4,128]{2,1,0:T(4,128)} %get-tuple-element.55), calls=%async_computation.2 | async-start | bytes 65536 | tf_op jit(solution)/shard_map/all_to_all | solution.py:861
  45.9 8.7 %all-to-all-start.3 = ((f32[16,4,128]{2,1,0:T(4,128)}), f32[16,4,128]{2,1,0:T(4,128)S(1)}, u32[]{:S(2)}, u32[]{:S(2)}) async-start(f32[16,4,128]{2,1,0:T(4,128)} %get-tuple-element.64), calls=%async_computation.3 | async-start | bytes 65536 | tf_op jit(solution)/shard_map/all_to_all | solution.py:861

commit v5 on v4

--- a/solution.py
+++ b/solution.py
@@ -200,7 +200,9 @@
     code = jnp.where(packed[0] > 0.5, packed[1] * LANES + packed[2], -1.0)
     slot_row, slot_lane = packed[6].astype(jnp.int32), packed[7].astype(jnp.int32)
     slots_ref[0], slots_ref[1], slots_ref[2] = packed[6], packed[7], code
-    for i, x in enumerate((weight, target, rank, cells, cell_high, cell_low)):
+    alone = -1 - iota(shape, 0) * LANES - iota(shape, 1)
+    cell = jnp.where(live, cells, alone)
+    for i, x in enumerate((weight, target, rank, cell, cell_high, cell_low)):
         rows_ref[i] = x.astype(F32)
     kept[3].start()
     message_ref[:, 0, 0, :] = code
@@ -270,17 +272,51 @@
     return rows.T
 
 
-def same_cell_sum(values, cell_rows, cell_columns):
-    value_columns = turned(values)
-    blocks = cell_rows.shape[0]
-    sums = [jnp.zeros((8, LANES), F32) for _ in range(blocks)]
+def find_chains(cells):
+    blocks = cells.shape[0]
+    columns = turned(cells)
+    none = float(blocks * LANES)
+    sublane, lane = iota((LANES, LANES), 0), iota((LANES, LANES), 1)
+    after = [jnp.full((8, LANES), none, F32) for _ in range(blocks)]
+    before = [jnp.full((8, LANES), -1.0, F32) for _ in range(blocks)]
+    count = [jnp.zeros((8, LANES), F32) for _ in range(blocks)]
     for j in range(blocks):
-        cell = jnp.broadcast_to(cell_columns[:, j : j + 1], (LANES, LANES))
-        value = jnp.broadcast_to(value_columns[:, j : j + 1], (LANES, LANES))
+        cell = jnp.broadcast_to(columns[:, j : j + 1], (LANES, LANES))
+        place = (sublane + j * LANES).astype(F32)
         for i in range(blocks):
-            hit = jnp.where(cell == cell_rows[i : i + 1], value, 0.0)
-            sums[i] = sums[i] + jnp.sum(hit.reshape(LANES // 8, 8, LANES), axis=0)
-    return jnp.concatenate([jnp.sum(x, axis=0, keepdims=True) for x in sums], axis=0)
+            same = cell == cells[i : i + 1]
+            parts = (LANES // 8, 8, LANES)
+            ones = jnp.where(same, 1.0, 0.0).reshape(parts)
+            count[i] = count[i] + jnp.sum(ones, axis=0)
+            if j >= i:
+                later = same & (sublane > lane) if j == i else same
+                found = jnp.where(later, place, none).reshape(parts)
+                after[i] = jnp.minimum(after[i], jnp.min(found, axis=0))
+            if j <= i:
+                sooner = same & (sublane < lane) if j == i else same
+                found = jnp.where(sooner, place, -1.0).reshape(parts)
+                before[i] = jnp.maximum(before[i], jnp.max(found, axis=0))
+    after = jnp.concatenate([jnp.min(x, axis=0, keepdims=True) for x in after], axis=0)
+    before = jnp.concatenate([jnp.max(x, axis=0, keepdims=True) for x in before], axis=0)
+    count = jnp.concatenate([jnp.sum(x, axis=0, keepdims=True) for x in count], axis=0)
+    return jnp.where(after < none, after, -1.0), before, count
+
+
+def same_cell_sum(values, chains_ref):
+    most = jnp.max(chains_ref[2]).astype(jnp.int32)
+    rounds = log2(values.size)
+    steps = sum((most > (1 << i)).astype(jnp.int32) for i in range(rounds))
+
+    def step(_, state):
+        after = []
+        for total, link in (state[:2], state[2:]):
+            row, lane = (link - 1) >> log2(LANES), (link - 1) & (LANES - 1)
+            after += [total + pick_entries(total, row, lane), pick_entries(link, row, lane)]
+        return tuple(after)
+
+    ahead, behind = [row_integer(chains_ref, i) + 1 for i in range(2)]
+    ahead, _, behind, _ = lax.fori_loop(0, steps, step, (values, ahead, values, behind))
+    return ahead + behind - values
 
 
 def relaxed(now, source, inverse, low_side, high_side, relaxation):
@@ -390,6 +426,7 @@
     edges_ref,
     row_partial_ref,
     row_inverse_ref,
+    chains_ref,
     matrix_ref,
     source_ref,
     storage_ref,
@@ -428,6 +465,9 @@
     row_partial_ref[...] = weight * stack_lanes(pick_cells(partial_ref, columns_ref, hot_ref, low))
     edges_ref[0] = matrix_ref[:, 0, :]
     edges_ref[1] = matrix_ref[:, area_rows - 1, :]
+    chains = find_chains(rows_ref[3])
+    for i, x in enumerate(chains):
+        chains_ref[i] = x
 
 
 def row_integer(rows_ref, index):
@@ -597,10 +637,16 @@
 
 
 def row_values(
-    relaxation, returned, slots_ref, rows_ref, row_partial_ref, row_inverse_ref, beside=None
+    relaxation,
+    returned,
+    slots_ref,
+    rows_ref,
+    row_partial_ref,
+    row_inverse_ref,
+    chains_ref,
+    beside=None,
 ):
-    cells = rows_ref[3]
-    total = same_cell_sum(returned_values(returned, rows_ref), cells, turned(cells))
+    total = same_cell_sum(returned_values(returned, rows_ref), chains_ref)
     if beside is not None:
         total = total + beside
     outgoing = row_partial_ref[...] + (relaxation * row_inverse_ref[...]) * total
@@ -663,6 +709,7 @@
     rows_ref,
     row_partial_ref,
     row_inverse_ref,
+    chains_ref,
     fracture_ref,
     link_sum_ref,
     fracture_source_ref,
@@ -682,6 +729,7 @@
         rows_ref,
         row_partial_ref,
         row_inverse_ref,
+        chains_ref,
         beside_rows(pair_ref, cross_ref, rows_ref, area_rows),
     )
     code = arrived_ref[:, 0, 0, :].astype(jnp.int32)
@@ -733,6 +781,7 @@
     rows_ref,
     row_partial_ref,
     row_inverse_ref,
+    chains_ref,
     fracture_ref,
     link_sum_ref,
     fracture_source_ref,
@@ -749,6 +798,7 @@
         rows_ref,
         row_partial_ref,
         row_inverse_ref,
+        chains_ref,
     )
     code = node_code_ref[...]
     fracture_next = next_fracture(
@@ -907,9 +957,9 @@
     arrived = exchange(message)
     pair = lax.ppermute(pair, "area", pairs)
     cross = lax.ppermute(cross, "area", crossings)
-    row_info, partial, scaled, inverse, edge_rows, row_partial, row_inverse = call(
+    row_info, partial, scaled, inverse, edge_rows, row_partial, row_inverse, chains = call(
         functools.partial(first_window_kernel, relax[0]),
-        [info, grid, grid, grid, edges, rows, rows],
+        [info, grid, grid, grid, edges, rows, rows, ((3,) + row_shape, F32)],
         [grids_start],
         "stencil_first",
         4.0,
@@ -929,6 +979,7 @@
             row_info,
             row_partial,
             row_inverse,
+            chains,
             fracture_now,
             link_sum,
             fracture_source,
@@ -978,7 +1029,8 @@
         fracture_now, message = call(
             functools.partial(step_kernel, relax[index], cap),
             [fracture, message_type],
-            [arrived, node_code, slot_info, row_info, row_partial, row_inverse] + fractures,
+            [arrived, node_code, slot_info, row_info, row_partial, row_inverse, chains]
+            + fractures,
             "couple",
             2.0,
             hbm_out=(1,),

time: 56.9 us -> 55.7 us (0.979)
  Pallas kernels: 23.3 us -> 22.4 us
    pallas_call x9, Pallas kernels: 23.3 us -> 22.4 us  [call(): pl.pallas_call(kernel, out_shape=[jax.ShapeDtypeStruct(shape, dtype) for...]
  transfers between devices with their start and end apart: 6 -> 6, of which waited for: 3 -> 3; matrix products, arithmetic and copies ran while one was open for 0% -> 0% of each run, Pallas kernels for 21% -> 23%
where the time goes in v5:
time: 55.7 us; the launch traced here: 55 us
  starting transfers between devices  28.6 us (51%)
  Pallas kernels  22.4 us (40%)
  waiting for transfers between devices  2.42 us (4%)
  between operations  1.52 us (3%)
    all_to_all x4, starting transfers between devices, exchange(): lax.all_to_all(message, 'area', split_axis=0, concat_axis=0, tiled=True,...  27.4 us
    pallas_call x9, Pallas kernels, call(): pl.pallas_call(kernel, out_shape=[jax.ShapeDtypeStruct(shape, dtype) for...  22.4 us
    all_to_all x4, waiting for transfers between devices, exchange(): lax.all_to_all(message, 'area', split_axis=0, concat_axis=0, tiled=True,...  2.41 us
  transfers between devices with their start and end apart: 6, of which 3 were waited for; matrix products, arithmetic and copies ran while one was open for 0% of the time, Pallas kernels for 23%

profile of v5, /device:TPU:0, one launch (start us, length us, event | category | flops | bytes accessed | tf_op | source)
XLA Modules:
  0.0 55.0 jit_solution(17051024264762329457)
XLA Ops:
  0.6 0.0 copy-start.1
  0.6 0.0 copy-start.2
  0.7 0.0 copy-start.4
  0.7 0.0 copy-start.3
  1.4 4.2 %place_rows.1 = (f32[3,16,128]{2,1,0:T(8,128)}, f32[16,5,4,128]{3,2,1,0:T(4,128)}, f32[11,8,1024]{2,1,0:T(8,128)}, f32[11,8,1024]{2,1,0:T(8,128)}, f32[72,8,16,1024]{3,2,1,0:T(8,128)}, /*index=5*/f32[8,256]{1,0:T(8,128)}) custom-call(s32[1,1]{1,0:T(1,128)} %bitcast.5.refs_0_, s32[1,128]{1,0:T(1,128)} %bitcast.9, s32[8,128]{1,0:T(8,128)} %bitcast.6, ...), custom_call_target="tpu_custom_call" | custom-call | bytes 15000000 | tf_op jit(solution)/shard_map/place_rows/pallas_call | solution.py:852
  5.6 0.0 copy-start.6
  5.6 0.5 collective-permute-start
  6.1 0.7 %collective-permute-start.1 = (f32[11,8,1024]{2,1,0:T(8,128)}, f32[11,8,1024]{2,1,0:T(8,128)S(1)}, u32[]{:S(2)}, u32[]{:S(2)}) collective-permute-start(f32[11,8,1024]{2,1,0:T(8,128)} %get-tuple-element.39), channel_id=1, source_target_pairs={{1,2},{2,1},{3,4},{4,3},{5,6},{6,5},{7,8},{8,7},{9,10},{10,9},{11,... | collective-permute-start | bytes 1081352 | tf_op jit(solution)/shard_map/ppermute | solution.py:959
  6.8 10.4 %all-to-all-start = ((f32[16,5,4,128]{3,2,1,0:T(4,128)}), f32[16,5,4,128]{3,2,1,0:T(4,128)S(1)}, u32[]{:S(2)}, u32[]{:S(2)}) async-start(f32[16,5,4,128]{3,2,1,0:T(4,128)} %get-tuple-element.37), calls=%async_computation | async-start | bytes 327680 | tf_op jit(solution)/shard_map/all_to_all | solution.py:911
  17.2 4.9 %stencil_first.1 = (f32[6,8,128]{2,1,0:T(8,128)S(1)}, f32[8,16,1024]{2,1,0:T(8,128)S(1)}, f32[8,16,1024]{2,1,0:T(8,128)S(1)}, f32[8,16,1024]{2,1,0:T(8,128)S(1)}...) custom-call(f32[72,8,16,1024]{3,2,1,0:T(8,128)} %get-tuple-element.41.grids_hbm), custom_call_target="tpu_custom_call" | custom-call | bytes 12000000 | tf_op jit(solution)/shard_map/stencil_first/pallas_call | solution.py:852
  22.1 0.0 all-to-all-done.arrived_ref
  22.1 0.0 collective-permute-done.pair_ref.refs_0_
  22.1 0.0 collective-permute-done.1.cross_ref.refs_1_
  22.1 0.0 copy-done.1
  22.2 0.0 copy-done.4
  22.2 0.0 copy-done.3
  22.2 0.0 copy-done.5
  22.2 0.0 copy-done
  22.2 0.0 copy-done.6
  22.2 1.5 %couple_first.1 = (f32[8,256]{1,0:T(8,128)S(1)}, f32[8,256]{1,0:T(8,128)S(1)}, s32[16,128]{1,0:T(8,128)S(1)}, f32[16,4,128]{2,1,0:T(4,128)}) custom-call(f32[16,5,4,128]{3,2,1,0:T(4,128)S(1)} %all-to-all-done.arrived_ref, f32[11,8,1024]{2,1,0:T(8,128)S(1)} %collective-permute-done.pair_ref.refs_0_, ...), custom_call_target="tpu_custom_call" | custom-call | bytes 6000000 | tf_op jit(solution)/shard_map/couple_first/pallas_call | solution.py:852
  23.7 6.2 %all-to-all-start.1 = ((f32[16,4,128]{2,1,0:T(4,128)}), f32[16,4,128]{2,1,0:T(4,128)S(1)}, u32[]{:S(2)}, u32[]{:S(2)}) async-start(f32[16,4,128]{2,1,0:T(4,128)} %get-tuple-element.47), calls=%async_computation.1 | async-start | bytes 65536 | tf_op jit(solution)/shard_map/all_to_all | solution.py:911
  29.9 3.1 %stencil.3 = (f32[8,16,1024]{2,1,0:T(8,128)S(1)}, f32[2,3,8,1024]{3,2,1,0:T(8,128)S(1)}, f32[8,256]{1,0:T(8,128)S(1)}, f32[2,3,8,1024]{3,2,1,0:T(8,128)S(1)}, f3...) custom-call(f32[16,5,4,128]{3,2,1,0:T(4,128)S(1)} %all-to-all-done.a, ...), custom_call_target="tpu_custom_call", output_to_operand_aliasing={{0}: (1, {})} | custom-call | bytes 9000000 | tf_op jit(solution)/shard_map/stencil/pallas_call | solution.py:852
  33.1 0.1 all-to-all-done.1.arrived_ref
  33.2 1.2 %couple.2 = (f32[8,256]{1,0:T(8,128)S(1)}, f32[16,4,128]{2,1,0:T(4,128)}) custom-call(f32[16,4,128]{2,1,0:T(4,128)S(1)} %all-to-all-done.1.arrived_ref, s32[16,128]{1,0:T(8,128)S(1)} %get-tuple-element.48.node_code_ref, f32[3,16,128]{2,1,0:T(8,128)S(1)} %copy-done, f32[6,8,128]{2,1,0:T(8,128)S(1)} %get-tuple-element.42.rows_ref, ...), custom_call_target="tpu_custom_call" | custom-call | bytes 6000000 | tf_op jit(solution)/shard_map/couple/pallas_call | solution.py:852
  34.5 5.5 %all-to-all-start.2 = ((f32[16,4,128]{2,1,0:T(4,128)}), f32[16,4,128]{2,1,0:T(4,128)S(1)}, u32[]{:S(2)}, u32[]{:S(2)}) async-start(f32[16,4,128]{2,1,0:T(4,128)} %get-tuple-element.57), calls=%async_computation.2 | async-start | bytes 65536 | tf_op jit(solution)/shard_map/all_to_all | solution.py:911
  39.9 2.7 %stencil.4 = (f32[8,16,1024]{2,1,0:T(8,128)S(1)}, f32[2,3,8,1024]{3,2,1,0:T(8,128)S(1)}, f32[8,256]{1,0:T(8,128)S(1)}, f32[8,128]{1,0:T(8,128)S(1)}) custom-call(f32[16,4,128]{2,1,0:T(4,128)S(1)} %all-to-all-done.1.arrived_ref, f32[8,16,1024]{2,1,0:T(8,128)S(1)} %get-tuple-element.58.partial_before_ref, ...), custom_call_target="tpu_custom_call", output_to_operand_aliasing={{0}: (1, {}), {1}: (9, {})} | custom-call | bytes 9000000 | tf_op jit(solution)/shard_map/stencil/pallas_call | solution.py:852
  42.7 0.6 %all-to-all-done.2.arrived_ref = f32[16,4,128]{2,1,0:T(4,128)S(1)} async-done(((f32[16,4,128]{2,1,0:T(4,128)}), f32[16,4,128]{2,1,0:T(4,128)S(1)}, u32[]{:S(2)}, u32[]{:S(2)}) %all-to-all-start.2) | async-done | bytes 32800 | tf_op jit(solution)/shard_map/all_to_all | solution.py:911
  43.2 1.2 %couple.3 = (f32[8,256]{1,0:T(8,128)S(1)}, f32[16,4,128]{2,1,0:T(4,128)}) custom-call(f32[16,4,128]{2,1,0:T(4,128)S(1)} %all-to-all-done.2.arrived_ref, s32[16,128]{1,0:T(8,128)S(1)} %get-tuple-element.48.node_code_ref, f32[3,16,128]{2,1,0:T(8,128)S(1)} %copy-done, f32[6,8,128]{2,1,0:T(8,128)S(1)} %get-tuple-element.42.rows_ref, ...), custom_call_target="tpu_custom_call" | custom-call | bytes 6000000 | tf_op jit(solution)/shard_map/couple/pallas_call | solution.py:852
  44.5 5.4 %all-to-all-start.3 = ((f32[16,4,128]{2,1,0:T(4,128)}), f32[16,4,128]{2,1,0:T(4,128)S(1)}, u32[]{:S(2)}, u32[]{:S(2)}) async-start(f32[16,4,128]{2,1,0:T(4,128)} %get-tuple-element.66), calls=%async_computation.3 | async-start | bytes 65536 | tf_op jit(solution)/shard_map/all_to_all | solution.py:911
  49.9 1.6 %stencil.5 = (f32[8,16,1024]{2,1,0:T(8,128)S(1)}, f32[2,3,8,1024]{3,2,1,0:T(8,128)S(1)}, f32[8,256]{1,0:T(8,128)S(1)}) custom-call(f32[16,4,128]{2,1,0:T(4,128)S(1)} %all-to-all-done.2.arrived_ref, f32[8,16,1024]{2,1,0:T(8,128)S(1)} %get-tuple-element.67.partial_before_ref, ...), custom_call_target="tpu_custom_call", output_to_operand_aliasing={{0}: (1, {}), {1}: (9, {})} | custom-call | bytes 9000000 | tf_op jit(solution)/shard_map/stencil/pallas_call | solution.py:852
  51.5 1.7 %all-to-all-done.3.arrived_ref = f32[16,4,128]{2,1,0:T(4,128)S(1)} async-done(((f32[16,4,128]{2,1,0:T(4,128)}), f32[16,4,128]{2,1,0:T(4,128)S(1)}, u32[]{:S(2)}, u32[]{:S(2)}) %all-to-all-start.3) | async-done | bytes 32800 | tf_op jit(solution)/shard_map/all_to_all | solution.py:911
  53.2 1.7 %couple_last.1 = (f32[8,16,1024]{2,1,0:T(8,128)}, f32[8,256]{1,0:T(8,128)}) custom-call(f32[16,4,128]{2,1,0:T(4,128)S(1)} %all-to-all-done.3.arrived_ref, s32[16,128]{1,0:T(8,128)S(1)} %get-tuple-element.48.node_code_ref, f32[8,16,1024]{2,1,0:T(8,128)S(1)} %get-tuple-element.70.partial_ref, f32[8,16,1024]{2,1,0:T(8,128)S(1)} %get-tuple-element.51.inverse_ref, ...), custom_call_target="tpu_custom_call" | custom-call | bytes 6000000 | tf_op jit(solution)/shard_map/couple_last/pallas_call | solution.py:852
  (3 shorter events, 0.0 us)
Async XLA Ops:
  0.6 21.5 %copy-start.1 = (f32[4,8,256]{2,1,0:T(8,128)S(1)}, f32[4,8,256]{2,1,0:T(8,128)}, u32[]{:S(2)}) copy-start(f32[4,8,256]{2,1,0:T(8,128)} %link_weights_ref.7) | copy-start | bytes 98308
  0.6 29.3 %copy-start.2 = (s32[4,8,256]{2,1,0:T(8,128)S(1)}, s32[4,8,256]{2,1,0:T(8,128)}, u32[]{:S(2)}) copy-start(s32[4,8,256]{2,1,0:T(8,128)} %links_ref.5) | copy-start | bytes 98308
  0.7 21.5 %copy-start.4 = (f32[8,256]{1,0:T(8,128)S(1)}, f32[8,256]{1,0:T(8,128)}, u32[]{:S(2)}) copy-start(f32[8,256]{1,0:T(8,128)} %fracture_ref.1) | copy-start | bytes 24580
  0.7 21.5 %copy-start.3 = (f32[8,256]{1,0:T(8,128)S(1)}, f32[8,256]{1,0:T(8,128)}, u32[]{:S(2)}) copy-start(f32[8,256]{1,0:T(8,128)} %fracture_source_ref.7) | copy-start | bytes 24580
  0.7 21.5 %copy-start.5 = (f32[8,256]{1,0:T(8,128)S(1)}, f32[8,256]{1,0:T(8,128)}, u32[]{:S(2)}) copy-start(f32[8,256]{1,0:T(8,128)} %leak_ref.1) | copy-start | bytes 24580
  5.6 16.6 %copy-start = (f32[3,16,128]{2,1,0:T(8,128)S(1)}, f32[3,16,128]{2,1,0:T(8,128)}, u32[]{:S(2)}) copy-start(f32[3,16,128]{2,1,0:T(8,128)} %get-tuple-element.40.slots_ref) | copy-start | bytes 73732
  5.6 16.6 %copy-start.6 = (f32[8,256]{1,0:T(8,128)S(1)}, f32[8,256]{1,0:T(8,128)}, u32[]{:S(2)}) copy-start(f32[8,256]{1,0:T(8,128)} %get-tuple-element.46.link_sum_ref) | copy-start | bytes 24580
  5.6 16.5 %collective-permute-start = (f32[11,8,1024]{2,1,0:T(8,128)}, f32[11,8,1024]{2,1,0:T(8,128)S(1)}, u32[]{:S(2)}, u32[]{:S(2)}) collective-permute-start(f32[11,8,1024]{2,1,0:T(8,128)} %get-tuple-element.38), channel_id=1, source_target_pairs={{0,1},{1,0},{2,3},{3,2},{4,5},{5,4},{6,7},{7,6},{8,9},{9,8},{10,11... | collective-permute-start | bytes 1081352 | tf_op jit(solution)/shard_map/ppermute | solution.py:958
  6.1 16.0 %collective-permute-start.1 = (f32[11,8,1024]{2,1,0:T(8,128)}, f32[11,8,1024]{2,1,0:T(8,128)S(1)}, u32[]{:S(2)}, u32[]{:S(2)}) collective-permute-start(f32[11,8,1024]{2,1,0:T(8,128)} %get-tuple-element.39), channel_id=1, source_target_pairs={{1,2},{2,1},{3,4},{4,3},{5,6},{6,5},{7,8},{8,7},{9,10},{10,9},{11,... | collective-permute-start | bytes 1081352 | tf_op jit(solution)/shard_map/ppermute | solution.py:959
  6.8 15.3 %all-to-all-start = ((f32[16,5,4,128]{3,2,1,0:T(4,128)}), f32[16,5,4,128]{3,2,1,0:T(4,128)S(1)}, u32[]{:S(2)}, u32[]{:S(2)}) async-start(f32[16,5,4,128]{3,2,1,0:T(4,128)} %get-tuple-element.37), calls=%async_computation | async-start | bytes 327680 | tf_op jit(solution)/shard_map/all_to_all | solution.py:911
  23.7 9.5 %all-to-all-start.1 = ((f32[16,4,128]{2,1,0:T(4,128)}), f32[16,4,128]{2,1,0:T(4,128)S(1)}, u32[]{:S(2)}, u32[]{:S(2)}) async-start(f32[16,4,128]{2,1,0:T(4,128)} %get-tuple-element.47), calls=%async_computation.1 | async-start | bytes 65536 | tf_op jit(solution)/shard_map/all_to_all | solution.py:911
  34.5 8.8 %all-to-all-start.2 = ((f32[16,4,128]{2,1,0:T(4,128)}), f32[16,4,128]{2,1,0:T(4,128)S(1)}, u32[]{:S(2)}, u32[]{:S(2)}) async-start(f32[16,4,128]{2,1,0:T(4,128)} %get-tuple-element.57), calls=%async_computation.2 | async-start | bytes 65536 | tf_op jit(solution)/shard_map/all_to_all | solution.py:911
  44.5 8.7 %all-to-all-start.3 = ((f32[16,4,128]{2,1,0:T(4,128)}), f32[16,4,128]{2,1,0:T(4,128)S(1)}, u32[]{:S(2)}, u32[]{:S(2)}) async-start(f32[16,4,128]{2,1,0:T(4,128)} %get-tuple-element.66), calls=%async_computation.3 | async-start | bytes 65536 | tf_op jit(solution)/shard_map/all_to_all | solution.py:911

commit v6 on v5

--- a/solution.py
+++ b/solution.py
@@ -31,7 +31,7 @@
 
 def group_order(devices):
     part = devices // 4
-    return [quarter * part + (i - 1) % part for quarter in (2, 0, 1, 3) for i in range(part)]
+    return [part * z + i for i in reversed(range(part)) for z in (2, 0, 1, 3)]
 
 
 def iota(shape, dim):
@@ -224,7 +224,7 @@
         (pair_ref, jnp.where(odd, places[1], places[0])),
         (cross_ref, jnp.where(odd, places[0], places[1])),
     ):
-        tile = ref.at[3 * HALO + 1]
+        tile = ref.at[3 * HALO]
         for i, x in enumerate([unstack_lanes(place, 1)] + info):
             tile[i : i + 1, :] = x
         tile[5:6, :half] = dense[:, :half]
@@ -240,16 +240,15 @@
         message_ref[:, 1 + i // 4, i % 4, :] = jnp.broadcast_to(
             node_table[i : i + 1], (devices, LANES)
         )
-    for ref, start, count in (
-        (matrix_ref, 0, HALO + 1),
-        (source_ref, HALO + 1, HALO),
-        (storage_ref, 2 * HALO + 1, HALO),
-    ):
-        for far in range(count):
+    for part, ref in enumerate((matrix_ref, source_ref, storage_ref)):
+        for far in range(HALO):
             up = ref[:, area_rows - 1 - far, :]
             down = ref[:, far, :]
-            pair_ref[start + far] = jnp.where(odd, down, up)
-            cross_ref[start + far] = jnp.where(odd, up, down)
+            if part == 1 and far == HALO - 1:
+                up = up + matrix_ref[:, area_rows - 1 - HALO, :]
+                down = down + matrix_ref[:, HALO, :]
+            pair_ref[part * HALO + far] = jnp.where(odd, down, up)
+            cross_ref[part * HALO + far] = jnp.where(odd, up, down)
     outs = [
         pltpu.make_async_copy(pair_ref, pair_hbm, sems.at[staged]),
         pltpu.make_async_copy(cross_ref, cross_hbm, sems.at[staged + 1]),
@@ -356,7 +355,7 @@
     return jnp.concatenate(sums, axis=1)
 
 
-def relaxed_side(now, beyond, edge, scaled, inverse, relaxation):
+def relaxed_side(now, edge, scaled, inverse, relaxation):
     depth, cols = edge.shape
     place = iota(edge.shape, 1)
     zero_plane = jnp.zeros((1, cols), F32)
@@ -370,8 +369,6 @@
         beside = beside + (edge if far == 0 else now[far - 1])
         if far + 1 < HALO:
             beside = beside + now[far + 1]
-        elif beyond is not None:
-            beside = beside + beyond
         after.append(
             (1.0 - relaxation) * here + relaxation * (scaled[far] + inverse[far] * beside)
         )
@@ -523,21 +520,19 @@
 def first_sides(relaxation, pair_ref, cross_ref, edges_ref, scaled_ref, inverse_ref, info_ref):
     depth, cols = edges_ref.shape[1:]
     partial = []
-    for side, tiles in enumerate(both_sides(pair_ref, cross_ref, range(3 * HALO + 2))):
-        info_ref[side] = tiles[3 * HALO + 1]
+    for side, tiles in enumerate(both_sides(pair_ref, cross_ref, range(3 * HALO + 1))):
+        info_ref[side] = tiles[3 * HALO]
         place, low, weight, _, _ = side_kernel_inputs(info_ref, side)
         added = spread_side(place, low, weight, depth, cols // LANES)
         scaled, inverse = [], []
         for far in range(HALO):
-            storage = tiles[2 * HALO + 1 + far]
+            storage = tiles[2 * HALO + far]
             inverse.append(jnp.where(storage > 0.0, 1.0 / (6.0 + storage + added[far]), 0.0))
-            scaled.append(tiles[HALO + 1 + far] * inverse[far])
+            scaled.append(tiles[HALO + far] * inverse[far])
             scaled_ref[side, far] = scaled[far]
             inverse_ref[side, far] = inverse[far]
         partial.append(
-            relaxed_side(
-                tiles[:HALO], tiles[HALO], edges_ref[side], scaled, inverse, relaxation
-            )
+            relaxed_side(tiles[:HALO], edges_ref[side], scaled, inverse, relaxation)
         )
     return partial
 
@@ -608,7 +603,6 @@
         edges.append(now[0])
         after = relaxed_side(
             now,
-            None,
             matrix_ref[:, edge, :],
             [side_scaled_ref[side, far] for far in range(HALO)],
             [side_inverse_ref[side, far] for far in range(HALO)],
@@ -895,7 +889,7 @@
     grid = (matrix_start.shape, F32)
     grids = ((GRID_SLOTS,) + matrix_start.shape, F32)
     fracture = (fracture_start.shape, F32)
-    side = ((3 * HALO + 2, depth, cols), F32)
+    side = ((3 * HALO + 1, depth, cols), F32)
     sides = ((2, HALO, depth, cols), F32)
     hot = pltpu.VMEM((cells, total_rows), BF16)
     columns = pltpu.VMEM((2 * LANES, cells), BF16)

time: 55.7 us -> 54.5 us (0.978)
  starting transfers between devices: 28.6 us -> 27.5 us
    all_to_all x4, starting transfers between devices: 27.4 us -> 26.3 us  [exchange(): lax.all_to_all(message, 'area', split_axis=0, concat_axis=0, tiled=True,...]
where the time goes in v6:
time: 54.5 us; the launch traced here: 54 us
  starting transfers between devices  27.5 us (50%)
  Pallas kernels  22.6 us (41%)
  waiting for transfers between devices  2.3 us (4%)
  between operations  1.52 us (3%)
    all_to_all x4, starting transfers between devices, exchange(): lax.all_to_all(message, 'area', split_axis=0, concat_axis=0, tiled=True,...  26.3 us
    pallas_call x9, Pallas kernels, call(): pl.pallas_call(kernel, out_shape=[jax.ShapeDtypeStruct(shape, dtype) for...  22.6 us
    all_to_all x4, waiting for transfers between devices, exchange(): lax.all_to_all(message, 'area', split_axis=0, concat_axis=0, tiled=True,...  2.3 us
  transfers between devices with their start and end apart: 6, of which 3 were waited for; matrix products, arithmetic and copies ran while one was open for 0% of the time, Pallas kernels for 23%

profile of v6, /device:TPU:0, one launch (start us, length us, event | category | flops | bytes accessed | tf_op | source)
XLA Modules:
  0.0 54.0 jit_solution(4819533192999103464)
XLA Ops:
  0.6 0.0 copy-start.1
  0.6 0.0 copy-start.2
  0.7 0.0 copy-start.4
  0.7 0.0 copy-start.3
  0.7 0.0 copy-start.5
  1.4 4.2 %place_rows.1 = (f32[3,16,128]{2,1,0:T(8,128)}, f32[16,5,4,128]{3,2,1,0:T(4,128)}, f32[10,8,1024]{2,1,0:T(8,128)}, f32[10,8,1024]{2,1,0:T(8,128)}, f32[72,8,16,1024]{3,2,1,0:T(8,128)}, /*index=5*/f32[8,256]{1,0:T(8,128)}) custom-call(s32[1,1]{1,0:T(1,128)} %bitcast.5.refs_0_, s32[1,128]{1,0:T(1,128)} %bitcast.9, s32[8,128]{1,0:T(8,128)} %bitcast.6, ...), custom_call_target="tpu_custom_call" | custom-call | bytes 15000000 | tf_op jit(solution)/shard_map/place_rows/pallas_call | solution.py:846
  5.6 0.0 copy-start
  5.6 0.0 copy-start.6
  5.6 0.5 collective-permute-start
  6.1 0.7 %collective-permute-start.1 = (f32[10,8,1024]{2,1,0:T(8,128)}, f32[10,8,1024]{2,1,0:T(8,128)S(1)}, u32[]{:S(2)}, u32[]{:S(2)}) collective-permute-start(f32[10,8,1024]{2,1,0:T(8,128)} %get-tuple-element.39), channel_id=1, source_target_pairs={{1,2},{2,1},{3,4},{4,3},{5,6},{6,5},{7,8},{8,7},{9,10},{10,9},{11,... | collective-permute-start | bytes 983048 | tf_op jit(solution)/shard_map/ppermute | solution.py:953
  6.8 10.4 %all-to-all-start = ((f32[16,5,4,128]{3,2,1,0:T(4,128)}), f32[16,5,4,128]{3,2,1,0:T(4,128)S(1)}, u32[]{:S(2)}, u32[]{:S(2)}) async-start(f32[16,5,4,128]{3,2,1,0:T(4,128)} %get-tuple-element.37), calls=%async_computation | async-start | bytes 327680 | tf_op jit(solution)/shard_map/all_to_all | solution.py:905
  17.2 4.9 %stencil_first.1 = (f32[6,8,128]{2,1,0:T(8,128)S(1)}, f32[8,16,1024]{2,1,0:T(8,128)S(1)}, f32[8,16,1024]{2,1,0:T(8,128)S(1)}, f32[8,16,1024]{2,1,0:T(8,128)S(1)}...) custom-call(f32[72,8,16,1024]{3,2,1,0:T(8,128)} %get-tuple-element.41.grids_hbm), custom_call_target="tpu_custom_call" | custom-call | bytes 12000000 | tf_op jit(solution)/shard_map/stencil_first/pallas_call | solution.py:846
  22.2 0.0 all-to-all-done.arrived_ref
  22.2 0.0 collective-permute-done.pair_ref.refs_0_
  22.2 0.0 collective-permute-done.1.cross_ref.refs_1_
  22.2 0.0 copy-done.1
  22.2 0.0 copy-done.4
  22.2 0.0 copy-done.3
  22.3 1.6 %couple_first.1 = (f32[8,256]{1,0:T(8,128)S(1)}, f32[8,256]{1,0:T(8,128)S(1)}, s32[16,128]{1,0:T(8,128)S(1)}, f32[16,4,128]{2,1,0:T(4,128)}) custom-call(f32[16,5,4,128]{3,2,1,0:T(4,128)S(1)} %all-to-all-done.arrived_ref, f32[10,8,1024]{2,1,0:T(8,128)S(1)} %collective-permute-done.pair_ref.refs_0_, ...), custom_call_target="tpu_custom_call" | custom-call | bytes 6000000 | tf_op jit(solution)/shard_map/couple_first/pallas_call | solution.py:846
  23.9 5.5 %all-to-all-start.1 = ((f32[16,4,128]{2,1,0:T(4,128)}), f32[16,4,128]{2,1,0:T(4,128)S(1)}, u32[]{:S(2)}, u32[]{:S(2)}) async-start(f32[16,4,128]{2,1,0:T(4,128)} %get-tuple-element.47), calls=%async_computation.1 | async-start | bytes 65536 | tf_op jit(solution)/shard_map/all_to_all | solution.py:905
  29.4 0.0 copy-done.2
  29.4 3.2 %stencil.3 = (f32[8,16,1024]{2,1,0:T(8,128)S(1)}, f32[2,3,8,1024]{3,2,1,0:T(8,128)S(1)}, f32[8,256]{1,0:T(8,128)S(1)}, f32[2,3,8,1024]{3,2,1,0:T(8,128)S(1)}, f3...) custom-call(f32[16,5,4,128]{3,2,1,0:T(4,128)S(1)} %all-to-all-done.a, ...), custom_call_target="tpu_custom_call", output_to_operand_aliasing={{0}: (1, {})} | custom-call | bytes 9000000 | tf_op jit(solution)/shard_map/stencil/pallas_call | solution.py:846
  32.5 0.1 all-to-all-done.1.arrived_ref
  32.6 1.3 %couple.2 = (f32[8,256]{1,0:T(8,128)S(1)}, f32[16,4,128]{2,1,0:T(4,128)}) custom-call(f32[16,4,128]{2,1,0:T(4,128)S(1)} %all-to-all-done.1.arrived_ref, s32[16,128]{1,0:T(8,128)S(1)} %get-tuple-element.48.node_code_ref, f32[3,16,128]{2,1,0:T(8,128)S(1)} %copy-done, f32[6,8,128]{2,1,0:T(8,128)S(1)} %get-tuple-element.42.rows_ref, ...), custom_call_target="tpu_custom_call" | custom-call | bytes 6000000 | tf_op jit(solution)/shard_map/couple/pallas_call | solution.py:846
  34.0 5.2 %all-to-all-start.2 = ((f32[16,4,128]{2,1,0:T(4,128)}), f32[16,4,128]{2,1,0:T(4,128)S(1)}, u32[]{:S(2)}, u32[]{:S(2)}) async-start(f32[16,4,128]{2,1,0:T(4,128)} %get-tuple-element.57), calls=%async_computation.2 | async-start | bytes 65536 | tf_op jit(solution)/shard_map/all_to_all | solution.py:905
  39.2 2.7 %stencil.4 = (f32[8,16,1024]{2,1,0:T(8,128)S(1)}, f32[2,3,8,1024]{3,2,1,0:T(8,128)S(1)}, f32[8,256]{1,0:T(8,128)S(1)}, f32[8,128]{1,0:T(8,128)S(1)}) custom-call(f32[16,4,128]{2,1,0:T(4,128)S(1)} %all-to-all-done.1.arrived_ref, f32[8,16,1024]{2,1,0:T(8,128)S(1)} %get-tuple-element.58.partial_before_ref, ...), custom_call_target="tpu_custom_call", output_to_operand_aliasing={{0}: (1, {}), {1}: (9, {})} | custom-call | bytes 9000000 | tf_op jit(solution)/shard_map/stencil/pallas_call | solution.py:846
  41.9 0.5 all-to-all-done.2.arrived_ref
  42.5 1.3 %couple.3 = (f32[8,256]{1,0:T(8,128)S(1)}, f32[16,4,128]{2,1,0:T(4,128)}) custom-call(f32[16,4,128]{2,1,0:T(4,128)S(1)} %all-to-all-done.2.arrived_ref, s32[16,128]{1,0:T(8,128)S(1)} %get-tuple-element.48.node_code_ref, f32[3,16,128]{2,1,0:T(8,128)S(1)} %copy-done, f32[6,8,128]{2,1,0:T(8,128)S(1)} %get-tuple-element.42.rows_ref, ...), custom_call_target="tpu_custom_call" | custom-call | bytes 6000000 | tf_op jit(solution)/shard_map/couple/pallas_call | solution.py:846
  43.8 5.2 %all-to-all-start.3 = ((f32[16,4,128]{2,1,0:T(4,128)}), f32[16,4,128]{2,1,0:T(4,128)S(1)}, u32[]{:S(2)}, u32[]{:S(2)}) async-start(f32[16,4,128]{2,1,0:T(4,128)} %get-tuple-element.66), calls=%async_computation.3 | async-start | bytes 65536 | tf_op jit(solution)/shard_map/all_to_all | solution.py:905
  49.0 1.6 %stencil.5 = (f32[8,16,1024]{2,1,0:T(8,128)S(1)}, f32[2,3,8,1024]{3,2,1,0:T(8,128)S(1)}, f32[8,256]{1,0:T(8,128)S(1)}) custom-call(f32[16,4,128]{2,1,0:T(4,128)S(1)} %all-to-all-done.2.arrived_ref, f32[8,16,1024]{2,1,0:T(8,128)S(1)} %get-tuple-element.67.partial_before_ref, ...), custom_call_target="tpu_custom_call", output_to_operand_aliasing={{0}: (1, {}), {1}: (9, {})} | custom-call | bytes 9000000 | tf_op jit(solution)/shard_map/stencil/pallas_call | solution.py:846
  50.6 1.7 %all-to-all-done.3.arrived_ref = f32[16,4,128]{2,1,0:T(4,128)S(1)} async-done(((f32[16,4,128]{2,1,0:T(4,128)}), f32[16,4,128]{2,1,0:T(4,128)S(1)}, u32[]{:S(2)}, u32[]{:S(2)}) %all-to-all-start.3) | async-done | bytes 32800 | tf_op jit(solution)/shard_map/all_to_all | solution.py:905
  52.3 1.7 %couple_last.1 = (f32[8,16,1024]{2,1,0:T(8,128)}, f32[8,256]{1,0:T(8,128)}) custom-call(f32[16,4,128]{2,1,0:T(4,128)S(1)} %all-to-all-done.3.arrived_ref, s32[16,128]{1,0:T(8,128)S(1)} %get-tuple-element.48.node_code_ref, f32[8,16,1024]{2,1,0:T(8,128)S(1)} %get-tuple-element.70.partial_ref, f32[8,16,1024]{2,1,0:T(8,128)S(1)} %get-tuple-element.51.inverse_ref, ...), custom_call_target="tpu_custom_call" | custom-call | bytes 6000000 | tf_op jit(solution)/shard_map/couple_last/pallas_call | solution.py:846
  (3 shorter events, 0.0 us)
Async XLA Ops:
  0.6 21.6 %copy-start.1 = (f32[4,8,256]{2,1,0:T(8,128)S(1)}, f32[4,8,256]{2,1,0:T(8,128)}, u32[]{:S(2)}) copy-start(f32[4,8,256]{2,1,0:T(8,128)} %link_weights_ref.7) | copy-start | bytes 98308
  0.6 28.7 %copy-start.2 = (s32[4,8,256]{2,1,0:T(8,128)S(1)}, s32[4,8,256]{2,1,0:T(8,128)}, u32[]{:S(2)}) copy-start(s32[4,8,256]{2,1,0:T(8,128)} %links_ref.5) | copy-start | bytes 98308
  0.7 21.6 %copy-start.4 = (f32[8,256]{1,0:T(8,128)S(1)}, f32[8,256]{1,0:T(8,128)}, u32[]{:S(2)}) copy-start(f32[8,256]{1,0:T(8,128)} %fracture_ref.1) | copy-start | bytes 24580
  0.7 21.6 %copy-start.3 = (f32[8,256]{1,0:T(8,128)S(1)}, f32[8,256]{1,0:T(8,128)}, u32[]{:S(2)}) copy-start(f32[8,256]{1,0:T(8,128)} %fracture_source_ref.7) | copy-start | bytes 24580
  0.7 21.6 %copy-start.5 = (f32[8,256]{1,0:T(8,128)S(1)}, f32[8,256]{1,0:T(8,128)}, u32[]{:S(2)}) copy-start(f32[8,256]{1,0:T(8,128)} %leak_ref.1) | copy-start | bytes 24580
  5.6 16.7 %copy-start = (f32[3,16,128]{2,1,0:T(8,128)S(1)}, f32[3,16,128]{2,1,0:T(8,128)}, u32[]{:S(2)}) copy-start(f32[3,16,128]{2,1,0:T(8,128)} %get-tuple-element.40.slots_ref) | copy-start | bytes 73732
  5.6 16.7 %copy-start.6 = (f32[8,256]{1,0:T(8,128)S(1)}, f32[8,256]{1,0:T(8,128)}, u32[]{:S(2)}) copy-start(f32[8,256]{1,0:T(8,128)} %get-tuple-element.46.link_sum_ref) | copy-start | bytes 24580
  5.6 16.6 %collective-permute-start = (f32[10,8,1024]{2,1,0:T(8,128)}, f32[10,8,1024]{2,1,0:T(8,128)S(1)}, u32[]{:S(2)}, u32[]{:S(2)}) collective-permute-start(f32[10,8,1024]{2,1,0:T(8,128)} %get-tuple-element.38), channel_id=1, source_target_pairs={{0,1},{1,0},{2,3},{3,2},{4,5},{5,4},{6,7},{7,6},{8,9},{9,8},{10,11... | collective-permute-start | bytes 983048 | tf_op jit(solution)/shard_map/ppermute | solution.py:952
  6.1 16.1 %collective-permute-start.1 = (f32[10,8,1024]{2,1,0:T(8,128)}, f32[10,8,1024]{2,1,0:T(8,128)S(1)}, u32[]{:S(2)}, u32[]{:S(2)}) collective-permute-start(f32[10,8,1024]{2,1,0:T(8,128)} %get-tuple-element.39), channel_id=1, source_target_pairs={{1,2},{2,1},{3,4},{4,3},{5,6},{6,5},{7,8},{8,7},{9,10},{10,9},{11,... | collective-permute-start | bytes 983048 | tf_op jit(solution)/shard_map/ppermute | solution.py:953
  6.8 15.4 %all-to-all-start = ((f32[16,5,4,128]{3,2,1,0:T(4,128)}), f32[16,5,4,128]{3,2,1,0:T(4,128)S(1)}, u32[]{:S(2)}, u32[]{:S(2)}) async-start(f32[16,5,4,128]{3,2,1,0:T(4,128)} %get-tuple-element.37), calls=%async_computation | async-start | bytes 327680 | tf_op jit(solution)/shard_map/all_to_all | solution.py:905
  23.9 8.7 %all-to-all-start.1 = ((f32[16,4,128]{2,1,0:T(4,128)}), f32[16,4,128]{2,1,0:T(4,128)S(1)}, u32[]{:S(2)}, u32[]{:S(2)}) async-start(f32[16,4,128]{2,1,0:T(4,128)} %get-tuple-element.47), calls=%async_computation.1 | async-start | bytes 65536 | tf_op jit(solution)/shard_map/all_to_all | solution.py:905
  34.0 8.5 %all-to-all-start.2 = ((f32[16,4,128]{2,1,0:T(4,128)}), f32[16,4,128]{2,1,0:T(4,128)S(1)}, u32[]{:S(2)}, u32[]{:S(2)}) async-start(f32[16,4,128]{2,1,0:T(4,128)} %get-tuple-element.57), calls=%async_computation.2 | async-start | bytes 65536 | tf_op jit(solution)/shard_map/all_to_all | solution.py:905
  43.8 8.5 %all-to-all-start.3 = ((f32[16,4,128]{2,1,0:T(4,128)}), f32[16,4,128]{2,1,0:T(4,128)S(1)}, u32[]{:S(2)}, u32[]{:S(2)}) async-start(f32[16,4,128]{2,1,0:T(4,128)} %get-tuple-element.66), calls=%async_computation.3 | async-start | bytes 65536 | tf_op jit(solution)/shard_map/all_to_all | solution.py:905

commit v7 on v6

--- a/solution.py
+++ b/solution.py
@@ -439,14 +439,15 @@
     ]
     for copy in copies:
         copy.start()
-    for copy in copies:
-        copy.wait()
+    copies[0].wait()
     depth, area_rows, cols = matrix_ref.shape
     plane_rows = depth * area_rows
     high, low = row_cells(rows_ref)
     weight = rows_ref[0]
     fill_hot(hot_ref, high)
     added = fold(matmul(hot_ref[...], masked_parts(low, unstack_lanes(weight, 1)), (1, 1)), 0)
+    for copy in copies[1:]:
+        copy.wait()
     for c in range(cols // LANES):
         lanes = slice(c * LANES, (c + 1) * LANES)
         extra = added[c * plane_rows : (c + 1) * plane_rows].reshape(depth, area_rows, LANES)
@@ -465,14 +466,6 @@
     chains = find_chains(rows_ref[3])
     for i, x in enumerate(chains):
         chains_ref[i] = x
-
-
-def row_integer(rows_ref, index):
-    return rows_ref[index].astype(jnp.int32)
-
-
-def row_cells(rows_ref):
-    return [unstack_lanes(row_integer(rows_ref, index), 1) for index in (4, 5)]
 
 
 def both_sides(pair_ref, cross_ref, tiles):
@@ -625,11 +618,6 @@
     link_sum_ref[...] = linked(fracture_ref[...], links_ref, link_weights_ref)
 
 
-def returned_values(returned, rows_ref):
-    target, rank = row_integer(rows_ref, 1), row_integer(rows_ref, 2)
-    return rows_ref[0] * pick_entries(returned, target, rank)
-
-
 def row_values(
     relaxation,
     returned,

time: 54.5 us -> 54.5 us (level)
  transfers between devices with their start and end apart: 6 -> 6, of which waited for: 3 -> 4; matrix products, arithmetic and copies ran while one was open for 0% -> 0% of each run, Pallas kernels for 23% -> 22%
where the time goes in v7:
time: 54.5 us; the launch traced here: 54.1 us
  starting transfers between devices  27.9 us (51%)
  Pallas kernels  22.2 us (41%)
  waiting for transfers between devices  2.48 us (5%)
  between operations  1.49 us (3%)
    all_to_all x4, starting transfers between devices, exchange(): lax.all_to_all(message, 'area', split_axis=0, concat_axis=0, tiled=True,...  26.7 us
    pallas_call x9, Pallas kernels, call(): pl.pallas_call(kernel, out_shape=[jax.ShapeDtypeStruct(shape, dtype) for...  22.2 us
    all_to_all x4, waiting for transfers between devices, exchange(): lax.all_to_all(message, 'area', split_axis=0, concat_axis=0, tiled=True,...  2.48 us
  transfers between devices with their start and end apart: 6, of which 4 were waited for; matrix products, arithmetic and copies ran while one was open for 0% of the time, Pallas kernels for 22%

profile of v7, /device:TPU:0, one launch (start us, length us, event | category | flops | bytes accessed | tf_op | source)
XLA Modules:
  0.0 54.1 jit_solution(9074569683954772344)
XLA Ops:
  0.6 0.0 copy-start.1
  0.6 0.0 copy-start.2
  0.7 0.0 copy-start.4
  0.7 0.0 copy-start.3
  0.7 0.0 copy-start.5
  1.4 4.2 %place_rows.1 = (f32[3,16,128]{2,1,0:T(8,128)}, f32[16,5,4,128]{3,2,1,0:T(4,128)}, f32[10,8,1024]{2,1,0:T(8,128)}, f32[10,8,1024]{2,1,0:T(8,128)}, f32[72,8,16,1024]{3,2,1,0:T(8,128)}, /*index=5*/f32[8,256]{1,0:T(8,128)}) custom-call(s32[1,1]{1,0:T(1,128)} %bitcast.5.refs_0_, s32[1,128]{1,0:T(1,128)} %bitcast.9, s32[8,128]{1,0:T(8,128)} %bitcast.6, ...), custom_call_target="tpu_custom_call" | custom-call | bytes 15000000 | tf_op jit(solution)/shard_map/place_rows/pallas_call | solution.py:834
  5.6 0.0 copy-start
  5.6 0.0 copy-start.6
  5.6 0.5 collective-permute-start
  6.1 0.7 %collective-permute-start.1 = (f32[10,8,1024]{2,1,0:T(8,128)}, f32[10,8,1024]{2,1,0:T(8,128)S(1)}, u32[]{:S(2)}, u32[]{:S(2)}) collective-permute-start(f32[10,8,1024]{2,1,0:T(8,128)} %get-tuple-element.39), channel_id=1, source_target_pairs={{1,2},{2,1},{3,4},{4,3},{5,6},{6,5},{7,8},{8,7},{9,10},{10,9},{11,... | collective-permute-start | bytes 983048 | tf_op jit(solution)/shard_map/ppermute | solution.py:941
  6.8 10.4 %all-to-all-start = ((f32[16,5,4,128]{3,2,1,0:T(4,128)}), f32[16,5,4,128]{3,2,1,0:T(4,128)S(1)}, u32[]{:S(2)}, u32[]{:S(2)}) async-start(f32[16,5,4,128]{3,2,1,0:T(4,128)} %get-tuple-element.37), calls=%async_computation | async-start | bytes 327680 | tf_op jit(solution)/shard_map/all_to_all | solution.py:893
  17.2 4.5 %stencil_first.1 = (f32[6,8,128]{2,1,0:T(8,128)S(1)}, f32[8,16,1024]{2,1,0:T(8,128)S(1)}, f32[8,16,1024]{2,1,0:T(8,128)S(1)}, f32[8,16,1024]{2,1,0:T(8,128)S(1)}...) custom-call(f32[72,8,16,1024]{3,2,1,0:T(8,128)} %get-tuple-element.41.grids_hbm), custom_call_target="tpu_custom_call" | custom-call | bytes 12000000 | tf_op jit(solution)/shard_map/stencil_first/pallas_call | solution.py:834
  21.7 0.2 all-to-all-done.arrived_ref
  21.9 0.0 collective-permute-done.pair_ref.refs_0_
  21.9 0.0 collective-permute-done.1.cross_ref.refs_1_
  21.9 0.0 copy-done.1
  21.9 0.0 copy-done.4
  21.9 0.0 copy-done.3
  21.9 0.0 copy-done.5
  22.0 1.6 %couple_first.1 = (f32[8,256]{1,0:T(8,128)S(1)}, f32[8,256]{1,0:T(8,128)S(1)}, s32[16,128]{1,0:T(8,128)S(1)}, f32[16,4,128]{2,1,0:T(4,128)}) custom-call(f32[16,5,4,128]{3,2,1,0:T(4,128)S(1)} %all-to-all-done.arrived_ref, f32[10,8,1024]{2,1,0:T(8,128)S(1)} %collective-permute-done.pair_ref.refs_0_, ...), custom_call_target="tpu_custom_call" | custom-call | bytes 6000000 | tf_op jit(solution)/shard_map/couple_first/pallas_call | solution.py:834
  23.6 5.9 %all-to-all-start.1 = ((f32[16,4,128]{2,1,0:T(4,128)}), f32[16,4,128]{2,1,0:T(4,128)S(1)}, u32[]{:S(2)}, u32[]{:S(2)}) async-start(f32[16,4,128]{2,1,0:T(4,128)} %get-tuple-element.47), calls=%async_computation.1 | async-start | bytes 65536 | tf_op jit(solution)/shard_map/all_to_all | solution.py:893
  29.5 3.2 %stencil.3 = (f32[8,16,1024]{2,1,0:T(8,128)S(1)}, f32[2,3,8,1024]{3,2,1,0:T(8,128)S(1)}, f32[8,256]{1,0:T(8,128)S(1)}, f32[2,3,8,1024]{3,2,1,0:T(8,128)S(1)}, f3...) custom-call(f32[16,5,4,128]{3,2,1,0:T(4,128)S(1)} %all-to-all-done.a, ...), custom_call_target="tpu_custom_call", output_to_operand_aliasing={{0}: (1, {})} | custom-call | bytes 9000000 | tf_op jit(solution)/shard_map/stencil/pallas_call | solution.py:834
  32.6 0.1 all-to-all-done.1.arrived_ref
  32.7 1.3 %couple.2 = (f32[8,256]{1,0:T(8,128)S(1)}, f32[16,4,128]{2,1,0:T(4,128)}) custom-call(f32[16,4,128]{2,1,0:T(4,128)S(1)} %all-to-all-done.1.arrived_ref, s32[16,128]{1,0:T(8,128)S(1)} %get-tuple-element.48.node_code_ref, f32[3,16,128]{2,1,0:T(8,128)S(1)} %copy-done, f32[6,8,128]{2,1,0:T(8,128)S(1)} %get-tuple-element.42.rows_ref, ...), custom_call_target="tpu_custom_call" | custom-call | bytes 6000000 | tf_op jit(solution)/shard_map/couple/pallas_call | solution.py:834
  34.1 5.2 %all-to-all-start.2 = ((f32[16,4,128]{2,1,0:T(4,128)}), f32[16,4,128]{2,1,0:T(4,128)S(1)}, u32[]{:S(2)}, u32[]{:S(2)}) async-start(f32[16,4,128]{2,1,0:T(4,128)} %get-tuple-element.57), calls=%async_computation.2 | async-start | bytes 65536 | tf_op jit(solution)/shard_map/all_to_all | solution.py:893
  39.3 2.7 %stencil.4 = (f32[8,16,1024]{2,1,0:T(8,128)S(1)}, f32[2,3,8,1024]{3,2,1,0:T(8,128)S(1)}, f32[8,256]{1,0:T(8,128)S(1)}, f32[8,128]{1,0:T(8,128)S(1)}) custom-call(f32[16,4,128]{2,1,0:T(4,128)S(1)} %all-to-all-done.1.arrived_ref, f32[8,16,1024]{2,1,0:T(8,128)S(1)} %get-tuple-element.58.partial_before_ref, ...), custom_call_target="tpu_custom_call", output_to_operand_aliasing={{0}: (1, {}), {1}: (9, {})} | custom-call | bytes 9000000 | tf_op jit(solution)/shard_map/stencil/pallas_call | solution.py:834
  42.0 0.5 all-to-all-done.2.arrived_ref
  42.6 1.3 %couple.3 = (f32[8,256]{1,0:T(8,128)S(1)}, f32[16,4,128]{2,1,0:T(4,128)}) custom-call(f32[16,4,128]{2,1,0:T(4,128)S(1)} %all-to-all-done.2.arrived_ref, s32[16,128]{1,0:T(8,128)S(1)} %get-tuple-element.48.node_code_ref, f32[3,16,128]{2,1,0:T(8,128)S(1)} %copy-done, f32[6,8,128]{2,1,0:T(8,128)S(1)} %get-tuple-element.42.rows_ref, ...), custom_call_target="tpu_custom_call" | custom-call | bytes 6000000 | tf_op jit(solution)/shard_map/couple/pallas_call | solution.py:834
  43.9 5.2 %all-to-all-start.3 = ((f32[16,4,128]{2,1,0:T(4,128)}), f32[16,4,128]{2,1,0:T(4,128)S(1)}, u32[]{:S(2)}, u32[]{:S(2)}) async-start(f32[16,4,128]{2,1,0:T(4,128)} %get-tuple-element.66), calls=%async_computation.3 | async-start | bytes 65536 | tf_op jit(solution)/shard_map/all_to_all | solution.py:893
  49.1 1.6 %stencil.5 = (f32[8,16,1024]{2,1,0:T(8,128)S(1)}, f32[2,3,8,1024]{3,2,1,0:T(8,128)S(1)}, f32[8,256]{1,0:T(8,128)S(1)}) custom-call(f32[16,4,128]{2,1,0:T(4,128)S(1)} %all-to-all-done.2.arrived_ref, f32[8,16,1024]{2,1,0:T(8,128)S(1)} %get-tuple-element.67.partial_before_ref, ...), custom_call_target="tpu_custom_call", output_to_operand_aliasing={{0}: (1, {}), {1}: (9, {})} | custom-call | bytes 9000000 | tf_op jit(solution)/shard_map/stencil/pallas_call | solution.py:834
  50.7 1.7 %all-to-all-done.3.arrived_ref = f32[16,4,128]{2,1,0:T(4,128)S(1)} async-done(((f32[16,4,128]{2,1,0:T(4,128)}), f32[16,4,128]{2,1,0:T(4,128)S(1)}, u32[]{:S(2)}, u32[]{:S(2)}) %all-to-all-start.3) | async-done | bytes 32800 | tf_op jit(solution)/shard_map/all_to_all | solution.py:893
  52.4 1.7 %couple_last.1 = (f32[8,16,1024]{2,1,0:T(8,128)}, f32[8,256]{1,0:T(8,128)}) custom-call(f32[16,4,128]{2,1,0:T(4,128)S(1)} %all-to-all-done.3.arrived_ref, s32[16,128]{1,0:T(8,128)S(1)} %get-tuple-element.48.node_code_ref, f32[8,16,1024]{2,1,0:T(8,128)S(1)} %get-tuple-element.70.partial_ref, f32[8,16,1024]{2,1,0:T(8,128)S(1)} %get-tuple-element.51.inverse_ref, ...), custom_call_target="tpu_custom_call" | custom-call | bytes 6000000 | tf_op jit(solution)/shard_map/couple_last/pallas_call | solution.py:834
  (3 shorter events, 0.0 us)
Async XLA Ops:
  0.6 21.3 %copy-start.1 = (f32[4,8,256]{2,1,0:T(8,128)S(1)}, f32[4,8,256]{2,1,0:T(8,128)}, u32[]{:S(2)}) copy-start(f32[4,8,256]{2,1,0:T(8,128)} %link_weights_ref.7) | copy-start | bytes 98308
  0.6 28.8 %copy-start.2 = (s32[4,8,256]{2,1,0:T(8,128)S(1)}, s32[4,8,256]{2,1,0:T(8,128)}, u32[]{:S(2)}) copy-start(s32[4,8,256]{2,1,0:T(8,128)} %links_ref.5) | copy-start | bytes 98308
  0.7 21.3 %copy-start.4 = (f32[8,256]{1,0:T(8,128)S(1)}, f32[8,256]{1,0:T(8,128)}, u32[]{:S(2)}) copy-start(f32[8,256]{1,0:T(8,128)} %fracture_ref.1) | copy-start | bytes 24580
  0.7 21.3 %copy-start.3 = (f32[8,256]{1,0:T(8,128)S(1)}, f32[8,256]{1,0:T(8,128)}, u32[]{:S(2)}) copy-start(f32[8,256]{1,0:T(8,128)} %fracture_source_ref.7) | copy-start | bytes 24580
  0.7 21.3 %copy-start.5 = (f32[8,256]{1,0:T(8,128)S(1)}, f32[8,256]{1,0:T(8,128)}, u32[]{:S(2)}) copy-start(f32[8,256]{1,0:T(8,128)} %leak_ref.1) | copy-start | bytes 24580
  5.6 16.4 %copy-start = (f32[3,16,128]{2,1,0:T(8,128)S(1)}, f32[3,16,128]{2,1,0:T(8,128)}, u32[]{:S(2)}) copy-start(f32[3,16,128]{2,1,0:T(8,128)} %get-tuple-element.40.slots_ref) | copy-start | bytes 73732
  5.6 16.4 %copy-start.6 = (f32[8,256]{1,0:T(8,128)S(1)}, f32[8,256]{1,0:T(8,128)}, u32[]{:S(2)}) copy-start(f32[8,256]{1,0:T(8,128)} %get-tuple-element.46.link_sum_ref) | copy-start | bytes 24580
  5.6 16.3 %collective-permute-start = (f32[10,8,1024]{2,1,0:T(8,128)}, f32[10,8,1024]{2,1,0:T(8,128)S(1)}, u32[]{:S(2)}, u32[]{:S(2)}) collective-permute-start(f32[10,8,1024]{2,1,0:T(8,128)} %get-tuple-element.38), channel_id=1, source_target_pairs={{0,1},{1,0},{2,3},{3,2},{4,5},{5,4},{6,7},{7,6},{8,9},{9,8},{10,11... | collective-permute-start | bytes 983048 | tf_op jit(solution)/shard_map/ppermute | solution.py:940
  6.1 15.8 %collective-permute-start.1 = (f32[10,8,1024]{2,1,0:T(8,128)}, f32[10,8,1024]{2,1,0:T(8,128)S(1)}, u32[]{:S(2)}, u32[]{:S(2)}) collective-permute-start(f32[10,8,1024]{2,1,0:T(8,128)} %get-tuple-element.39), channel_id=1, source_target_pairs={{1,2},{2,1},{3,4},{4,3},{5,6},{6,5},{7,8},{8,7},{9,10},{10,9},{11,... | collective-permute-start | bytes 983048 | tf_op jit(solution)/shard_map/ppermute | solution.py:941
  6.8 15.1 %all-to-all-start = ((f32[16,5,4,128]{3,2,1,0:T(4,128)}), f32[16,5,4,128]{3,2,1,0:T(4,128)S(1)}, u32[]{:S(2)}, u32[]{:S(2)}) async-start(f32[16,5,4,128]{3,2,1,0:T(4,128)} %get-tuple-element.37), calls=%async_computation | async-start | bytes 327680 | tf_op jit(solution)/shard_map/all_to_all | solution.py:893
  23.6 9.1 %all-to-all-start.1 = ((f32[16,4,128]{2,1,0:T(4,128)}), f32[16,4,128]{2,1,0:T(4,128)S(1)}, u32[]{:S(2)}, u32[]{:S(2)}) async-start(f32[16,4,128]{2,1,0:T(4,128)} %get-tuple-element.47), calls=%async_computation.1 | async-start | bytes 65536 | tf_op jit(solution)/shard_map/all_to_all | solution.py:893
  34.1 8.5 %all-to-all-start.2 = ((f32[16,4,128]{2,1,0:T(4,128)}), f32[16,4,128]{2,1,0:T(4,128)S(1)}, u32[]{:S(2)}, u32[]{:S(2)}) async-start(f32[16,4,128]{2,1,0:T(4,128)} %get-tuple-element.57), calls=%async_computation.2 | async-start | bytes 65536 | tf_op jit(solution)/shard_map/all_to_all | solution.py:893
  43.9 8.5 %all-to-all-start.3 = ((f32[16,4,128]{2,1,0:T(4,128)}), f32[16,4,128]{2,1,0:T(4,128)S(1)}, u32[]{:S(2)}, u32[]{:S(2)}) async-start(f32[16,4,128]{2,1,0:T(4,128)} %get-tuple-element.66), calls=%async_computation.3 | async-start | bytes 65536 | tf_op jit(solution)/shard_map/all_to_all | solution.py:893

commit v8 on v7

--- a/solution.py
+++ b/solution.py
@@ -234,12 +234,15 @@
         copy.wait()
     for copy in kept[:3]:
         copy.start()
-    link_sum_ref[...] = linked(fracture_ref[...], links_ref, link_weights_ref)
     node_table = stack_lanes(fracture_ref[...])
     for i in range(node_table.shape[0]):
         message_ref[:, 1 + i // 4, i % 4, :] = jnp.broadcast_to(
             node_table[i : i + 1], (devices, LANES)
         )
+    picked = stack_lanes(pick_cells(matrix_ref, columns_ref, hot_ref, low))
+    message_ref[:, 0, 2, :] = pick_entries(weight * picked, slot_row, slot_lane)
+    message_copy = pltpu.make_async_copy(message_ref, message_hbm, sems.at[staged + 2])
+    message_copy.start()
     for part, ref in enumerate((matrix_ref, source_ref, storage_ref)):
         for far in range(HALO):
             up = ref[:, area_rows - 1 - far, :]
@@ -252,13 +255,11 @@
     outs = [
         pltpu.make_async_copy(pair_ref, pair_hbm, sems.at[staged]),
         pltpu.make_async_copy(cross_ref, cross_hbm, sems.at[staged + 1]),
-        pltpu.make_async_copy(message_ref, message_hbm, sems.at[staged + 2]),
+        message_copy,
     ]
     outs[0].start()
     outs[1].start()
-    picked = stack_lanes(pick_cells(matrix_ref, columns_ref, hot_ref, low))
-    message_ref[:, 0, 2, :] = pick_entries(weight * picked, slot_row, slot_lane)
-    outs[2].start()
+    link_sum_ref[...] = linked(fracture_ref[...], links_ref, link_weights_ref)
     for out in outs + kept:
         out.wait()
 

time: 54.5 us -> 54.6 us (level)
  no operation moved by 1% of the time
where the time goes in v8:
time: 54.6 us; the launch traced here: 54 us
  starting transfers between devices  27.9 us (51%)
  Pallas kernels  22.1 us (40%)
  waiting for transfers between devices  2.49 us (5%)
  between operations  1.49 us (3%)
    all_to_all x4, starting transfers between devices, exchange(): lax.all_to_all(message, 'area', split_axis=0, concat_axis=0, tiled=True,...  26.8 us
    pallas_call x9, Pallas kernels, call(): pl.pallas_call(kernel, out_shape=[jax.ShapeDtypeStruct(shape, dtype) for...  22.1 us
    all_to_all x4, waiting for transfers between devices, exchange(): lax.all_to_all(message, 'area', split_axis=0, concat_axis=0, tiled=True,...  2.48 us
  transfers between devices with their start and end apart: 6, of which 4 were waited for; matrix products, arithmetic and copies ran while one was open for 0% of the time, Pallas kernels for 22%

profile of v8, /device:TPU:0, one launch (start us, length us, event | category | flops | bytes accessed | tf_op | source)
XLA Modules:
  0.0 54.0 jit_solution(14940468334320155335)
XLA Ops:
  0.6 0.0 copy-start.1
  0.6 0.0 copy-start.2
  0.7 0.0 copy-start.4
  0.7 0.0 copy-start.3
  0.7 0.0 copy-start.5
  1.4 4.1 %place_rows.1 = (f32[3,16,128]{2,1,0:T(8,128)}, f32[16,5,4,128]{3,2,1,0:T(4,128)}, f32[10,8,1024]{2,1,0:T(8,128)}, f32[10,8,1024]{2,1,0:T(8,128)}, f32[72,8,16,1024]{3,2,1,0:T(8,128)}, /*index=5*/f32[8,256]{1,0:T(8,128)}) custom-call(s32[1,1]{1,0:T(1,128)} %bitcast.5.refs_0_, s32[1,128]{1,0:T(1,128)} %bitcast.9, s32[8,128]{1,0:T(8,128)} %bitcast.6, ...), custom_call_target="tpu_custom_call" | custom-call | bytes 15000000 | tf_op jit(solution)/shard_map/place_rows/pallas_call | solution.py:835
  5.5 0.0 copy-start.6
  5.5 0.5 collective-permute-start
  6.0 0.7 %collective-permute-start.1 = (f32[10,8,1024]{2,1,0:T(8,128)}, f32[10,8,1024]{2,1,0:T(8,128)S(1)}, u32[]{:S(2)}, u32[]{:S(2)}) collective-permute-start(f32[10,8,1024]{2,1,0:T(8,128)} %get-tuple-element.39), channel_id=1, source_target_pairs={{1,2},{2,1},{3,4},{4,3},{5,6},{6,5},{7,8},{8,7},{9,10},{10,9},{11,... | collective-permute-start | bytes 983048 | tf_op jit(solution)/shard_map/ppermute | solution.py:942
  6.7 10.4 %all-to-all-start = ((f32[16,5,4,128]{3,2,1,0:T(4,128)}), f32[16,5,4,128]{3,2,1,0:T(4,128)S(1)}, u32[]{:S(2)}, u32[]{:S(2)}) async-start(f32[16,5,4,128]{3,2,1,0:T(4,128)} %get-tuple-element.37), calls=%async_computation | async-start | bytes 327680 | tf_op jit(solution)/shard_map/all_to_all | solution.py:894
  17.1 4.5 %stencil_first.1 = (f32[6,8,128]{2,1,0:T(8,128)S(1)}, f32[8,16,1024]{2,1,0:T(8,128)S(1)}, f32[8,16,1024]{2,1,0:T(8,128)S(1)}, f32[8,16,1024]{2,1,0:T(8,128)S(1)}...) custom-call(f32[72,8,16,1024]{3,2,1,0:T(8,128)} %get-tuple-element.41.grids_hbm), custom_call_target="tpu_custom_call" | custom-call | bytes 12000000 | tf_op jit(solution)/shard_map/stencil_first/pallas_call | solution.py:835
  21.6 0.2 all-to-all-done.arrived_ref
  21.8 0.0 collective-permute-done.pair_ref.refs_0_
  21.8 0.0 collective-permute-done.1.cross_ref.refs_1_
  21.8 0.0 copy-done.4
  21.8 0.0 copy-done.3
  21.8 0.0 copy-done.5
  21.8 0.0 copy-done
  21.9 0.0 copy-done.6
  21.9 1.6 %couple_first.1 = (f32[8,256]{1,0:T(8,128)S(1)}, f32[8,256]{1,0:T(8,128)S(1)}, s32[16,128]{1,0:T(8,128)S(1)}, f32[16,4,128]{2,1,0:T(4,128)}) custom-call(f32[16,5,4,128]{3,2,1,0:T(4,128)S(1)} %all-to-all-done.arrived_ref, f32[10,8,1024]{2,1,0:T(8,128)S(1)} %collective-permute-done.pair_ref.refs_0_, ...), custom_call_target="tpu_custom_call" | custom-call | bytes 6000000 | tf_op jit(solution)/shard_map/couple_first/pallas_call | solution.py:835
  23.5 5.9 %all-to-all-start.1 = ((f32[16,4,128]{2,1,0:T(4,128)}), f32[16,4,128]{2,1,0:T(4,128)S(1)}, u32[]{:S(2)}, u32[]{:S(2)}) async-start(f32[16,4,128]{2,1,0:T(4,128)} %get-tuple-element.47), calls=%async_computation.1 | async-start | bytes 65536 | tf_op jit(solution)/shard_map/all_to_all | solution.py:894
  29.4 3.1 %stencil.3 = (f32[8,16,1024]{2,1,0:T(8,128)S(1)}, f32[2,3,8,1024]{3,2,1,0:T(8,128)S(1)}, f32[8,256]{1,0:T(8,128)S(1)}, f32[2,3,8,1024]{3,2,1,0:T(8,128)S(1)}, f3...) custom-call(f32[16,5,4,128]{3,2,1,0:T(4,128)S(1)} %all-to-all-done.a, ...), custom_call_target="tpu_custom_call", output_to_operand_aliasing={{0}: (1, {})} | custom-call | bytes 9000000 | tf_op jit(solution)/shard_map/stencil/pallas_call | solution.py:835
  32.5 0.1 all-to-all-done.1.arrived_ref
  32.6 1.3 %couple.2 = (f32[8,256]{1,0:T(8,128)S(1)}, f32[16,4,128]{2,1,0:T(4,128)}) custom-call(f32[16,4,128]{2,1,0:T(4,128)S(1)} %all-to-all-done.1.arrived_ref, s32[16,128]{1,0:T(8,128)S(1)} %get-tuple-element.48.node_code_ref, f32[3,16,128]{2,1,0:T(8,128)S(1)} %copy-done, f32[6,8,128]{2,1,0:T(8,128)S(1)} %get-tuple-element.42.rows_ref, ...), custom_call_target="tpu_custom_call" | custom-call | bytes 6000000 | tf_op jit(solution)/shard_map/couple/pallas_call | solution.py:835
  34.0 5.2 %all-to-all-start.2 = ((f32[16,4,128]{2,1,0:T(4,128)}), f32[16,4,128]{2,1,0:T(4,128)S(1)}, u32[]{:S(2)}, u32[]{:S(2)}) async-start(f32[16,4,128]{2,1,0:T(4,128)} %get-tuple-element.57), calls=%async_computation.2 | async-start | bytes 65536 | tf_op jit(solution)/shard_map/all_to_all | solution.py:894
  39.2 2.7 %stencil.4 = (f32[8,16,1024]{2,1,0:T(8,128)S(1)}, f32[2,3,8,1024]{3,2,1,0:T(8,128)S(1)}, f32[8,256]{1,0:T(8,128)S(1)}, f32[8,128]{1,0:T(8,128)S(1)}) custom-call(f32[16,4,128]{2,1,0:T(4,128)S(1)} %all-to-all-done.1.arrived_ref, f32[8,16,1024]{2,1,0:T(8,128)S(1)} %get-tuple-element.58.partial_before_ref, ...), custom_call_target="tpu_custom_call", output_to_operand_aliasing={{0}: (1, {}), {1}: (9, {})} | custom-call | bytes 9000000 | tf_op jit(solution)/shard_map/stencil/pallas_call | solution.py:835
  41.9 0.5 all-to-all-done.2.arrived_ref
  42.5 1.3 %couple.3 = (f32[8,256]{1,0:T(8,128)S(1)}, f32[16,4,128]{2,1,0:T(4,128)}) custom-call(f32[16,4,128]{2,1,0:T(4,128)S(1)} %all-to-all-done.2.arrived_ref, s32[16,128]{1,0:T(8,128)S(1)} %get-tuple-element.48.node_code_ref, f32[3,16,128]{2,1,0:T(8,128)S(1)} %copy-done, f32[6,8,128]{2,1,0:T(8,128)S(1)} %get-tuple-element.42.rows_ref, ...), custom_call_target="tpu_custom_call" | custom-call | bytes 6000000 | tf_op jit(solution)/shard_map/couple/pallas_call | solution.py:835
  43.8 5.2 %all-to-all-start.3 = ((f32[16,4,128]{2,1,0:T(4,128)}), f32[16,4,128]{2,1,0:T(4,128)S(1)}, u32[]{:S(2)}, u32[]{:S(2)}) async-start(f32[16,4,128]{2,1,0:T(4,128)} %get-tuple-element.66), calls=%async_computation.3 | async-start | bytes 65536 | tf_op jit(solution)/shard_map/all_to_all | solution.py:894
  49.0 1.6 %stencil.5 = (f32[8,16,1024]{2,1,0:T(8,128)S(1)}, f32[2,3,8,1024]{3,2,1,0:T(8,128)S(1)}, f32[8,256]{1,0:T(8,128)S(1)}) custom-call(f32[16,4,128]{2,1,0:T(4,128)S(1)} %all-to-all-done.2.arrived_ref, f32[8,16,1024]{2,1,0:T(8,128)S(1)} %get-tuple-element.67.partial_before_ref, ...), custom_call_target="tpu_custom_call", output_to_operand_aliasing={{0}: (1, {}), {1}: (9, {})} | custom-call | bytes 9000000 | tf_op jit(solution)/shard_map/stencil/pallas_call | solution.py:835
  50.6 1.7 %all-to-all-done.3.arrived_ref = f32[16,4,128]{2,1,0:T(4,128)S(1)} async-done(((f32[16,4,128]{2,1,0:T(4,128)}), f32[16,4,128]{2,1,0:T(4,128)S(1)}, u32[]{:S(2)}, u32[]{:S(2)}) %all-to-all-start.3) | async-done | bytes 32800 | tf_op jit(solution)/shard_map/all_to_all | solution.py:894
  52.3 1.7 %couple_last.1 = (f32[8,16,1024]{2,1,0:T(8,128)}, f32[8,256]{1,0:T(8,128)}) custom-call(f32[16,4,128]{2,1,0:T(4,128)S(1)} %all-to-all-done.3.arrived_ref, s32[16,128]{1,0:T(8,128)S(1)} %get-tuple-element.48.node_code_ref, f32[8,16,1024]{2,1,0:T(8,128)S(1)} %get-tuple-element.70.partial_ref, f32[8,16,1024]{2,1,0:T(8,128)S(1)} %get-tuple-element.51.inverse_ref, ...), custom_call_target="tpu_custom_call" | custom-call | bytes 6000000 | tf_op jit(solution)/shard_map/couple_last/pallas_call | solution.py:835
  (3 shorter events, 0.0 us)
Async XLA Ops:
  0.6 21.2 %copy-start.1 = (f32[4,8,256]{2,1,0:T(8,128)S(1)}, f32[4,8,256]{2,1,0:T(8,128)}, u32[]{:S(2)}) copy-start(f32[4,8,256]{2,1,0:T(8,128)} %link_weights_ref.7) | copy-start | bytes 98308
  0.6 28.7 %copy-start.2 = (s32[4,8,256]{2,1,0:T(8,128)S(1)}, s32[4,8,256]{2,1,0:T(8,128)}, u32[]{:S(2)}) copy-start(s32[4,8,256]{2,1,0:T(8,128)} %links_ref.5) | copy-start | bytes 98308
  0.7 21.2 %copy-start.4 = (f32[8,256]{1,0:T(8,128)S(1)}, f32[8,256]{1,0:T(8,128)}, u32[]{:S(2)}) copy-start(f32[8,256]{1,0:T(8,128)} %fracture_ref.1) | copy-start | bytes 24580
  0.7 21.2 %copy-start.3 = (f32[8,256]{1,0:T(8,128)S(1)}, f32[8,256]{1,0:T(8,128)}, u32[]{:S(2)}) copy-start(f32[8,256]{1,0:T(8,128)} %fracture_source_ref.7) | copy-start | bytes 24580
  0.7 21.2 %copy-start.5 = (f32[8,256]{1,0:T(8,128)S(1)}, f32[8,256]{1,0:T(8,128)}, u32[]{:S(2)}) copy-start(f32[8,256]{1,0:T(8,128)} %leak_ref.1) | copy-start | bytes 24580
  5.5 16.4 %copy-start = (f32[3,16,128]{2,1,0:T(8,128)S(1)}, f32[3,16,128]{2,1,0:T(8,128)}, u32[]{:S(2)}) copy-start(f32[3,16,128]{2,1,0:T(8,128)} %get-tuple-element.40.slots_ref) | copy-start | bytes 73732
  5.5 16.4 %copy-start.6 = (f32[8,256]{1,0:T(8,128)S(1)}, f32[8,256]{1,0:T(8,128)}, u32[]{:S(2)}) copy-start(f32[8,256]{1,0:T(8,128)} %get-tuple-element.46.link_sum_ref) | copy-start | bytes 24580
  5.5 16.3 %collective-permute-start = (f32[10,8,1024]{2,1,0:T(8,128)}, f32[10,8,1024]{2,1,0:T(8,128)S(1)}, u32[]{:S(2)}, u32[]{:S(2)}) collective-permute-start(f32[10,8,1024]{2,1,0:T(8,128)} %get-tuple-element.38), channel_id=1, source_target_pairs={{0,1},{1,0},{2,3},{3,2},{4,5},{5,4},{6,7},{7,6},{8,9},{9,8},{10,11... | collective-permute-start | bytes 983048 | tf_op jit(solution)/shard_map/ppermute | solution.py:941
  6.0 15.8 %collective-permute-start.1 = (f32[10,8,1024]{2,1,0:T(8,128)}, f32[10,8,1024]{2,1,0:T(8,128)S(1)}, u32[]{:S(2)}, u32[]{:S(2)}) collective-permute-start(f32[10,8,1024]{2,1,0:T(8,128)} %get-tuple-element.39), channel_id=1, source_target_pairs={{1,2},{2,1},{3,4},{4,3},{5,6},{6,5},{7,8},{8,7},{9,10},{10,9},{11,... | collective-permute-start | bytes 983048 | tf_op jit(solution)/shard_map/ppermute | solution.py:942
  6.7 15.1 %all-to-all-start = ((f32[16,5,4,128]{3,2,1,0:T(4,128)}), f32[16,5,4,128]{3,2,1,0:T(4,128)S(1)}, u32[]{:S(2)}, u32[]{:S(2)}) async-start(f32[16,5,4,128]{3,2,1,0:T(4,128)} %get-tuple-element.37), calls=%async_computation | async-start | bytes 327680 | tf_op jit(solution)/shard_map/all_to_all | solution.py:894
  23.5 9.1 %all-to-all-start.1 = ((f32[16,4,128]{2,1,0:T(4,128)}), f32[16,4,128]{2,1,0:T(4,128)S(1)}, u32[]{:S(2)}, u32[]{:S(2)}) async-start(f32[16,4,128]{2,1,0:T(4,128)} %get-tuple-element.47), calls=%async_computation.1 | async-start | bytes 65536 | tf_op jit(solution)/shard_map/all_to_all | solution.py:894
  34.0 8.5 %all-to-all-start.2 = ((f32[16,4,128]{2,1,0:T(4,128)}), f32[16,4,128]{2,1,0:T(4,128)S(1)}, u32[]{:S(2)}, u32[]{:S(2)}) async-start(f32[16,4,128]{2,1,0:T(4,128)} %get-tuple-element.57), calls=%async_computation.2 | async-start | bytes 65536 | tf_op jit(solution)/shard_map/all_to_all | solution.py:894
  43.8 8.5 %all-to-all-start.3 = ((f32[16,4,128]{2,1,0:T(4,128)}), f32[16,4,128]{2,1,0:T(4,128)S(1)}, u32[]{:S(2)}, u32[]{:S(2)}) async-start(f32[16,4,128]{2,1,0:T(4,128)} %get-tuple-element.66), calls=%async_computation.3 | async-start | bytes 65536 | tf_op jit(solution)/shard_map/all_to_all | solution.py:894
